TPU v7x, 128 devices: a whole 4x4x4 slice. The times are simulated.
128 devices in a mesh: ctx: 16 (over x, y_hi, core), dp: 2 (over y_lo), fsdp: 4 (over z).
Axes of the slice: x: 4, y: 4 (y_hi: 2, y_lo: 2; y = y_hi * 2 + y_lo), z: 4, core: 2. Of those that a mesh axis runs over, the one named last changes fastest.
Arguments:
- hidden_in: bfloat16 [2, 8192, 1024], P('dp', ('ctx', 'fsdp')), may hold values from -6 to 6
- positions: int32 [2, 8192], P('dp', ('ctx', 'fsdp')), may hold values from 0 to 8191, as said below
- attn_gain: bfloat16 [1024], P(('dp', 'fsdp')), may hold values from 0.5 to 1.5
- query_weight: bfloat16 [1024, 2048], P(('dp', 'fsdp')), may hold values from -0.1875 to 0.1875
- key_matrix: bfloat16 [1024, 1024], P(('dp', 'fsdp')), may hold values from -0.1875 to 0.1875
- value_matrix: bfloat16 [1024, 1024], P(('dp', 'fsdp')), may hold values from -0.1875 to 0.1875
- output_weight: bfloat16 [2048, 1024], P(('dp', 'fsdp')), may hold values from -6 to 6
- query_norm_gain: bfloat16 [128], P(('dp', 'fsdp')), may hold values from 0.5 to 1.5
- key_gain: bfloat16 [128], P(('dp', 'fsdp')), may hold values from 0.5 to 1.5
- mlp_gain: bfloat16 [1024], P(('dp', 'fsdp')), may hold values from 0.5 to 1.5
- gate_weight: bfloat16 [1024, 3072], P(('dp', 'fsdp')), may hold values from -0.1875 to 0.1875
- up_weight: bfloat16 [1024, 3072], P(('dp', 'fsdp')), may hold values from -0.1875 to 0.1875
- down_weight: bfloat16 [3072, 1024], P(('dp', 'fsdp')), may hold values from -0.109375 to 0.109375
- cotangent: bfloat16 [2, 8192, 1024], P('dp', ('ctx', 'fsdp')), may hold values from -6 to 6
Outputs:
- layer_out: bfloat16 [2, 8192, 1024], P('dp', ('ctx', 'fsdp'))
- input_grad: float32 [2, 8192, 1024], P('dp', ('ctx', 'fsdp'))
- attn_gain_grad: float32 [1024], P(('dp', 'fsdp'))
- query_weight_grad: float32 [1024, 2048], P(('dp', 'fsdp'))
- key_weight_grad: float32 [1024, 1024], P(('dp', 'fsdp'))
- value_weight_grad: float32 [1024, 1024], P(('dp', 'fsdp'))
- output_weight_grad: float32 [2048, 1024], P(('dp', 'fsdp'))
- query_gain_grad: float32 [128], P(('dp', 'fsdp'))
- key_gain_grad: float32 [128], P(('dp', 'fsdp'))
- mlp_gain_grad: float32 [1024], P(('dp', 'fsdp'))
- gate_weight_grad: float32 [1024, 3072], P(('dp', 'fsdp'))
- up_weight_grad: float32 [1024, 3072], P(('dp', 'fsdp'))
- down_weight_grad: float32 [3072, 1024], P(('dp', 'fsdp'))
Inputs may be any that keep to these rules, and one draw needn't show every extreme that they name: In each sequence the positions take every value 0 to 8191 once; they come in runs of 128 consecutive rising positions that start at multiples of 128, one run to each device, in an order drawn at random.
All inputs are finite; a program needn't handle non-finite values.
Results may differ from a plain program's by a relative error of at most 0.025.
Values may be sent and summed in bfloat16 or wider, within the bound.
A program may use at most 448 MiB of HBM per device.

v0:
```python
import math

import jax
import jax.numpy as jnp
from jax import lax
from jax.sharding import PartitionSpec as P

QUERY_HEADS = 16
KEY_VALUE_HEADS = 8
HEAD_SIZE = 128


EPS = 1e-06
THETA = 1000000.0
NEGATIVE_LIMIT = -1e30


def rotary_tables(places, width):
    inverse = 1.0 / THETA ** (jnp.arange(0, width, 2, dtype=jnp.float32) / width)
    angle = places.astype(jnp.float32)[:, None] * inverse[None, :]
    return (jnp.cos(angle)[:, None, :], jnp.sin(angle)[:, None, :])


def apply_rotary(value, cosine_table, sine_table):
    half = value.shape[-1] // 2
    first, second = (value[..., :half], value[..., half:])
    return jnp.concatenate(
        [first * cosine_table - second * sine_table, second * cosine_table + first * sine_table],
        axis=-1,
    )


def rotary_reverse(grad, cosine_table, sine_table):
    half = grad.shape[-1] // 2
    first, second = (grad[..., :half], grad[..., half:])
    return jnp.concatenate(
        [first * cosine_table + second * sine_table, second * cosine_table - first * sine_table],
        axis=-1,
    )


def norm_apply(value, gain):
    inverse = lax.rsqrt(jnp.mean(value * value, axis=-1, keepdims=True) + EPS)
    return (value * inverse * gain, inverse)


def norm_back(value, inverse, gain, grad):
    width = value.shape[-1]
    scaled = grad * gain
    inner = jnp.sum(scaled * value, axis=-1, keepdims=True)
    value_grad = inverse * scaled - value * inverse * inverse * inverse * inner / width
    gain_grad = jnp.sum((grad * value * inverse).reshape(-1, width), axis=0)
    return (value_grad, gain_grad)


def block_scores(query_low, query_places, key_tile_block, key_places):
    row_count = key_tile_block.shape[0]
    key_tensor = key_tile_block.reshape(row_count, KEY_VALUE_HEADS, HEAD_SIZE)
    scores = jnp.einsum(
        "tkgd,rkd->kgtr", query_low, key_tensor, preferred_element_type=jnp.float32
    ) * HEAD_SIZE ** (-0.5)
    allowed = query_places[:, None] >= key_places[None, :]
    return (scores, allowed)


def split_blocks(whole):
    length_total = whole[0].shape[0]
    block_tile = math.gcd(length_total, 512)
    count_total = length_total // block_tile
    return (
        tuple((piece.reshape((count_total, block_tile) + piece.shape[1:]) for piece in whole)),
        count_total,
        block_tile,
    )


def local(
    hidden_in,
    positions,
    attn_gain,
    query_weight,
    key_matrix,
    value_matrix,
    output_weight,
    query_norm_gain,
    key_gain,
    mlp_gain,
    gate_weight,
    up_weight,
    down_weight,
    cotangent,
):
    attn_norm, query_full, key_full, value_full, output_full, query_norm, key_norm = (
        lax.all_gather(attn_gain, ("dp", "fsdp"), axis=0, tiled=True),
        lax.all_gather(query_weight, ("dp", "fsdp"), axis=0, tiled=True),
        lax.all_gather(key_matrix, ("dp", "fsdp"), axis=0, tiled=True),
        lax.all_gather(value_matrix, ("dp", "fsdp"), axis=0, tiled=True),
        lax.all_gather(output_weight, ("dp", "fsdp"), axis=0, tiled=True),
        lax.all_gather(query_norm_gain, ("dp", "fsdp"), axis=0, tiled=True),
        lax.all_gather(key_gain, ("dp", "fsdp"), axis=0, tiled=True),
    )
    token_rows = hidden_in.shape[1]
    query_groups = QUERY_HEADS // KEY_VALUE_HEADS
    scale = HEAD_SIZE ** (-0.5)
    places = positions[0]
    residual = hidden_in[0].astype(jnp.float32)
    cosine_table, sine_table = rotary_tables(places, HEAD_SIZE)
    attn_scale = attn_norm.astype(jnp.float32)
    normed, attn_inverse = norm_apply(residual, attn_scale)
    normed_low = normed.astype(jnp.bfloat16)
    query_prenorm = jnp.dot(normed_low, query_full, preferred_element_type=jnp.float32).reshape(
        token_rows, QUERY_HEADS, HEAD_SIZE
    )
    key_prenorm = jnp.dot(normed_low, key_full, preferred_element_type=jnp.float32).reshape(
        token_rows, KEY_VALUE_HEADS, HEAD_SIZE
    )
    value_rows = jnp.dot(normed_low, value_full, preferred_element_type=jnp.float32).astype(
        jnp.bfloat16
    )
    query_scale = query_norm.astype(jnp.float32)
    key_scale = key_norm.astype(jnp.float32)
    query_after_norm, query_inverse = norm_apply(query_prenorm, query_scale)
    key_after_norm, key_inverse = norm_apply(key_prenorm, key_scale)
    query_low = (
        apply_rotary(query_after_norm, cosine_table, sine_table)
        .astype(jnp.bfloat16)
        .reshape(token_rows, KEY_VALUE_HEADS, query_groups, HEAD_SIZE)
    )
    key_row_stack = (
        apply_rotary(key_after_norm, cosine_table, sine_table)
        .astype(jnp.bfloat16)
        .reshape(token_rows, KEY_VALUE_HEADS * HEAD_SIZE)
    )
    start_state = (
        jnp.full((KEY_VALUE_HEADS, query_groups, token_rows), NEGATIVE_LIMIT, jnp.float32),
        jnp.zeros((KEY_VALUE_HEADS, query_groups, token_rows), jnp.float32),
        jnp.zeros((KEY_VALUE_HEADS, query_groups, token_rows, HEAD_SIZE), jnp.float32),
    )
    key_tile_block = lax.all_gather(key_row_stack, ("ctx", "fsdp"), axis=0, tiled=True)
    value_tile_block = lax.all_gather(value_rows, ("ctx", "fsdp"), axis=0, tiled=True)
    key_places = lax.all_gather(places, ("ctx", "fsdp"), axis=0, tiled=True)
    row_count = key_tile_block.shape[0]

    def visit_work(state):
        best, total, accum = state
        scores, allowed = block_scores(query_low, places, key_tile_block, key_places)
        peak = jnp.max(jnp.where(allowed, scores, NEGATIVE_LIMIT), axis=-1)
        newbest = jnp.maximum(best, peak)
        weights = jnp.where(allowed, jnp.exp(scores - newbest[..., None]), 0.0)
        total = jnp.sum(weights, axis=-1)
        value_tensor = value_tile_block.reshape(row_count, KEY_VALUE_HEADS, HEAD_SIZE)
        accum = jnp.einsum(
            "kgtr,rkd->kgtd",
            weights.astype(jnp.bfloat16),
            value_tensor,
            preferred_element_type=jnp.float32,
        )
        return (newbest, total, accum)

    def keep_state(state):
        return state

    best, total, accum = lax.cond(
        jnp.min(key_places) <= jnp.max(places), visit_work, keep_state, start_state
    )
    attention_heads = accum / total[..., None]
    log_total = best + jnp.log(total)
    mixed_low = (
        jnp.transpose(attention_heads, (2, 0, 1, 3))
        .reshape(token_rows, QUERY_HEADS * HEAD_SIZE)
        .astype(jnp.bfloat16)
    )
    middle = residual + jnp.dot(mixed_low, output_full, preferred_element_type=jnp.float32)
    mlp_norm, gate_full, up_full, down_full = (
        lax.all_gather(mlp_gain, ("dp", "fsdp"), axis=0, tiled=True),
        lax.all_gather(gate_weight, ("dp", "fsdp"), axis=0, tiled=True),
        lax.all_gather(up_weight, ("dp", "fsdp"), axis=0, tiled=True),
        lax.all_gather(down_weight, ("dp", "fsdp"), axis=0, tiled=True),
    )
    mlp_scale = mlp_norm.astype(jnp.float32)
    normed_two, mlp_inverse = norm_apply(middle, mlp_scale)
    normed_two_low = normed_two.astype(jnp.bfloat16)
    gate = jnp.dot(normed_two_low, gate_full, preferred_element_type=jnp.float32)
    up = jnp.dot(normed_two_low, up_full, preferred_element_type=jnp.float32)
    sigma = jax.nn.sigmoid(gate)
    swish = gate * sigma
    inner_low = (swish * up).astype(jnp.bfloat16)
    layer_out = (middle + jnp.dot(inner_low, down_full, preferred_element_type=jnp.float32)).astype(
        jnp.bfloat16
    )
    cot_low = cotangent[0]
    down_wgrad = jnp.dot(inner_low.T, cot_low, preferred_element_type=jnp.float32)
    inner_grad = jnp.dot(cot_low, down_full.T, preferred_element_type=jnp.float32)
    gate_grad = (inner_grad * up * sigma * (1.0 + gate * (1.0 - sigma))).astype(jnp.bfloat16)
    up_grad = (inner_grad * swish).astype(jnp.bfloat16)
    gate_wgrad = jnp.dot(normed_two_low.T, gate_grad, preferred_element_type=jnp.float32)
    up_wgrad = jnp.dot(normed_two_low.T, up_grad, preferred_element_type=jnp.float32)
    normed_two_grad = jnp.dot(gate_grad, gate_full.T, preferred_element_type=jnp.float32) + jnp.dot(
        up_grad, up_full.T, preferred_element_type=jnp.float32
    )
    middle_back, mlp_gain_grad = norm_back(middle, mlp_inverse, mlp_scale, normed_two_grad)
    middle_grad = cot_low.astype(jnp.float32) + middle_back
    mlp_shards = (
        lax.psum_scatter(
            mlp_gain_grad.astype(jnp.bfloat16), ("dp", "fsdp"), scatter_dimension=0, tiled=True
        ).astype(jnp.float32),
        lax.psum_scatter(
            gate_wgrad.astype(jnp.bfloat16), ("dp", "fsdp"), scatter_dimension=0, tiled=True
        ).astype(jnp.float32),
        lax.psum_scatter(
            up_wgrad.astype(jnp.bfloat16), ("dp", "fsdp"), scatter_dimension=0, tiled=True
        ).astype(jnp.float32),
        lax.psum_scatter(
            down_wgrad.astype(jnp.bfloat16), ("dp", "fsdp"), scatter_dimension=0, tiled=True
        ).astype(jnp.float32),
    )
    branch_grad = middle_grad.astype(jnp.bfloat16)
    output_wgrad = jnp.dot(mixed_low.T, branch_grad, preferred_element_type=jnp.float32)
    blended_gradient = jnp.dot(
        branch_grad, output_full.T, preferred_element_type=jnp.float32
    ).astype(jnp.bfloat16)
    gradient_heads = blended_gradient.reshape(token_rows, KEY_VALUE_HEADS, query_groups, HEAD_SIZE)
    delta = jnp.sum(
        jnp.transpose(gradient_heads.astype(jnp.float32), (1, 2, 0, 3)) * attention_heads, axis=-1
    )
    stored = (
        lax.all_gather(key_row_stack, ("ctx", "fsdp"), axis=0, tiled=True),
        lax.all_gather(value_rows, ("ctx", "fsdp"), axis=0, tiled=True),
        lax.all_gather(places, ("ctx", "fsdp"), axis=0, tiled=True),
    )
    stacked_reverse, count_back, block_back = split_blocks(stored)

    def reverse_pass_step(query_acc, pieces):
        key_tile_block, value_tile_block, key_places = pieces
        row_count = key_tile_block.shape[0]

        def reverse_work(unused):
            scores, allowed = block_scores(query_low, places, key_tile_block, key_places)
            probs = jnp.where(allowed, jnp.exp(scores - log_total[..., None]), 0.0)
            value_tensor = value_tile_block.reshape(row_count, KEY_VALUE_HEADS, HEAD_SIZE)
            key_tensor = key_tile_block.reshape(row_count, KEY_VALUE_HEADS, HEAD_SIZE)
            prob_grad = jnp.einsum(
                "tkgd,rkd->kgtr", gradient_heads, value_tensor, preferred_element_type=jnp.float32
            )
            score_grad = (probs * (prob_grad - delta[..., None])).astype(jnp.bfloat16)
            query_increment = (
                jnp.einsum(
                    "kgtr,rkd->kgtd", score_grad, key_tensor, preferred_element_type=jnp.float32
                )
                * scale
            )
            key_increment = (
                jnp.einsum(
                    "kgtr,tkgd->rkd", score_grad, query_low, preferred_element_type=jnp.float32
                )
                * scale
            )
            value_increment = jnp.einsum(
                "kgtr,tkgd->rkd",
                probs.astype(jnp.bfloat16),
                gradient_heads,
                preferred_element_type=jnp.float32,
            )
            return (
                query_increment,
                key_increment.reshape(row_count, KEY_VALUE_HEADS * HEAD_SIZE),
                value_increment.reshape(row_count, KEY_VALUE_HEADS * HEAD_SIZE),
            )

        def skip(unused):
            return (
                jnp.zeros((KEY_VALUE_HEADS, query_groups, token_rows, HEAD_SIZE), jnp.float32),
                jnp.zeros((row_count, KEY_VALUE_HEADS * HEAD_SIZE), jnp.float32),
                jnp.zeros((row_count, KEY_VALUE_HEADS * HEAD_SIZE), jnp.float32),
            )

        query_increment, key_increment, value_increment = lax.cond(
            jnp.min(key_places) <= jnp.max(places), reverse_work, skip, 0
        )
        return (query_acc + query_increment, (key_increment, value_increment))

    query_acc, (key_portions, value_portions) = lax.scan(
        reverse_pass_step,
        jnp.zeros((KEY_VALUE_HEADS, query_groups, token_rows, HEAD_SIZE), jnp.float32),
        stacked_reverse,
    )
    length_total = count_back * block_back
    key_portions = key_portions.reshape(length_total, KEY_VALUE_HEADS * HEAD_SIZE)
    value_portions = value_portions.reshape(length_total, KEY_VALUE_HEADS * HEAD_SIZE)
    key_resident, value_local = (
        lax.psum_scatter(key_portions, ("ctx", "fsdp"), scatter_dimension=0, tiled=True),
        lax.psum_scatter(value_portions, ("ctx", "fsdp"), scatter_dimension=0, tiled=True),
    )
    query_total = jnp.transpose(query_acc, (2, 0, 1, 3)).reshape(token_rows, QUERY_HEADS, HEAD_SIZE)
    query_back = rotary_reverse(query_total, cosine_table, sine_table)
    query_pre_grad, query_gain_grad = norm_back(
        query_prenorm, query_inverse, query_scale, query_back
    )
    key_reverse = rotary_reverse(
        key_resident.reshape(token_rows, KEY_VALUE_HEADS, HEAD_SIZE), cosine_table, sine_table
    )
    key_prenorm_gradient, key_gain_grad = norm_back(
        key_prenorm, key_inverse, key_scale, key_reverse
    )
    query_pre_low = query_pre_grad.reshape(token_rows, QUERY_HEADS * HEAD_SIZE).astype(jnp.bfloat16)
    key_prenorm_reduced = key_prenorm_gradient.reshape(
        token_rows, KEY_VALUE_HEADS * HEAD_SIZE
    ).astype(jnp.bfloat16)
    value_low = value_local.astype(jnp.bfloat16)
    query_wgrad = jnp.dot(normed_low.T, query_pre_low, preferred_element_type=jnp.float32)
    key_wgrad = jnp.dot(normed_low.T, key_prenorm_reduced, preferred_element_type=jnp.float32)
    value_wgrad = jnp.dot(normed_low.T, value_low, preferred_element_type=jnp.float32)
    normed_grad = (
        jnp.dot(query_pre_low, query_full.T, preferred_element_type=jnp.float32)
        + jnp.dot(key_prenorm_reduced, key_full.T, preferred_element_type=jnp.float32)
        + jnp.dot(value_low, value_full.T, preferred_element_type=jnp.float32)
    )
    input_back, attn_gain_grad = norm_back(residual, attn_inverse, attn_scale, normed_grad)
    input_grad = middle_grad + input_back
    attn_shards = (
        lax.psum_scatter(
            attn_gain_grad.astype(jnp.bfloat16), ("dp", "fsdp"), scatter_dimension=0, tiled=True
        ).astype(jnp.float32),
        lax.psum_scatter(
            query_wgrad.astype(jnp.bfloat16), ("dp", "fsdp"), scatter_dimension=0, tiled=True
        ).astype(jnp.float32),
        lax.psum_scatter(
            key_wgrad.astype(jnp.bfloat16), ("dp", "fsdp"), scatter_dimension=0, tiled=True
        ).astype(jnp.float32),
        lax.psum_scatter(
            value_wgrad.astype(jnp.bfloat16), ("dp", "fsdp"), scatter_dimension=0, tiled=True
        ).astype(jnp.float32),
        lax.psum_scatter(
            output_wgrad.astype(jnp.bfloat16), ("dp", "fsdp"), scatter_dimension=0, tiled=True
        ).astype(jnp.float32),
        lax.psum_scatter(
            query_gain_grad.astype(jnp.bfloat16), ("dp", "fsdp"), scatter_dimension=0, tiled=True
        ).astype(jnp.float32),
        lax.psum_scatter(
            key_gain_grad.astype(jnp.bfloat16), ("dp", "fsdp"), scatter_dimension=0, tiled=True
        ).astype(jnp.float32),
    )
    totals = (
        lax.psum(attn_shards[0].astype(jnp.bfloat16), "ctx").astype(jnp.float32),
        lax.psum(attn_shards[1].astype(jnp.bfloat16), "ctx").astype(jnp.float32),
        lax.psum(attn_shards[2].astype(jnp.bfloat16), "ctx").astype(jnp.float32),
        lax.psum(attn_shards[3].astype(jnp.bfloat16), "ctx").astype(jnp.float32),
        lax.psum(attn_shards[4].astype(jnp.bfloat16), "ctx").astype(jnp.float32),
        lax.psum(attn_shards[5].astype(jnp.bfloat16), "ctx").astype(jnp.float32),
        lax.psum(attn_shards[6].astype(jnp.bfloat16), "ctx").astype(jnp.float32),
        lax.psum(mlp_shards[0].astype(jnp.bfloat16), "ctx").astype(jnp.float32),
        lax.psum(mlp_shards[1].astype(jnp.bfloat16), "ctx").astype(jnp.float32),
        lax.psum(mlp_shards[2].astype(jnp.bfloat16), "ctx").astype(jnp.float32),
        lax.psum(mlp_shards[3].astype(jnp.bfloat16), "ctx").astype(jnp.float32),
    )
    return (
        layer_out[None],
        input_grad[None],
        totals[0],
        totals[1],
        totals[2],
        totals[3],
        totals[4],
        totals[5],
        totals[6],
        totals[7],
        totals[8],
        totals[9],
        totals[10],
    )


def solution(mesh):
    in_specs = (
        P("dp", ("ctx", "fsdp"), None),
        P("dp", ("ctx", "fsdp")),
        P(("dp", "fsdp")),
        P(("dp", "fsdp"), None),
        P(("dp", "fsdp"), None),
        P(("dp", "fsdp"), None),
        P(("dp", "fsdp"), None),
        P(("dp", "fsdp")),
        P(("dp", "fsdp")),
        P(("dp", "fsdp")),
        P(("dp", "fsdp"), None),
        P(("dp", "fsdp"), None),
        P(("dp", "fsdp"), None),
        P("dp", ("ctx", "fsdp"), None),
    )
    out_specs = (
        P("dp", ("ctx", "fsdp"), None),
        P("dp", ("ctx", "fsdp"), None),
        P(("dp", "fsdp")),
        P(("dp", "fsdp"), None),
        P(("dp", "fsdp"), None),
        P(("dp", "fsdp"), None),
        P(("dp", "fsdp"), None),
        P(("dp", "fsdp")),
        P(("dp", "fsdp")),
        P(("dp", "fsdp")),
        P(("dp", "fsdp"), None),
        P(("dp", "fsdp"), None),
        P(("dp", "fsdp"), None),
    )
    return jax.shard_map(local, mesh=mesh, in_specs=in_specs, out_specs=out_specs, check_vma=False)
```

profile of v0, /device:TPU:1, one launch (start us, length us, event | category | flops | bytes accessed | tf_op | source)
XLA Modules:
  0.0 2486.6 jit_solution(58568732621285269)
XLA Ops:
  9.5 17.7 all-gather.1
  28.3 21.1 all-gather.19.cloned.1.call-done
  54.1 16.0 all-reduce.9
  71.0 20.9 all-gather.13.cloned.1.call-done
  100.4 15.4 all-gather.2
  116.5 157.2 %all-gather = s32[1,8192]{1,0:T(1,128)S(1)} all-gather(s32[1,128]{1,0:T(1,128)S(1)} %copy-done.55), channel_id=2, replica_groups=mesh['ctx'=16,'dp'=2,'fsdp'=4] {'ctx','fsdp'}, dimensions={1}, use_global_device_ids=true | all-gather | bytes 33280 | tf_op jit(solution)/shard_map/all_gather | solution.py:141
  289.7 77.5 %all-gather.15.cloned.1.call-done = bf16[8192,1024]{1,0:T(8,128)(2,1)} async-done(((bf16[128,1024]{1,0:T(8,128)(2,1)}), bf16[8192,1024]{1,0:T(8,128)(2,1)}) %all-gather.15.cloned.1.call-update) | async-done | bytes 16777232 | tf_op jit(solution)/shard_map/all_gather | solution.py:139
  367.2 114.5 %conditional.2 = (f32[8,2,128]{2,1,0:T(2,128)}, f32[8,2,128]{2,1,0:T(2,128)}, f32[8,2,128]{2,1,0:T(2,128)S(1)}, f32[8,2,128,128]{2,3,1,0:T(8,128)}) conditional(s32[]{:T(128)} %convert_element_type.214, () %tuple.46, (s32[1,128]{1,0:T(1,128)S(1)}, s32[8192]{0:T(1024)S(1)}, bf16[8192,1024]{1,0:T(8,128)(2,1)}, bf16[128,8,2,128]{0,3,2,1:T(8,128)(2,1)}, ...), branch_computations={%region_5.0_spmd, %region_6.9_spmd} | conditional | flops 8775530496 | bytes 358187648 | solution.py:163
  367.5 17.5 copy.158
  397.9 29.7 %fusion = (f32[8,2,128]{2,1,0:T(2,128)S(1)}, f32[8,8192,128,2]{2,1,3,0:T(8,128)}) fusion(pred[128,8192]{0,1:T(8,128)(4,1)S(1)} %broadcast_compare_fusion, bf16[128,8,2,128]{0,3,2,1:T(8,128)(2,1)} %get-tuple-element.375, bf16[8192,8,128,1]{2,1,0,3:T(8,128)(2,1)} %bitcast.218), kind=kOutput, calls=%fused_computation.2 | convolution fusion | flops 4345296896 | bytes 85467136 | tf_op jit(solution)/shard_map/cond/branch_1_fun/tkgd,rkd->kgtr/dot_general | solution.py:59
  428.1 29.8 %fusion.5 = f32[8,2,128,128]{2,3,1,0:T(8,128)} fusion(f32[8,8192,128,2]{2,1,3,0:T(8,128)} %get-tuple-element.443, f32[8,2,128]{2,1,0:T(2,128)} %broadcast_maximum_fusion, pred[128,8192]{0,1:T(8,128)(4,1)S(1)} %broadcast_compare_fusion, bf16[8192,8,128,1]{2,1,0,3:T(8,128)(2,1)} %bitcast.217), kind=kOutput, calls=%fused_computation.7 | convolution fusion | flops 4362076160 | bytes 85991424 | tf_op jit(solution)/shard_map/cond | solution.py:163
  457.9 22.8 fusion.4
  496.5 67.8 %all-gather.25.cloned.1.call-done = bf16[1024,3072]{1,0:T(8,128)(2,1)} async-done(((bf16[128,3072]{1,0:T(8,128)(2,1)}), bf16[1024,3072]{1,0:T(8,128)(2,1)}) %all-gather.25.cloned.1.call-update) | async-done | bytes 6291472 | tf_op jit(solution)/shard_map/all_gather | solution.py:176
  569.2 67.9 %all-gather.29.cloned.1.call-done = bf16[3072,1024]{1,0:T(8,128)(2,1)} async-done(((bf16[384,1024]{1,0:T(8,128)(2,1)}), bf16[3072,1024]{1,0:T(8,128)(2,1)}) %all-gather.29.cloned.1.call-update) | async-done | bytes 6291472 | tf_op jit(solution)/shard_map/all_gather | solution.py:178
  656.6 22.1 copy.106
  678.7 21.7 copy.107
  701.1 407.4 %while.17 = (s32[]{:T(128)}, f32[8,2,128,128]{3,2,1,0:T(8,128)}, f32[16,512,1024]{2,1,0:T(8,128)}, f32[16,512,1024]{2,1,0:T(8,128)}, s32[16,512]{1,0:T(8,128)}, ...) while((s32[]{:T(128)}, f32[8,2,128,128]{3,2,1,0:T(8,128)}, ...), condition=%wide.region_16.17_spmd.clone, body=%wide.region_12.16_spmd.clone.sunk | while | flops 1354039808 | bytes 62094644 | solution.py:282
  823.2 12.2 conditional.5
  875.6 12.3 conditional.5
  980.4 12.3 conditional.5
  1137.7 366.0 %reduce-scatter.12.cloned.1.call-done = f32[128,1024]{1,0:T(8,128)} async-done(((f32[8192,1024]{1,0:T(8,128)}), f32[128,1024]{1,0:T(8,128)}) %reduce-scatter.12.cloned.1.call-update) | async-done | bytes 524304 | tf_op jit(solution)/shard_map/reduce_scatter | solution.py:292
  1506.9 387.8 %reduce-scatter.10.cloned.1.call-done = f32[128,1024]{1,0:T(8,128)} async-done(((f32[8192,1024]{1,0:T(8,128)}), f32[128,1024]{1,0:T(8,128)}) %reduce-scatter.10.cloned.1.call-update) | async-done | bytes 524304 | tf_op jit(solution)/shard_map/reduce_scatter | solution.py:291
  1900.0 52.2 %reduce-scatter.20.cloned.1.call-done = bf16[256,1024]{1,0:T(8,128)(2,1)} async-done(((bf16[2048,1024]{1,0:T(8,128)(2,1)}), bf16[256,1024]{1,0:T(8,128)(2,1)}) %reduce-scatter.20.cloned.1.call-update) | async-done | bytes 524304 | tf_op jit(solution)/shard_map/reduce_scatter | solution.py:333
  1952.2 54.4 %reduce-scatter.14.cloned.1.call-done = bf16[128,2048]{1,0:T(8,128)(2,1)} async-done(((bf16[1024,2048]{1,0:T(8,128)(2,1)}), bf16[128,2048]{1,0:T(8,128)(2,1)}) %reduce-scatter.14.cloned.1.call-update) | async-done | bytes 524304 | tf_op jit(solution)/shard_map/reduce_scatter | solution.py:324
  2006.6 74.1 %reduce-scatter.26.cloned.1.call-done = bf16[384,1024]{1,0:T(8,128)(2,1)} async-done(((bf16[3072,1024]{1,0:T(8,128)(2,1)}), bf16[384,1024]{1,0:T(8,128)(2,1)}) %reduce-scatter.26.cloned.1.call-update) | async-done | bytes 786448 | tf_op jit(solution)/shard_map/reduce_scatter | solution.py:213
  2080.6 74.1 %reduce-scatter.24.cloned.1.call-done = bf16[128,3072]{1,0:T(8,128)(2,1)} async-done(((bf16[1024,3072]{1,0:T(8,128)(2,1)}), bf16[128,3072]{1,0:T(8,128)(2,1)}) %reduce-scatter.24.cloned.1.call-update) | async-done | bytes 786448 | tf_op jit(solution)/shard_map/reduce_scatter | solution.py:210
  2154.7 74.1 %reduce-scatter.22.cloned.1.call-done = bf16[128,3072]{1,0:T(8,128)(2,1)} async-done(((bf16[1024,3072]{1,0:T(8,128)(2,1)}), bf16[128,3072]{1,0:T(8,128)(2,1)}) %reduce-scatter.22.cloned.1.call-update) | async-done | bytes 786448 | tf_op jit(solution)/shard_map/reduce_scatter | solution.py:207
  2228.8 38.4 %reduce-scatter.18.cloned.1.call-done = bf16[128,1024]{1,0:T(8,128)(2,1)} async-done(((bf16[1024,1024]{1,0:T(8,128)(2,1)}), bf16[128,1024]{1,0:T(8,128)(2,1)}) %reduce-scatter.18.cloned.1.call-update) | async-done | bytes 262160 | tf_op jit(solution)/shard_map/reduce_scatter | solution.py:330
  2267.1 43.7 %reduce-scatter.16.cloned.1.call-done = bf16[128,1024]{1,0:T(8,128)(2,1)} async-done(((bf16[1024,1024]{1,0:T(8,128)(2,1)}), bf16[128,1024]{1,0:T(8,128)(2,1)}) %reduce-scatter.16.cloned.1.call-update) | async-done | bytes 262160 | tf_op jit(solution)/shard_map/reduce_scatter | solution.py:327
  2322.4 15.3 all-reduce.8
  2338.1 40.9 %all-reduce.6 = (bf16[128]{0:T(256)(128)(2,1)S(1)}, bf16[16]{0:T(256)(128)(2,1)S(1)}, bf16[16]{0:T(256)(128)(2,1)S(1)}, bf16[128]{0:T(256)(128)(2,1)S(1)}) all-reduce(bf16[128]{0:T(256)(128)(2,1)S(1)} %dynamic-slice.3, bf16[16]{0:T(256)(128)(2,1)S(1)} %dynamic-slice.5, ...), channel_id=1, replica_groups=mesh['ctx'=16,'dp'=2,'fsdp'=4] {'ctx'}, use_global_device_ids=true, to_apply=%region_24.25 | all-reduce | flops 288 | bytes 1152 | tf_op jit(solution)/shard_map/psum | solution.py:344
  2382.1 85.8 %all-reduce.12.cloned.1.call-done = (bf16[128,2048]{1,0:T(8,128)(2,1)}, bf16[128,1024]{1,0:T(8,128)(2,1)}, bf16[128,1024]{1,0:T(8,128)(2,1)}, bf16[256,1024]{1,0...) async-done(((bf16[128,2048]{1,0:T(8,128)(2,1)}, bf16[128,1024]{1,0:T(8,128)(2,1)}, bf16[128,1024]{1,0:T(8,128)(2,1)}, ...) | async-done | bytes 3932176 | tf_op jit(solution)/shard_map/psum | solution.py:345
  (501 shorter events, 683.0 us)
Async XLA Ops:
  7.2 42.1 %all-gather.19.cloned.1.call-start = ((), (), s32[]{:S(2)}) async-start(), calls=%async_computation.12 | async-start | bytes 2359296 | tf_op jit(solution)/shard_map/all_gather | solution.py:97
  8.0 86.8 %copy-start.3 = (bf16[1,128,1024]{2,1,0:T(8,128)(2,1)S(1)}, bf16[1,128,1024]{2,1,0:T(8,128)(2,1)}, u32[]{:S(2)}) copy-start(bf16[1,128,1024]{2,1,0:T(8,128)(2,1)} %param.20) | copy-start | bytes 786436
  8.0 84.0 %all-gather.13.cloned.1.call-start = ((), (), s32[]{:S(2)}) async-start(), calls=%async_computation.9 | async-start | bytes 2359296 | tf_op jit(solution)/shard_map/all_gather | solution.py:96
  8.7 268.7 %all-gather.17.cloned.1.call-start = ((), (), s32[]{:S(2)}) async-start(), calls=%async_computation.11 | async-start | bytes 4718592 | tf_op jit(solution)/shard_map/all_gather | solution.py:95
  9.5 280.2 %all-gather.21.cloned.1.call-start = ((), (), s32[]{:S(2)}) async-start(), calls=%async_computation.13 | async-start | bytes 17039360 | tf_op jit(solution)/shard_map/all_gather | solution.py:140
  27.2 256.7 %copy-start.44 = (f32[8,1,128]{2,1,0:T(1,128)}, f32[8,1,128]{2,1,0:T(1,128)S(1)}, u32[]{:S(2)}) copy-start(f32[8,1,128]{2,1,0:T(1,128)S(1)} %convert_element_type.266) | copy-start | bytes 12292
  28.3 255.6 %copy-start.49 = (f32[128]{0:T(128)}, f32[128]{0:T(128)S(1)}, u32[]{:S(2)}) copy-start(f32[128]{0:T(128)S(1)} %add_rsqrt_fusion.3) | copy-start | bytes 1540
  52.3 314.9 %all-gather.15.cloned.1.call-start = ((), (), s32[]{:S(2)}) async-start(), calls=%async_computation.10 | async-start | bytes 17039360 | tf_op jit(solution)/shard_map/all_gather | solution.py:139
  71.0 217.7 %copy-start.37 = (f32[128,64]{0,1:T(8,128)}, f32[128,64]{0,1:T(8,128)S(1)}, u32[]{:S(2)}) copy-start(f32[128,64]{0,1:T(8,128)S(1)} %get-tuple-element.459) | copy-start | bytes 98308
  71.0 217.7 %copy-start.39 = (f32[128,64]{0,1:T(8,128)}, f32[128,64]{0,1:T(8,128)S(1)}, u32[]{:S(2)}) copy-start(f32[128,64]{0,1:T(8,128)S(1)} %get-tuple-element.460) | copy-start | bytes 98308
  97.5 386.2 %all-gather.23.cloned.1.call-start = ((), (), s32[]{:S(2)}) async-start(), calls=%async_computation.14 | async-start | bytes 4718592 | tf_op jit(solution)/shard_map/all_gather | solution.py:98
  98.1 393.4 %all-gather.27.cloned.1.call-start = ((), (), s32[]{:S(2)}) async-start(), calls=%async_computation.16 | async-start | bytes 7077888 | tf_op jit(solution)/shard_map/all_gather | solution.py:177
  98.8 465.5 %all-gather.25.cloned.1.call-start = ((), (), s32[]{:S(2)}) async-start(), calls=%async_computation.15 | async-start | bytes 7077888 | tf_op jit(solution)/shard_map/all_gather | solution.py:176
  99.6 537.5 %all-gather.29.cloned.1.call-start = ((), (), s32[]{:S(2)}) async-start(), calls=%async_computation.17 | async-start | bytes 7077888 | tf_op jit(solution)/shard_map/all_gather | solution.py:178
  100.3 1403.3 %reduce-scatter.12.cloned.1.call-start = ((), (), s32[]{:S(2)}) async-start(), calls=%async_computation.19 | async-start | bytes 34078720 | tf_op jit(solution)/shard_map/reduce_scatter | solution.py:292
  100.4 187.1 %copy-start.61 = (f32[128]{0:T(128)}, f32[128]{0:T(128)S(1)}, u32[]{:S(2)}) copy-start(f32[128]{0:T(128)S(1)} %convert_element_type.222) | copy-start | bytes 1540
  367.2 116.5 %copy-start.4 = (bf16[1,128,1024]{2,1,0:T(8,128)(2,1)S(1)}, bf16[1,128,1024]{2,1,0:T(8,128)(2,1)}, u32[]{:S(2)}) copy-start(bf16[1,128,1024]{2,1,0:T(8,128)(2,1)} %param.20) | copy-start | bytes 786436
  486.9 165.5 %copy-start.9 = (f32[128,1024]{1,0:T(8,128)}, f32[128,1024]{1,0:T(8,128)S(1)}, u32[]{:S(2)}) copy-start(f32[128,1024]{1,0:T(8,128)S(1)} %get-tuple-element.470) | copy-start | bytes 1572868
  496.4 140.6 %copy-start.29 = (bf16[1,128,1024]{2,1,0:T(8,128)(2,1)S(1)}, bf16[1,128,1024]{2,1,0:T(8,128)(2,1)}, u32[]{:S(2)}) copy-start(bf16[1,128,1024]{2,1,0:T(8,128)(2,1)} %param.33) | copy-start | bytes 786436
  1108.6 786.1 %reduce-scatter.10.cloned.1.call-start = ((), (), s32[]{:S(2)}) async-start(), calls=%async_computation.18 | async-start | bytes 34078720 | tf_op jit(solution)/shard_map/reduce_scatter | solution.py:291
  1109.3 842.9 %reduce-scatter.20.cloned.1.call-start = ((), (), s32[]{:S(2)}) async-start(), calls=%async_computation.23 | async-start | bytes 4718592 | tf_op jit(solution)/shard_map/reduce_scatter | solution.py:333
  1113.1 893.5 %reduce-scatter.14.cloned.1.call-start = ((), (), s32[]{:S(2)}) async-start(), calls=%async_computation.20 | async-start | bytes 4718592 | tf_op jit(solution)/shard_map/reduce_scatter | solution.py:324
  1121.5 959.2 %reduce-scatter.26.cloned.1.call-start = ((), (), s32[]{:S(2)}) async-start(), calls=%async_computation.26 | async-start | bytes 7077888 | tf_op jit(solution)/shard_map/reduce_scatter | solution.py:213
  1126.2 1028.5 %reduce-scatter.24.cloned.1.call-start = ((), (), s32[]{:S(2)}) async-start(), calls=%async_computation.25 | async-start | bytes 7077888 | tf_op jit(solution)/shard_map/reduce_scatter | solution.py:210
  1132.0 1096.8 %reduce-scatter.22.cloned.1.call-start = ((), (), s32[]{:S(2)}) async-start(), calls=%async_computation.24 | async-start | bytes 7077888 | tf_op jit(solution)/shard_map/reduce_scatter | solution.py:207
  1137.6 759.1 %copy-start.21 = (f32[128,8,128]{0,2,1:T(8,128)S(1)}, f32[128,8,128]{0,2,1:T(8,128)}, u32[]{:S(2)}) copy-start(f32[128,8,128]{0,2,1:T(8,128)} %copy-done.20) | copy-start | bytes 1572868
  1137.6 759.1 %copy-start.52 = (f32[128,8]{0,1:T(8,128)S(1)}, f32[128,8]{0,1:T(8,128)}, u32[]{:S(2)}) copy-start(f32[128,8]{0,1:T(8,128)} %copy-done.51) | copy-start | bytes 12292
  1137.6 759.1 %copy-start.60 = (f32[128]{0:T(128)S(1)}, f32[128]{0:T(128)}, u32[]{:S(2)}) copy-start(f32[128]{0:T(128)} %copy-done.59) | copy-start | bytes 1540
  1137.6 1129.5 %reduce-scatter.18.cloned.1.call-start = ((), (), s32[]{:S(2)}) async-start(), calls=%async_computation.22 | async-start | bytes 2359296 | tf_op jit(solution)/shard_map/reduce_scatter | solution.py:330
  1506.9 804.0 %reduce-scatter.16.cloned.1.call-start = ((), (), s32[]{:S(2)}) async-start(), calls=%async_computation.21 | async-start | bytes 2359296 | tf_op jit(solution)/shard_map/reduce_scatter | solution.py:327
  1899.9 413.7 %copy-start.10 = (f32[128,1024]{1,0:T(8,128)S(1)}, f32[128,1024]{1,0:T(8,128)}, u32[]{:S(2)}) copy-start(f32[128,1024]{1,0:T(8,128)} %copy-done.9) | copy-start | bytes 1572868
  1899.9 568.0 %all-reduce.12.cloned.1.call-start = ((), (), s32[]{:S(2)}) async-start(), calls=%async_computation.27 | async-start | bytes 7864320 | tf_op jit(solution)/shard_map/psum | solution.py:345
  (72 other events, 691.8 us)
Sparse Core Ops, SparseCore 0:
  9.7 39.6 all-gather.18
  51.0 40.8 all-gather.12
  93.6 57.3 all-gather.16
  154.6 105.2 all-gather.20
  263.4 103.7 all-gather.14
  368.7 49.9 all-gather.22
  420.4 71.0 all-gather.26
  493.2 71.0 all-gather.24
  566.0 71.0 all-gather.28
  1108.7 394.9 reduce-scatter.11
  1506.1 388.5 reduce-scatter.9
  1896.9 55.2 reduce-scatter.19
  1954.6 51.9 reduce-scatter.13
  2008.8 71.7 reduce-scatter.25
  2082.9 71.7 reduce-scatter.23
  2157.0 71.7 reduce-scatter.21
  2231.0 36.0 reduce-scatter.17
  2269.4 41.3 reduce-scatter.15
  2313.9 153.9 all-reduce.11
where the time goes:
time: 2500 us; the launch traced here: 2490 us
  waiting for transfers between devices  1520 us (61%)
  matrix products  286 us (11%)
  local copies, waits for them, and re-layouts  267 us (11%)
  blocking collectives  263 us (11%)
  other arithmetic  115 us (5%)
    reduce_scatter x1, waiting for transfers between devices, local(): lax.psum_scatter(key_portions, ('ctx', 'fsdp'), scatter_dimension=0, tile...  388 us
    reduce_scatter x1, waiting for transfers between devices, local(): lax.psum_scatter(value_portions, ('ctx', 'fsdp'), scatter_dimension=0, ti...  366 us
    all_gather x1, blocking collectives, local(): key_places = lax.all_gather(places, ('ctx', 'fsdp'), axis=0, tiled=True)  157 us
    dynamic_update_slice x48, local copies, waits for them, and re-layouts, local(): lax.scan(reverse_pass_step, jnp.zeros((KEY_VALUE_HEADS, query_groups, tok...  143 us
    psum x1, waiting for transfers between devices, local(): lax.psum(attn_shards[1].astype(jnp.bfloat16), 'ctx').astype(jnp.float32)  85.8 us
    all_gather x1, waiting for transfers between devices, local(): lax.all_gather(key_row_stack, ('ctx', 'fsdp'), axis=0, tiled=True)  77.5 us
    reduce_scatter x1, waiting for transfers between devices, local(): lax.psum_scatter(down_wgrad.astype(jnp.bfloat16), ('dp', 'fsdp'), scatter...  74.1 us
    reduce_scatter x1, waiting for transfers between devices, local(): lax.psum_scatter(gate_wgrad.astype(jnp.bfloat16), ('dp', 'fsdp'), scatter...  74.1 us
  transfers between devices with their start and end apart: 19, of which 16 were waited for; matrix products, arithmetic and copies ran while one was open for 8% of the time, Pallas kernels for 0%

commit v1 on v0

v1 whole, which is shorter than its diff:
```python
import functools

import jax
import jax.numpy as jnp
from jax import lax
from jax.experimental import pallas as pl
from jax.experimental.pallas import tpu as pltpu
from jax.sharding import PartitionSpec as P

HEAD = 128
EPS = 1e-06
THETA = 1000000.0
SCALE = HEAD ** (-0.5)
LOG2E = 1.4426950408889634
RUN = 128
CHUNK = 512
BF = jnp.bfloat16
F32 = jnp.float32
MESH = pl.DeviceIdType.MESH


class Place:
    def __init__(self):
        self.ctx = lax.axis_index("ctx")
        self.dp = lax.axis_index("dp")
        self.fsdp = lax.axis_index("fsdp")
        self.chip = self.ctx // 2
        self.core = self.ctx % 2


def spread_tokens(me, k):
    head = me.dp * 4 + me.fsdp
    mine = me.core * 4 + me.fsdp
    n = (head + k) % 8
    slot = (mine + k) % 8
    dest = (me.chip * 2 + me.dp, n // 4, n % 4)
    source = (me.chip * 2 + slot // 4, me.core, slot % 4)
    return dest, n, source, slot, mine, me.core == me.dp


def return_tokens(me, k):
    head = me.dp * 4 + me.fsdp
    mine = me.core * 4 + me.fsdp
    n = (mine + k) % 8
    slot = (head + k) % 8
    dest = (me.chip * 2 + n // 4, me.core, n % 4)
    source = (me.chip * 2 + me.dp, slot // 4, slot % 4)
    return dest, n, source, slot, head, me.core == me.dp


def weight_group(me, k):
    head = me.dp * 4 + me.fsdp
    n = (head + k) % 8
    slot = (head + 8 - k) % 8
    dest = (me.ctx, n // 4, n % 4)
    source = (me.ctx, slot // 4, slot % 4)
    return dest, n, source, slot, head, True


def chips(me, k):
    n = (me.chip + k) % 8
    slot = (me.chip + 8 - k) % 8
    dest = (n * 2 + me.core, me.dp, me.fsdp)
    source = (slot * 2 + me.core, me.dp, me.fsdp)
    return dest, n, source, slot, me.chip, True


def exchange(moves, collective_id, out_shapes, *arrays):
    n_in, n_out = len(arrays), len(out_shapes)
    patterns = []
    for move in moves:
        if move[0] not in patterns:
            patterns.append(move[0])

    def kernel(*refs):
        ins, outs = refs[:n_in], refs[n_in : n_in + n_out]
        send_sem, recv_sem = refs[n_in + n_out :]
        me = Place()
        barrier = pltpu.get_barrier_semaphore()
        count = 0
        for pattern in patterns:
            for k in range(8):
                _, _, source, _, _, stays = pattern(me, k)
                if k == 0:
                    if stays is True:
                        continue

                    @pl.when(jnp.logical_not(stays))
                    def _():
                        pl.semaphore_signal(barrier, inc=1, device_id=source, device_id_type=MESH)

                    count = count + jnp.where(stays, 0, 1)
                else:
                    pl.semaphore_signal(barrier, inc=1, device_id=source, device_id_type=MESH)
                    count = count + 1
        pl.semaphore_wait(barrier, count)

        def remote(t, k):
            pattern, a, b, block, landing = moves[t]
            dest, n, _, slot, mine, _ = pattern(me, k)
            return pltpu.make_async_remote_copy(
                src_ref=block(ins[a], n),
                dst_ref=landing(outs[b], mine),
                send_sem=send_sem.at[t, k],
                recv_sem=recv_sem.at[t, mine],
                device_id=dest,
                device_id_type=MESH,
            )

        def arrival(t, k):
            pattern, a, b, block, landing = moves[t]
            dest, n, _, slot, mine, _ = pattern(me, k)
            return pltpu.make_async_remote_copy(
                src_ref=block(ins[a], n),
                dst_ref=landing(outs[b], slot),
                send_sem=send_sem.at[t, k],
                recv_sem=recv_sem.at[t, slot],
                device_id=dest,
                device_id_type=MESH,
            )

        def local(t):
            pattern, a, b, block, landing = moves[t]
            _, n, _, _, mine, _ = pattern(me, 0)
            return pltpu.make_async_copy(
                block(ins[a], n), landing(outs[b], mine), send_sem.at[t, 0]
            )

        def split(t, here, there):
            stays = moves[t][0](me, 0)[-1]
            if stays is True:
                here()
            else:
                pl.when(stays)(here)
                pl.when(jnp.logical_not(stays))(there)

        for k in range(1, 8):
            for t in range(len(moves)):
                remote(t, k).start()
        for t in range(len(moves)):
            split(t, lambda: local(t).start(), lambda: remote(t, 0).start())
        for t in range(len(moves)):
            split(t, lambda: local(t).wait(), lambda: remote(t, 0).wait_send())
            split(t, lambda: None, lambda: arrival(t, 0).wait_recv())
            for k in range(1, 8):
                remote(t, k).wait_send()
                arrival(t, k).wait_recv()

    return pl.pallas_call(
        kernel,
        out_shape=tuple(jax.ShapeDtypeStruct(s, d) for s, d in out_shapes),
        in_specs=[pl.BlockSpec(memory_space=pl.ANY)] * n_in,
        out_specs=tuple([pl.BlockSpec(memory_space=pl.ANY)] * n_out),
        scratch_shapes=[
            pltpu.SemaphoreType.DMA((len(moves), 8)),
            pltpu.SemaphoreType.DMA((len(moves), 8)),
        ],
        compiler_params=pltpu.CompilerParams(collective_id=collective_id, has_side_effects=True),
        name="exchange_%d" % collective_id,
    )(*arrays)


def whole(ref, n):
    return ref


def rows(size):
    def pick(ref, n):
        return ref.at[pl.ds(pl.multiple_of(n * size, size), size)]

    return pick


def columns(size):
    def pick(ref, n):
        return ref.at[:, pl.ds(pl.multiple_of(n * size, size), size)]

    return pick


def rows_at(size, start, width):
    def pick(ref, n):
        return ref.at[pl.ds(pl.multiple_of(n * size, size), size), pl.ds(start, width)]

    return pick


NT = (((1,), (1,)), ((), ()))
NN = (((1,), (0,)), ((), ()))


def mm(a, b, dims=NN):
    return lax.dot_general(a, b, dims, preferred_element_type=F32)


def stacked(ref):
    return jnp.concatenate([ref[:, :HEAD], ref[:, HEAD:]], axis=0)


def forward_kernel(order, own, q_ref, kv_ref, o_ref, l_ref, keys, vals, acc):
    step = pl.program_id(0)
    n_runs = order.shape[0]

    @pl.when(step == 0)
    def _():
        def place(r, _):
            src = pl.ds(pl.multiple_of(r * RUN, RUN), RUN)
            dst = pl.ds(pl.multiple_of(order[r] * RUN, RUN), RUN)
            keys[dst, :] = kv_ref[src, :HEAD]
            vals[dst, :HEAD] = kv_ref[src, HEAD:]
            vals[dst, HEAD:] = jnp.ones((RUN, HEAD), BF)
            return 0

        lax.fori_loop(0, n_runs, place, 0)

    run = own[step]
    query = stacked(q_ref)
    acc[...] = jnp.zeros_like(acc)

    def visit(j, masked):
        at = pl.ds(pl.multiple_of(j * CHUNK, CHUNK), CHUNK)
        s = mm(query, keys[at, :], NT)
        p = jnp.exp2(s * (SCALE * LOG2E))
        if masked:
            row = lax.broadcasted_iota(jnp.int32, p.shape, 0) % RUN + run * RUN
            col = lax.broadcasted_iota(jnp.int32, p.shape, 1) + j * CHUNK
            p = jnp.where(col <= row, p, 0.0)
        acc[...] += mm(p.astype(BF), vals[at, :])

    last = run // (CHUNK // RUN)

    def plain(j, _):
        visit(j, False)
        return 0

    lax.fori_loop(0, last, plain, 0)
    visit(last, True)
    total = acc[:, HEAD:]
    out = acc[:, :HEAD] / total
    log = jnp.log2(total)
    o_ref[:, :HEAD] = out[:RUN]
    o_ref[:, HEAD:] = out[RUN:]
    l_ref[:, :HEAD] = log[:RUN]
    l_ref[:, HEAD:] = log[RUN:]


def attention_forward(order, own, q, kv):
    length = kv.shape[0]
    tokens = q.shape[0]
    block = pl.BlockSpec((RUN, 2 * HEAD), lambda i, *_: (i, 0))
    return pl.pallas_call(
        forward_kernel,
        grid_spec=pltpu.PrefetchScalarGridSpec(
            num_scalar_prefetch=2,
            grid=(tokens // RUN,),
            in_specs=[block, pl.BlockSpec((length, 2 * HEAD), lambda i, *_: (0, 0))],
            out_specs=[block, block],
            scratch_shapes=[
                pltpu.VMEM((length, HEAD), BF),
                pltpu.VMEM((length, 2 * HEAD), BF),
                pltpu.VMEM((2 * RUN, 2 * HEAD), F32),
            ],
        ),
        out_shape=(jax.ShapeDtypeStruct(q.shape, F32), jax.ShapeDtypeStruct(q.shape, F32)),
        compiler_params=pltpu.CompilerParams(
            dimension_semantics=("arbitrary",), vmem_limit_bytes=48 * 2**20
        ),
        name="attention_forward",
    )(order, own, q, kv)


def backward_kernel(
    order, own, q_ref, g_ref, o_ref, l_ref, kv_ref, dq_ref, dkv_ref,
    keys, keys_t, vals, dk, dv, dq_t, q_t, g_t,
):
    step = pl.program_id(0)
    n_runs = order.shape[0]

    @pl.when(step == 0)
    def _():
        dk[...] = jnp.zeros_like(dk)
        dv[...] = jnp.zeros_like(dv)

        def place(r, _):
            src = pl.ds(pl.multiple_of(r * RUN, RUN), RUN)
            dst = pl.ds(pl.multiple_of(order[r] * RUN, RUN), RUN)
            k = kv_ref[src, :HEAD]
            keys[dst, :] = k
            keys_t[:, dst] = k.T
            vals[dst, :] = kv_ref[src, HEAD:]
            return 0

        lax.fori_loop(0, n_runs, place, 0)

    run = own[step]
    query = stacked(q_ref)
    grad = stacked(g_ref)
    q_t[...] = query.T
    g_t[...] = grad.T
    delta = jnp.sum((grad.astype(F32) * stacked(o_ref)).T, axis=0, keepdims=True)
    log = stacked(l_ref).T[:1]
    dq_t[...] = jnp.zeros_like(dq_t)

    def visit(j, masked):
        at = pl.ds(pl.multiple_of(j * CHUNK, CHUNK), CHUNK)
        s = mm(keys[at, :], q_t[...])
        p = jnp.exp2(s * (SCALE * LOG2E) - log)
        if masked:
            row = lax.broadcasted_iota(jnp.int32, p.shape, 1) % RUN + run * RUN
            col = lax.broadcasted_iota(jnp.int32, p.shape, 0) + j * CHUNK
            p = jnp.where(col <= row, p, 0.0)
        dp = mm(vals[at, :], g_t[...])
        ds = (p * (dp - delta)).astype(BF)
        dv[at, :] += mm(p.astype(BF), grad)
        dk[at, :] += mm(ds, query)
        dq_t[...] += mm(keys_t[:, at], ds)

    last = run // (CHUNK // RUN)

    def plain(j, _):
        visit(j, False)
        return 0

    lax.fori_loop(0, last, plain, 0)
    visit(last, True)
    out = dq_t[...].T * SCALE
    dq_ref[:, :HEAD] = out[:RUN]
    dq_ref[:, HEAD:] = out[RUN:]

    @pl.when(step == pl.num_programs(0) - 1)
    def _():
        def give(r, _):
            dst = pl.ds(pl.multiple_of(r * RUN, RUN), RUN)
            src = pl.ds(pl.multiple_of(order[r] * RUN, RUN), RUN)
            dkv_ref[dst, :HEAD] = (dk[src, :] * SCALE).astype(BF)
            dkv_ref[dst, HEAD:] = dv[src, :].astype(BF)
            return 0

        lax.fori_loop(0, n_runs, give, 0)


def attention_backward(order, own, q, g, o, log, kv):
    length = kv.shape[0]
    tokens = q.shape[0]
    block = pl.BlockSpec((RUN, 2 * HEAD), lambda i, *_: (i, 0))
    all_rows = pl.BlockSpec((length, 2 * HEAD), lambda i, *_: (0, 0))
    return pl.pallas_call(
        backward_kernel,
        grid_spec=pltpu.PrefetchScalarGridSpec(
            num_scalar_prefetch=2,
            grid=(tokens // RUN,),
            in_specs=[block, block, block, block, all_rows],
            out_specs=[block, all_rows],
            scratch_shapes=[
                pltpu.VMEM((length, HEAD), BF),
                pltpu.VMEM((HEAD, length), BF),
                pltpu.VMEM((length, HEAD), BF),
                pltpu.VMEM((length, HEAD), F32),
                pltpu.VMEM((length, HEAD), F32),
                pltpu.VMEM((HEAD, 2 * RUN), F32),
                pltpu.VMEM((HEAD, 2 * RUN), BF),
                pltpu.VMEM((HEAD, 2 * RUN), BF),
            ],
        ),
        out_shape=(jax.ShapeDtypeStruct(q.shape, F32), jax.ShapeDtypeStruct(kv.shape, BF)),
        compiler_params=pltpu.CompilerParams(
            dimension_semantics=("arbitrary",), vmem_limit_bytes=48 * 2**20
        ),
        name="attention_backward",
    )(order, own, q, g, o, log, kv)


def rotate(value, cos, sin):
    a, b = value[..., : HEAD // 2], value[..., HEAD // 2 :]
    return jnp.concatenate([a * cos - b * sin, b * cos + a * sin], axis=-1)


def rotate_back(grad, cos, sin):
    a, b = grad[..., : HEAD // 2], grad[..., HEAD // 2 :]
    return jnp.concatenate([a * cos + b * sin, b * cos - a * sin], axis=-1)


def inverse_rms(value):
    return lax.rsqrt(jnp.mean(value * value, axis=-1, keepdims=True) + EPS)


def norm_back(value, inverse, gain, grad):
    scaled = grad * gain
    inner = jnp.sum(scaled * value, axis=-1, keepdims=True)
    return inverse * scaled - value * inverse * inverse * inverse * inner / value.shape[-1]


def dot(a, b):
    return jnp.dot(a, b, preferred_element_type=F32)


def dot_t(a, b):
    return lax.dot_general(a, b, (((0,), (0,)), ((), ())), preferred_element_type=F32)


def summed(parts, count):
    return jnp.sum(parts.reshape((count, -1) + parts.shape[1:]).astype(F32), axis=0)


def row_of(vector):
    return jnp.pad(vector.reshape(1, -1), ((0, 0), (0, 128 - vector.shape[-1])))


def local(
    hidden_in, positions, attn_gain, query_weight, key_matrix, value_matrix, output_weight,
    query_norm_gain, key_gain, mlp_gain, gate_weight, up_weight, down_weight, cotangent,
):
    hidden = hidden_in[0]
    cot = cotangent[0]
    tokens, width = hidden.shape
    group = 8 * tokens
    ff = gate_weight.shape[1] // 8
    part = width // 8

    place_tile = jnp.broadcast_to(positions, (8, tokens))
    gain_tile = jnp.concatenate(
        [row_of(g.astype(F32)) for g in (attn_gain, mlp_gain, query_norm_gain, key_gain)]
        + [jnp.zeros((4, 128), F32)],
        axis=0,
    )
    x_all, places, gains, w_qkv = exchange(
        (
            (spread_tokens, 0, 0, whole, rows(tokens)),
            (spread_tokens, 1, 1, whole, rows(8)),
            (weight_group, 2, 2, whole, rows(8)),
            (weight_group, 3, 3, columns(256), rows_at(part, 0, 256)),
            (weight_group, 4, 3, columns(128), rows_at(part, 256, 128)),
            (weight_group, 5, 3, columns(128), rows_at(part, 384, 128)),
        ),
        1,
        (((group, width), BF), ((64, tokens), jnp.int32), ((64, 128), F32), ((width, 512), BF)),
        hidden, place_tile, gain_tile, query_weight, key_matrix, value_matrix,
    )
    gains = gains.reshape(8, 8, 128)
    attn_scale = gains[:, 0].reshape(1, width)
    mlp_scale = gains[:, 1].reshape(1, width)
    query_scale = gains[:, 2, :16].reshape(1, HEAD)
    key_scale = gains[:, 3, :16].reshape(1, HEAD)

    x_wide = x_all.astype(F32)
    attn_inverse_all = inverse_rms(x_wide)
    norm_one = (x_wide * attn_inverse_all * attn_scale).astype(BF)
    qkv = dot(norm_one, w_qkv)
    pre = qkv[:, :384].reshape(group, 3, HEAD)
    head_scale = jnp.stack([query_scale, query_scale, key_scale], axis=1)
    head_inverse = inverse_rms(pre)
    place_rows = places.reshape(8, 8, tokens)[:, 0].reshape(group)
    frequency = 1.0 / THETA ** (jnp.arange(0, HEAD, 2, dtype=F32) / HEAD)
    angle = place_rows.astype(F32)[:, None] * frequency[None, :]
    cos, sin = jnp.cos(angle)[:, None, :], jnp.sin(angle)[:, None, :]
    turned = rotate(pre * head_inverse * head_scale, cos, sin).astype(BF).reshape(group, 384)
    queries = turned[:, :256]
    kv = jnp.concatenate([turned[:, 256:], qkv[:, 384:].astype(BF)], axis=1)

    kv_all, all_places, cot_all, w_gu = exchange(
        (
            (chips, 0, 0, whole, rows(group)),
            (chips, 1, 1, whole, rows(64)),
            (spread_tokens, 2, 2, whole, rows(tokens)),
            (weight_group, 3, 3, columns(ff), rows_at(part, 0, ff)),
            (weight_group, 4, 3, columns(ff), rows_at(part, ff, ff)),
        ),
        2,
        (((8 * group, 256), BF), ((512, tokens), jnp.int32), ((group, width), BF), ((width, 2 * ff), BF)),
        kv, places, cot, gate_weight, up_weight,
    )
    order = all_places.reshape(64, 8, tokens)[:, 0, 0] // RUN
    own = places.reshape(8, 8, tokens)[:, 0, 0] // RUN
    attention, log_total = attention_forward(order, own, queries, kv_all)
    mixed = attention.astype(BF)
    branch_part = dot(mixed, output_weight).astype(BF)

    (branch,) = exchange(
        ((return_tokens, 0, 0, rows(tokens), rows(tokens)),), 3, (((group, width), BF),), branch_part
    )
    residual = hidden.astype(F32)
    middle = residual + summed(branch, 8)
    mlp_inverse = inverse_rms(middle)
    norm_two_own = (middle * mlp_inverse * mlp_scale).astype(BF)

    (norm_two,) = exchange(
        ((spread_tokens, 0, 0, whole, rows(tokens)),), 4, (((group, width), BF),), norm_two_own
    )
    gate_up = dot(norm_two, w_gu)
    gate, up = gate_up[:, :ff], gate_up[:, ff:]
    sigma = jax.nn.sigmoid(gate)
    swish = gate * sigma
    inner = (swish * up).astype(BF)
    inner_grad = lax.dot_general(cot_all, down_weight, NT, preferred_element_type=F32)
    gate_up_grad = jnp.concatenate(
        [
            (inner_grad * up * sigma * (1.0 + gate * (1.0 - sigma))).astype(BF),
            (inner_grad * swish).astype(BF),
        ],
        axis=1,
    )
    norm_two_part = lax.dot_general(gate_up_grad, w_gu, NT, preferred_element_type=F32).astype(BF)

    (norm_two_parts,) = exchange(
        ((return_tokens, 0, 0, rows(tokens), rows(tokens)),), 5, (((group, width), BF),), norm_two_part
    )
    norm_two_grad = summed(norm_two_parts, 8)
    middle_grad = cot.astype(F32) + norm_back(middle, mlp_inverse, mlp_scale, norm_two_grad)
    mlp_gain_part = jnp.sum(norm_two_grad * middle * mlp_inverse, axis=0)
    branch_grad_own = middle_grad.astype(BF)
    down_part = dot(inner, down_weight).astype(BF)
    down_wgrad = dot_t(inner, cot_all).astype(BF)
    gate_up_wgrad = dot_t(norm_two, gate_up_grad).astype(BF)

    branch_grad, gate_wgrad, up_wgrad = exchange(
        (
            (spread_tokens, 0, 0, whole, rows(tokens)),
            (weight_group, 1, 1, lambda r, n: rows_at(part, 0, ff)(r, n), columns(ff)),
            (weight_group, 1, 2, lambda r, n: rows_at(part, ff, ff)(r, n), columns(ff)),
        ),
        6,
        (((group, width), BF), ((part, 8 * ff), BF), ((part, 8 * ff), BF)),
        branch_grad_own, gate_up_wgrad,
    )
    mixed_grad = lax.dot_general(branch_grad, output_weight, NT, preferred_element_type=F32).astype(BF)
    output_wgrad = dot_t(mixed, branch_grad).astype(BF)
    gate_wgrad, up_wgrad, down_wgrad, output_wgrad = lax.psum(
        (gate_wgrad, up_wgrad, down_wgrad, output_wgrad), "ctx"
    )
    query_turn, kv_part = attention_backward(
        order, own, queries, mixed_grad, attention, log_total, kv_all
    )

    kv_parts, down_parts = exchange(
        (
            (chips, 0, 0, rows(group), rows(group)),
            (return_tokens, 1, 1, rows(tokens), rows(tokens)),
        ),
        7,
        (((8 * group, 256), BF), ((group, width), BF)),
        kv_part, down_part,
    )
    layer_out = (middle + summed(down_parts, 8)).astype(BF)
    kv_sum = summed(kv_parts, 8)
    turn = jnp.concatenate([query_turn, kv_sum[:, :HEAD]], axis=1).reshape(group, 3, HEAD)
    head_grad = rotate_back(turn, cos, sin)
    pre_grad = norm_back(pre, head_inverse, head_scale, head_grad)
    head_gain_parts = jnp.sum(head_grad * pre * head_inverse, axis=0)
    qkv_grad = jnp.concatenate(
        [pre_grad.reshape(group, 384).astype(BF), kv_sum[:, HEAD:].astype(BF)], axis=1
    )
    qkv_wgrad = dot_t(norm_one, qkv_grad).astype(BF)
    norm_one_wide = lax.dot_general(qkv_grad, w_qkv, NT, preferred_element_type=F32)
    attn_gain_part = jnp.sum(norm_one_wide * x_wide * attn_inverse_all, axis=0)
    query_gain_part = (head_gain_parts[0] + head_gain_parts[1]).reshape(8, 1, 16)
    key_gain_part = head_gain_parts[2].reshape(8, 1, 16)
    gain_parts = jnp.concatenate(
        [
            attn_gain_part.reshape(8, 1, 128),
            mlp_gain_part.reshape(8, 1, 128),
            jnp.pad(query_gain_part, ((0, 0), (0, 0), (0, 112))),
            jnp.pad(key_gain_part, ((0, 0), (0, 0), (0, 112))),
            jnp.zeros((8, 4, 128), F32),
        ],
        axis=1,
    ).reshape(64, 128)

    norm_one_parts, query_wgrad, key_wgrad, value_wgrad, gain_sums = exchange(
        (
            (return_tokens, 0, 0, rows(tokens), rows(tokens)),
            (weight_group, 1, 1, rows_at(part, 0, 256), columns(256)),
            (weight_group, 1, 2, rows_at(part, 256, 128), columns(128)),
            (weight_group, 1, 3, rows_at(part, 384, 128), columns(128)),
            (weight_group, 2, 4, rows(8), rows(8)),
        ),
        8,
        (
            ((group, width), BF), ((part, 2048), BF), ((part, 1024), BF), ((part, 1024), BF),
            ((64, 128), F32),
        ),
        norm_one_wide.astype(BF), qkv_wgrad, gain_parts,
    )
    gain_sum = summed(gain_sums, 8)
    query_wgrad, key_wgrad, value_wgrad, gain_sum = lax.psum(
        (query_wgrad, key_wgrad, value_wgrad, gain_sum.astype(BF)), "ctx"
    )
    attn_inverse = inverse_rms(residual)
    input_grad = middle_grad + norm_back(residual, attn_inverse, attn_scale, summed(norm_one_parts, 8))
    gain_sum = gain_sum.astype(F32)
    return (
        layer_out[None],
        input_grad[None],
        gain_sum[0],
        query_wgrad.astype(F32),
        key_wgrad.astype(F32),
        value_wgrad.astype(F32),
        output_wgrad.astype(F32),
        gain_sum[2, :16],
        gain_sum[3, :16],
        gain_sum[1],
        gate_wgrad.astype(F32),
        up_wgrad.astype(F32),
        down_wgrad.astype(F32),
    )


def solution(mesh):
    tokens = P("dp", ("ctx", "fsdp"), None)
    places = P("dp", ("ctx", "fsdp"))
    vector = P(("dp", "fsdp"))
    matrix = P(("dp", "fsdp"), None)
    in_specs = (
        tokens, places, vector, matrix, matrix, matrix, matrix,
        vector, vector, vector, matrix, matrix, matrix, tokens,
    )
    out_specs = (
        tokens, tokens, vector, matrix, matrix, matrix, matrix,
        vector, vector, vector, matrix, matrix, matrix,
    )
    return jax.shard_map(local, mesh=mesh, in_specs=in_specs, out_specs=out_specs, check_vma=False)
```

time: 2500 us -> 769 us (0.31)
  waiting for transfers between devices: 1520 us -> 113 us
  Pallas kernels: 0 us -> 520 us
  matrix products: 286 us -> 31.7 us
  local copies, waits for them, and re-layouts: 267 us -> 18 us
  blocking collectives: 263 us -> 37.7 us
  other arithmetic: 115 us -> 35.9 us
    reduce_scatter x9 -> x0, waiting for transfers between devices: 1160 us -> none  [the longest x1 388 us: local(): lax.psum_scatter(key_portions, ('ctx', 'fsdp'), scatter_dimension=0, tile...]
    pallas_call x0 -> x10, Pallas kernels: none -> 520 us  [the longest x8 445 us: exchange(): pl.pallas_call(kernel, out_shape=tuple((jax.ShapeDtypeStruct(s, d) for s,...]
    all_gather x9 -> x0, waiting for transfers between devices: 260 us -> none  [the longest x1 77.5 us: local(): lax.all_gather(key_row_stack, ('ctx', 'fsdp'), axis=0, tiled=True)]
    dot_general x97 -> x12, matrix products: 256 us -> 31.7 us  [the longest x4 11.4 us: dot(): return jnp.dot(a, b, preferred_element_type=F32)]
    all_gather x3 -> x0, blocking collectives: 190 us -> none  [the longest x1 157 us: local(): key_places = lax.all_gather(places, ('ctx', 'fsdp'), axis=0, tiled=True)]
    dynamic_update_slice x48 -> x0, local copies, waits for them, and re-layouts: 143 us -> none  [local(): lax.scan(reverse_pass_step, jnp.zeros((KEY_VALUE_HEADS, query_groups, tok...]
    unnamed x142 -> x81, local copies, waits for them, and re-layouts: 54.6 us -> 7.54 us
    add x20 -> x2, other arithmetic: 38 us -> 1.58 us  [the longest x1 1.37 us: local(): middle_grad + norm_back(residual, attn_inverse, attn_scale, summed(norm_o...]
  transfers between devices with their start and end apart: 19 -> 1, of which waited for: 16 -> 1; matrix products, arithmetic and copies ran while one was open for 8% -> 1% of each run, Pallas kernels for 0% -> 0%
where the time goes in v1:
time: 769 us; the launch traced here: 771 us
  Pallas kernels  520 us (68%)
  waiting for transfers between devices  113 us (15%)
  blocking collectives  37.7 us (5%)
  other arithmetic  35.9 us (5%)
  matrix products  31.7 us (4%)
  local copies, waits for them, and re-layouts  18 us (2%)
  between operations  14.6 us (2%)
    pallas_call x8, Pallas kernels, exchange(): pl.pallas_call(kernel, out_shape=tuple((jax.ShapeDtypeStruct(s, d) for s,...  445 us
    psum x1, waiting for transfers between devices, local(): lax.psum((query_wgrad, key_wgrad, value_wgrad, gain_sum.astype(BF)), 'ctx')  113 us
    pallas_call x1, Pallas kernels, attention_backward(): pl.pallas_call(backward_kernel, grid_spec=pltpu.PrefetchScalarGridSpec(nu...  44.6 us
    psum x1, blocking collectives, local(): lax.psum((query_wgrad, key_wgrad, value_wgrad, gain_sum.astype(BF)), 'ctx')  37.7 us
    pallas_call x1, Pallas kernels, attention_forward(): pl.pallas_call(forward_kernel, grid_spec=pltpu.PrefetchScalarGridSpec(num...  30.7 us
  transfers between devices with their start and end apart: 1, of which 1 were waited for; matrix products, arithmetic and copies ran while one was open for 1% of the time, Pallas kernels for 0%

profile of v1, /device:TPU:1, one launch (start us, length us, event | category | flops | bytes accessed | tf_op | source)
XLA Modules:
  0.0 771.4 jit_solution(11687469914762217349)
XLA Ops:
  10.5 51.5 %exchange_1.1 = (bf16[1024,1024]{1,0:T(8,128)(2,1)}, s32[64,128]{1,0:T(8,128)}, f32[64,128]{1,0:T(8,128)}, bf16[1024,512]{1,0:T(8,128)(2,1)}) custom-call(bf16[128,1024]{1,0:T(8,128)(2,1)} %bitcast.161, s32[8,128]{1,0:T(8,128)} %broadcast_in_dim.9.refs_1_, f32[8,128]{1,0:T(8,128)} %concatenate.27.refs_2_, bf16[128,2048]{1,0:T(8,128)(2,1)} %refs_3_.2, ...), custom_call_target="tpu_custom_call" | custom-call | tf_op jit(solution)/shard_map/exchange_1/pallas_call | solution.py:149
  65.4 2.1 fusion.1
  67.5 2.7 fusion.17
  75.4 108.3 %exchange_2.1 = (bf16[8192,256]{1,0:T(8,128)(2,1)}, s32[512,128]{1,0:T(8,128)}, bf16[1024,1024]{1,0:T(8,128)(2,1)}, bf16[1024,768]{1,0:T(8,128)(2,1)}) custom-call(bf16[1024,256]{1,0:T(8,128)(2,1)} %pad_maximum_fusion.9.refs_0_, s32[64,128]{1,0:T(8,128)} %get-tuple-element.38.refs_1_, bf16[128,1024]{1,0:T(8,128)(2,1)} %bitcast.168, ...), custom_call_target="tpu_custom_call" | custom-call | tf_op jit(solution)/shard_map/exchange_2/pallas_call | solution.py:149
  184.8 30.7 %attention_forward.1 = (f32[1024,256]{1,0:T(8,128)S(1)}, f32[1024,256]{1,0:T(8,128)S(1)}) custom-call(s32[64]{0:T(128)S(1)} %and_select_fusion.1.order, s32[8]{0:T(128)S(1)} %and_select_fusion.own, bf16[1024,256]{1,0:T(8,128)(2,1)S(1)} %copy.55.q_ref, bf16[8192,256]{1,0:T(8,128)(2,1)} %get-tuple-element.40.kv_ref), custom_call_target="tpu_custom_call" | custom-call | tf_op jit(solution)/shard_map/attention_forward/pallas_call | solution.py:251
  216.4 2.1 convolution_convert_fusion.1.refs_0_
  218.5 38.9 %exchange_3.1 = bf16[1024,1024]{1,0:T(8,128)(2,1)} custom-call(bf16[1024,1024]{1,0:T(8,128)(2,1)} %convolution_convert_fusion.1.refs_0_), custom_call_target="tpu_custom_call" | custom-call | tf_op jit(solution)/shard_map/exchange_3/pallas_call | solution.py:149
  257.4 2.1 convert_reduce_fusion.4
  260.5 32.4 %exchange_4.1 = bf16[1024,1024]{1,0:T(8,128)(2,1)} custom-call(bf16[128,1024]{1,0:T(8,128)(2,1)} %multiply_convert_fusion.3.refs_0_), custom_call_target="tpu_custom_call" | custom-call | tf_op jit(solution)/shard_map/exchange_4/pallas_call | solution.py:149
  292.9 4.1 fusion.43
  297.0 2.5 multiply_convert_fusion.2
  299.5 3.0 convolution_convert_fusion.3.refs_1_
  302.5 3.2 convolution_convert_fusion.2.refs_0_
  305.7 31.3 %exchange_5.1 = bf16[1024,1024]{1,0:T(8,128)(2,1)} custom-call(bf16[1024,1024]{1,0:T(8,128)(2,1)} %convolution_convert_fusion.2.refs_0_), custom_call_target="tpu_custom_call" | custom-call | tf_op jit(solution)/shard_map/exchange_5/pallas_call | solution.py:149
  337.0 2.1 convert_reduce_fusion.3
  340.9 56.0 %exchange_6.1 = (bf16[1024,1024]{1,0:T(8,128)(2,1)}, bf16[128,3072]{1,0:T(8,128)(2,1)}, bf16[128,3072]{1,0:T(8,128)(2,1)}) custom-call(bf16[128,1024]{1,0:T(8,128)(2,1)} %add_convert_fusion.1.refs_0_, bf16[1024,768]{1,0:T(8,128)(2,1)} %convolution_convert_fusion.3.refs_1_), custom_call_target="tpu_custom_call" | custom-call | tf_op jit(solution)/shard_map/exchange_6/pallas_call | solution.py:149
  396.9 3.3 convolution_convert_fusion.6
  401.9 1.9 convolution_convert_fusion.5
  403.8 2.6 convolution_convert_fusion.refs_1_
  406.4 44.6 %attention_backward.1 = (f32[1024,256]{1,0:T(8,128)S(1)}, bf16[8192,256]{1,0:T(8,128)(2,1)}) custom-call(s32[64]{0:T(128)S(1)} %and_select_fusion.1.order, s32[8]{0:T(128)S(1)} %and_select_fusion.own, bf16[1024,256]{1,0:T(8,128)(2,1)S(1)} %copy.55.q_ref, bf16[1024,256]{1,0:T(8,128)(2,1)S(1)} %convolution_convert_fusion.7.g_ref, ...), custom_call_target="tpu_custom_call" | custom-call | tf_op jit(solution)/shard_map/attention_backward/pallas_call | solution.py:347
  450.9 84.5 %exchange_7.1 = (bf16[8192,256]{1,0:T(8,128)(2,1)}, bf16[1024,1024]{1,0:T(8,128)(2,1)}) custom-call(bf16[8192,256]{1,0:T(8,128)(2,1)} %get-tuple-element.46.refs_0_, bf16[1024,1024]{1,0:T(8,128)(2,1)} %convolution_convert_fusion.refs_1_), custom_call_target="tpu_custom_call" | custom-call | tf_op jit(solution)/shard_map/exchange_7/pallas_call | solution.py:149
  535.5 2.9 convert_reduce_fusion
  540.4 1.9 copy.46
  546.4 2.9 fusion.10
  549.3 2.6 convolution_convert_fusion.4.refs_1_
  551.9 3.2 fusion.5
  555.9 42.2 %exchange_8.1 = (bf16[1024,1024]{1,0:T(8,128)(2,1)}, bf16[128,2048]{1,0:T(8,128)(2,1)}, bf16[128,1024]{1,0:T(8,128)(2,1)}, bf16[128,1024]{1,0:T(8,128)(2,1)}, f32[64,128]{1,0:T(8,128)}) custom-call(bf16[1024,1024]{1,0:T(8,128)(2,1)} %get-tuple-element.70.refs_0_, bf16[1024,512]{1,0:T(8,128)(2,1)} %convolution_convert_fusion.4.refs_1_, f32[64,128]{1,0:T(8,128)} %bitcast.171), custom_call_target="tpu_custom_call" | custom-call | tf_op jit(solution)/shard_map/exchange_8/pallas_call | solution.py:149
  598.8 37.7 %psum.56 = bf16[8,128]{1,0:T(8,128)(2,1)S(1)} all-reduce(bf16[8,128]{1,0:T(8,128)(2,1)S(1)} %bitcast_reduce_fusion), channel_id=1, replica_groups=mesh['ctx'=16,'dp'=2,'fsdp'=4] {'ctx'}, use_global_device_ids=true, to_apply=%region_16.17 | all-reduce | flops 1024 | bytes 4096 | tf_op jit(solution)/shard_map/psum | solution.py:584
  636.5 2.0 convert_reduce_fusion.1
  641.6 113.1 %all-reduce.7.cloned.1.call-done = (bf16[128,2048]{1,0:T(8,128)(2,1)}, bf16[128,1024]{1,0:T(8,128)(2,1)}, bf16[128,1024]{1,0:T(8,128)(2,1)}, bf16[256,1024]{1,0:...) async-done(((bf16[128,2048]{1,0:T(8,128)(2,1)}, bf16[128,1024]{1,0:T(8,128)(2,1)}, bf16[128,1024]{1,0:T(8,128)(2,1)}, ...) | async-done | bytes 3932176 | tf_op jit(solution)/shard_map/psum | solution.py:584
  754.6 2.2 convert_element_type.191
  756.9 1.8 convert_element_type.192
  (144 shorter events, 34.8 us)
Async XLA Ops:
  7.2 289.8 %copy-start = (bf16[384,1024]{1,0:T(8,128)(2,1)S(1)}, bf16[384,1024]{1,0:T(8,128)(2,1)}, u32[]{:S(2)}) copy-start(bf16[384,1024]{1,0:T(8,128)(2,1)} %param.26) | copy-start | bytes 2359300
  7.2 747.4 %all-reduce.7.cloned.1.call-start = ((), (), s32[]{:S(2)}) async-start(), calls=%async_computation | async-start | bytes 7864320 | tf_op jit(solution)/shard_map/psum | solution.py:584
  62.1 5.4 copy-start.22
  71.6 1.6 copy-start.4
  184.8 31.7 %copy-start.28 = (bf16[256,1024]{1,0:T(8,128)(2,1)S(1)}, bf16[256,1024]{1,0:T(8,128)(2,1)}, u32[]{:S(2)}) copy-start(bf16[256,1024]{1,0:T(8,128)(2,1)} %param.20) | copy-start | bytes 1572868
  257.4 2.1 copy-start.8
  259.5 79.9 %copy-start.6 = (f32[128,1024]{1,0:T(8,128)}, f32[128,1024]{1,0:T(8,128)S(1)}, u32[]{:S(2)}) copy-start(f32[128,1024]{1,0:T(8,128)S(1)} %convert_reduce_fusion.4) | copy-start | bytes 1572868
  292.9 4.1 copy-start.33
  297.0 2.5 copy-start.21
  299.5 3.0 copy-start.35
  337.0 2.9 copy-start.13
  396.8 3.3 copy-start.20
  396.8 3.3 copy-start.29
  400.1 1.6 copy-start.34
  400.1 1.8 copy-start.37
  403.8 2.6 copy-start.3
  540.4 2.0 copy-start.16
  540.4 2.0 copy-start.18
  542.3 1.4 copy-start.5
  546.4 2.9 copy-start.23
  549.2 2.6 copy-start.36
  598.1 40.5 %copy-start.9 = (bf16[1,128,1024]{2,1,0:T(8,128)(2,1)S(1)}, bf16[1,128,1024]{2,1,0:T(8,128)(2,1)}, u32[]{:S(2)}) copy-start(bf16[1,128,1024]{2,1,0:T(8,128)(2,1)} %param.14) | copy-start | bytes 786436
  598.1 40.7 %copy-start.19 = (bf16[1024,1024]{1,0:T(8,128)(2,1)S(1)}, bf16[1024,1024]{1,0:T(8,128)(2,1)}, u32[]{:S(2)}) copy-start(bf16[1024,1024]{1,0:T(8,128)(2,1)} %get-tuple-element.47) | copy-start | bytes 6291460
  638.6 1.6 copy-start.7
  638.6 1.6 copy-start.11
  638.6 1.6 copy-start.14
  754.6 4.0 copy-start.31
  754.6 4.9 copy-start.30
  754.6 6.0 copy-start.27
  759.5 2.4 copy-start.26
  760.6 2.6 copy-start.25
  761.9 2.6 copy-start.1
  (7 other events, 6.3 us)
Sparse Core Ops, SparseCore 0:
  598.2 156.3 all-reduce.6

commit v2 on v1

v2 whole, which is shorter than its diff:
```python
import jax
import jax.numpy as jnp
from jax import lax
from jax.experimental import pallas as pl
from jax.experimental.pallas import tpu as pltpu
from jax.sharding import PartitionSpec as P

HEAD = 128
EPS = 1e-06
THETA = 1000000.0
SCALE = HEAD ** (-0.5)
LOG2E = 1.4426950408889634
RUN = 128
CHUNK = 512
TAG = 16
X_ROWS = RUN + TAG
KV_ROWS = 8 * RUN + TAG
BF = jnp.bfloat16
F32 = jnp.float32
MESH = pl.DeviceIdType.MESH


class At:
    def __init__(self, x, y, c, d, z):
        self.x, self.y, self.c, self.d, self.z = x, y, c, d, z

    def but(self, **new):
        return At(**{**self.__dict__, **new})

    def chip(self):
        return self.x * 2 + self.y

    def head(self):
        return self.d * 4 + self.z

    def slot(self):
        return self.z * 2 + self.c

    def device(self):
        return ((self.x * 2 + self.y) * 2 + self.c, self.d, self.z)


def here():
    ctx = lax.axis_index("ctx")
    return At(ctx // 4, ctx // 2 % 2, ctx % 2, lax.axis_index("dp"), lax.axis_index("fsdp"))


class Shift:
    def __init__(self, x=0, y=0, c=0, d=0, z=0):
        self.by = (x, y, c, d, z)

    def move(self, at, sign):
        x, y, c, d, z = self.by
        return At(
            (at.x + 4 + sign * x) % 4 if x else at.x,
            1 - at.y if y else at.y,
            1 - at.c if c else at.c,
            1 - at.d if d else at.d,
            (at.z + 4 + sign * z) % 4 if z else at.z,
        )

    def to(self, at):
        return self.move(at, 1)

    def back(self, at):
        return self.move(at, -1)

    def key(self):
        return self.by


class Op:
    def __init__(self, shift, src, dst, cond=None, needs=()):
        self.shift, self.src, self.dst, self.cond, self.needs = shift, src, dst, cond, needs


def exchange(ops, collective_id, out_shapes, *arrays):
    n_in, n_out, n_ops = len(arrays), len(out_shapes), len(ops)

    def kernel(*refs):
        io = refs[: n_in + n_out]
        send_sem, recv_sem = refs[n_in + n_out :]
        me = here()

        def when(cond, act):
            if cond is None:
                act()
            else:
                pl.when(cond)(act)

        barrier = pltpu.get_barrier_semaphore()
        seen, count = set(), 0
        for op in ops:
            if op.shift is None or (op.shift.key(), op.cond) in seen:
                continue
            seen.add((op.shift.key(), op.cond))
            source = op.shift.back(me)

            def greet(source=source):
                pl.semaphore_signal(barrier, inc=1, device_id=source.device(), device_id_type=MESH)

            when(op.cond and op.cond(source), greet)
            count = count + (1 if op.cond is None else jnp.where(op.cond(me), 1, 0))
        pl.semaphore_wait(barrier, count)

        def copy(t, sender):
            op = ops[t]
            if op.shift is None:
                return pltpu.make_async_copy(op.src(io, me), op.dst(io, me), send_sem.at[t])
            return pltpu.make_async_remote_copy(
                src_ref=op.src(io, sender),
                dst_ref=op.dst(io, sender),
                send_sem=send_sem.at[t],
                recv_sem=recv_sem.at[t],
                device_id=op.shift.to(me).device(),
                device_id_type=MESH,
            )

        arrived = set()

        def arrive(t):
            if t in arrived:
                return
            arrived.add(t)
            op = ops[t]
            source = me if op.shift is None else op.shift.back(me)

            def wait():
                if op.shift is None:
                    copy(t, me).wait()
                else:
                    copy(t, source).wait_recv()

            when(op.cond and op.cond(source), wait)

        for t, op in enumerate(ops):
            for need in op.needs:
                arrive(need)
            when(op.cond and op.cond(me), lambda t=t: copy(t, me).start())
        for t, op in enumerate(ops):
            arrive(t)
            if op.shift is not None:
                when(op.cond and op.cond(me), lambda t=t: copy(t, me).wait_send())

    return pl.pallas_call(
        kernel,
        out_shape=tuple(jax.ShapeDtypeStruct(s, d) for s, d in out_shapes),
        in_specs=[pl.BlockSpec(memory_space=pl.ANY)] * n_in,
        out_specs=tuple([pl.BlockSpec(memory_space=pl.ANY)] * n_out),
        scratch_shapes=[
            pltpu.SemaphoreType.DMA((n_ops,)),
            pltpu.SemaphoreType.DMA((n_ops,)),
        ],
        compiler_params=pltpu.CompilerParams(collective_id=collective_id, has_side_effects=True),
        name="exchange_%d" % collective_id,
    )(*arrays)

def home(at):
    return at.c == at.d


def away(at):
    return at.c != at.d


def block(index, start, size):
    return lambda io, at: io[index].at[pl.ds(pl.multiple_of(start(at) * size, size), size)]


def full(index):
    return lambda io, at: io[index]


class Plan(list):
    def add(self, *args, **named):
        self.append(Op(*args, **named))
        return len(self) - 1

    def gather_tokens(self, src, dst, size):
        mine = block(dst, At.slot, size)
        self.add(None, full(src), mine, home)
        got = {}
        for name, by in (("side", {"d": 1}), ("up", {"z": 1}), ("down", {"z": -1})):
            got[name] = [
                self.add(Shift(**by), full(src), mine, home),
                self.add(Shift(c=1, **by), full(src), mine, away),
            ]
        self.add(Shift(c=1), full(src), mine, away)

        def relays():
            both = block(dst, lambda at: at.z, 2 * size)
            below = block(dst, lambda at: (at.z + 3) % 4 * 2, size)
            above = block(dst, lambda at: (at.z + 1) % 4 * 2 + 1, size)
            up = self.add(Shift(z=1), both, both, away, got["side"])
            down = self.add(Shift(z=-1), both, both, away, got["side"])
            self.add(Shift(z=1), below, below, home, got["up"])
            self.add(Shift(z=-1), above, above, home, got["down"])
            self.add(Shift(z=1), below, below, away, [up])
            self.add(Shift(z=-1), above, above, away, [down])

        return relays

    def return_tokens(self, src, dst, size):
        land = block(dst, At.head, size)
        for k in (0, 1, 3, 2):
            for c in (0, 1):
                for d, cond in ((0, home), (1, away)):
                    shift = Shift(z=k, c=c, d=d)
                    if not (k or c or d):
                        self.add(None, block(src, At.slot, size), land, cond)
                    else:
                        self.add(shift, block(src, lambda at, s=shift: s.to(at).slot(), size), land, cond)

    def group_shifts(self):
        return [Shift(d=d, z=z) for z in (1, 3, 0, 2) for d in (0, 1) if d or z]

    def chip_shifts(self):
        return [Shift(x=x, y=y) for x in (1, 3, 2, 0) for y in (0, 1) if x or y]

    def weights(self, src, dst, rows, width, start):
        half = rows // 2

        def cut(at, to):
            return lambda io: io[src].at[
                pl.ds(pl.multiple_of(at.c * half, half), half),
                pl.ds(pl.multiple_of(to.head() * width, width), width),
            ]

        def land(io, at):
            first = pl.multiple_of(at.head() * rows + at.c * half, half)
            return io[dst].at[pl.ds(first, half), pl.ds(start, width)]

        got = []
        for shift in self.group_shifts():
            got.append(
                (shift, self.add(shift, lambda io, at, s=shift: cut(at, s.to(at))(io), land))
            )
        self.add(
            None,
            lambda io, at: io[src].at[:, pl.ds(pl.multiple_of(at.head() * width, width), width)],
            lambda io, at: io[dst].at[pl.ds(pl.multiple_of(at.head() * rows, rows), rows), pl.ds(start, width)],
        )

        def relays():
            for shift, need in got:
                piece = lambda io, at, s=shift: land(io, s.back(at))
                self.add(Shift(c=1), piece, piece, needs=[need])

        return relays

    def gather_group(self, src, dst, size):
        for shift in self.group_shifts():
            self.add(shift, full(src), block(dst, At.head, size))
        self.add(None, full(src), block(dst, At.head, size))

    def gather_context(self, src, dst, size):
        land = block(dst, lambda at: at.chip() * 2 + at.c, size)
        for shift in self.chip_shifts():
            for c in (0, 1):
                self.add(Shift(shift.by[0], shift.by[1], c), full(src), land)
        self.add(Shift(c=1), full(src), land)
        self.add(None, full(src), land)

    def scatter_group(self, src, dst):
        ids = []
        for shift in self.group_shifts():
            ids.append(
                self.add(
                    shift,
                    lambda io, at, s=shift: src(io, s.to(at).head()),
                    lambda io, at: dst(io, at.head()),
                )
            )
        ids.append(
            self.add(None, lambda io, at: src(io, at.head()), lambda io, at: dst(io, at.head()))
        )
        return ids

    def scatter_chips(self, src, dst):
        for shift in self.chip_shifts():
            self.add(
                shift,
                lambda io, at, s=shift: src(io, s.to(at).chip()),
                lambda io, at: dst(io, at.chip()),
            )
        self.add(None, lambda io, at: src(io, at.chip()), lambda io, at: dst(io, at.chip()))

    def gather_chips(self, src, land, whole, needs=()):
        at_own = lambda io, at: land(io, at.chip(), at.c)
        ids = [self.add(None, src, at_own, needs=needs)]
        side = self.add(Shift(y=1), src, at_own, needs=needs)
        ids.append(side)
        for x in (1, 3, 2):
            ids.append(self.add(Shift(x=x), src, at_own, needs=needs))

        def relays():
            other = lambda io, at: land(io, at.but(y=1 - at.y).chip(), at.c)
            for x in (1, 3, 2):
                ids.append(self.add(Shift(x=x), other, other, needs=[side]))

        def share():
            mine = lambda io, at: whole(io, at.c)
            self.add(Shift(c=1), mine, mine, needs=list(ids))

        return relays, share


NT = (((1,), (1,)), ((), ()))
NN = (((1,), (0,)), ((), ()))


def mm(a, b, dims=NN):
    return lax.dot_general(a, b, dims, preferred_element_type=F32)


def stacked(ref):
    return jnp.concatenate([ref[:, :HEAD], ref[:, HEAD:]], axis=0)


def forward_kernel(order, own, q_ref, kv_ref, o_ref, l_ref, keys, vals, acc):
    step = pl.program_id(0)
    n_runs = order.shape[0]

    @pl.when(step == 0)
    def _():
        def place(r, _):
            src = pl.ds(pl.multiple_of(r // 8 * KV_ROWS + r % 8 * RUN, 16), RUN)
            dst = pl.ds(pl.multiple_of(order[r] * RUN, RUN), RUN)
            keys[dst, :] = kv_ref[src, :HEAD]
            vals[dst, :HEAD] = kv_ref[src, HEAD:]
            vals[dst, HEAD:] = jnp.ones((RUN, HEAD), BF)
            return 0

        lax.fori_loop(0, n_runs, place, 0)

    run = own[step]
    query = stacked(q_ref)
    acc[...] = jnp.zeros_like(acc)

    def visit(j, masked):
        at = pl.ds(pl.multiple_of(j * CHUNK, CHUNK), CHUNK)
        s = mm(query, keys[at, :], NT)
        p = jnp.exp2(s * (SCALE * LOG2E))
        if masked:
            row = lax.broadcasted_iota(jnp.int32, p.shape, 0) % RUN + run * RUN
            col = lax.broadcasted_iota(jnp.int32, p.shape, 1) + j * CHUNK
            p = jnp.where(col <= row, p, 0.0)
        acc[...] += mm(p.astype(BF), vals[at, :])

    last = run // (CHUNK // RUN)

    def plain(j, _):
        visit(j, False)
        return 0

    lax.fori_loop(0, last, plain, 0)
    visit(last, True)
    total = acc[:, HEAD:]
    out = acc[:, :HEAD] / total
    log = jnp.log2(total)
    o_ref[:, :HEAD] = out[:RUN]
    o_ref[:, HEAD:] = out[RUN:]
    l_ref[:, :HEAD] = log[:RUN]
    l_ref[:, HEAD:] = log[RUN:]


def attention_forward(order, own, q, kv):
    length = order.shape[0] * RUN
    tokens = q.shape[0]
    block = pl.BlockSpec((RUN, 2 * HEAD), lambda i, *_: (i, 0))
    return pl.pallas_call(
        forward_kernel,
        grid_spec=pltpu.PrefetchScalarGridSpec(
            num_scalar_prefetch=2,
            grid=(tokens // RUN,),
            in_specs=[block, pl.BlockSpec(kv.shape, lambda i, *_: (0, 0))],
            out_specs=[block, block],
            scratch_shapes=[
                pltpu.VMEM((length, HEAD), BF),
                pltpu.VMEM((length, 2 * HEAD), BF),
                pltpu.VMEM((2 * RUN, 2 * HEAD), F32),
            ],
        ),
        out_shape=(jax.ShapeDtypeStruct(q.shape, F32), jax.ShapeDtypeStruct(q.shape, F32)),
        compiler_params=pltpu.CompilerParams(
            dimension_semantics=("arbitrary",), vmem_limit_bytes=48 * 2**20
        ),
        name="attention_forward",
    )(order, own, q, kv)


def backward_kernel(
    order, own, q_ref, g_ref, o_ref, l_ref, kv_ref, dq_ref, dkv_ref,
    keys, keys_t, vals, dk, dv, dq_t, q_t, g_t,
):
    step = pl.program_id(0)
    n_runs = order.shape[0]

    @pl.when(step == 0)
    def _():
        dk[...] = jnp.zeros_like(dk)
        dv[...] = jnp.zeros_like(dv)

        def place(r, _):
            src = pl.ds(pl.multiple_of(r // 8 * KV_ROWS + r % 8 * RUN, 16), RUN)
            dst = pl.ds(pl.multiple_of(order[r] * RUN, RUN), RUN)
            k = kv_ref[src, :HEAD]
            keys[dst, :] = k
            keys_t[:, dst] = k.T
            vals[dst, :] = kv_ref[src, HEAD:]
            return 0

        lax.fori_loop(0, n_runs, place, 0)

    run = own[step]
    query = stacked(q_ref)
    grad = stacked(g_ref)
    q_t[...] = query.T
    g_t[...] = grad.T
    delta = jnp.sum((grad.astype(F32) * stacked(o_ref)).T, axis=0, keepdims=True)
    log = stacked(l_ref).T[:1]
    dq_t[...] = jnp.zeros_like(dq_t)

    def visit(j, masked):
        at = pl.ds(pl.multiple_of(j * CHUNK, CHUNK), CHUNK)
        s = mm(keys[at, :], q_t[...])
        p = jnp.exp2(s * (SCALE * LOG2E) - log)
        if masked:
            row = lax.broadcasted_iota(jnp.int32, p.shape, 1) % RUN + run * RUN
            col = lax.broadcasted_iota(jnp.int32, p.shape, 0) + j * CHUNK
            p = jnp.where(col <= row, p, 0.0)
        dp = mm(vals[at, :], g_t[...])
        ds = (p * (dp - delta)).astype(BF)
        dv[at, :] += mm(p.astype(BF), grad)
        dk[at, :] += mm(ds, query)
        dq_t[...] += mm(keys_t[:, at], ds)

    last = run // (CHUNK // RUN)

    def plain(j, _):
        visit(j, False)
        return 0

    lax.fori_loop(0, last, plain, 0)
    visit(last, True)
    out = dq_t[...].T * SCALE
    dq_ref[:, :HEAD] = out[:RUN]
    dq_ref[:, HEAD:] = out[RUN:]

    @pl.when(step == pl.num_programs(0) - 1)
    def _():
        def give(r, _):
            dst = pl.ds(pl.multiple_of(r * RUN, RUN), RUN)
            src = pl.ds(pl.multiple_of(order[r] * RUN, RUN), RUN)
            dkv_ref[dst, :HEAD] = (dk[src, :] * SCALE).astype(BF)
            dkv_ref[dst, HEAD:] = dv[src, :].astype(BF)
            return 0

        lax.fori_loop(0, n_runs, give, 0)


def attention_backward(order, own, q, g, o, log, kv):
    length = order.shape[0] * RUN
    tokens = q.shape[0]
    block = pl.BlockSpec((RUN, 2 * HEAD), lambda i, *_: (i, 0))
    all_rows = pl.BlockSpec((length, 2 * HEAD), lambda i, *_: (0, 0))
    return pl.pallas_call(
        backward_kernel,
        grid_spec=pltpu.PrefetchScalarGridSpec(
            num_scalar_prefetch=2,
            grid=(tokens // RUN,),
            in_specs=[block, block, block, block, pl.BlockSpec(kv.shape, lambda i, *_: (0, 0))],
            out_specs=[block, all_rows],
            scratch_shapes=[
                pltpu.VMEM((length, HEAD), BF),
                pltpu.VMEM((HEAD, length), BF),
                pltpu.VMEM((length, HEAD), BF),
                pltpu.VMEM((length, HEAD), F32),
                pltpu.VMEM((length, HEAD), F32),
                pltpu.VMEM((HEAD, 2 * RUN), F32),
                pltpu.VMEM((HEAD, 2 * RUN), BF),
                pltpu.VMEM((HEAD, 2 * RUN), BF),
            ],
        ),
        out_shape=(jax.ShapeDtypeStruct(q.shape, F32), jax.ShapeDtypeStruct((length, 2 * HEAD), BF)),
        compiler_params=pltpu.CompilerParams(
            dimension_semantics=("arbitrary",), vmem_limit_bytes=48 * 2**20
        ),
        name="attention_backward",
    )(order, own, q, g, o, log, kv)


def rotate(value, cos, sin):
    a, b = value[..., : HEAD // 2], value[..., HEAD // 2 :]
    return jnp.concatenate([a * cos - b * sin, b * cos + a * sin], axis=-1)


def rotate_back(grad, cos, sin):
    a, b = grad[..., : HEAD // 2], grad[..., HEAD // 2 :]
    return jnp.concatenate([a * cos + b * sin, b * cos - a * sin], axis=-1)


def inverse_rms(value):
    return lax.rsqrt(jnp.mean(value * value, axis=-1, keepdims=True) + EPS)


def norm_back(value, inverse, gain, grad):
    scaled = grad * gain
    inner = jnp.sum(scaled * value, axis=-1, keepdims=True)
    return inverse * scaled - value * inverse * inverse * inverse * inner / value.shape[-1]


def dot(a, b):
    return jnp.dot(a, b, preferred_element_type=F32)


def dot_t(a, b):
    return lax.dot_general(a, b, (((0,), (0,)), ((), ())), preferred_element_type=F32)


def summed(parts, count):
    return jnp.sum(parts.reshape((count, -1) + parts.shape[1:]).astype(F32), axis=0)


def row_of(vector):
    return jnp.pad(vector.reshape(1, -1), ((0, 0), (0, 128 - vector.shape[-1])))


def local(
    hidden_in, positions, attn_gain, query_weight, key_matrix, value_matrix, output_weight,
    query_norm_gain, key_gain, mlp_gain, gate_weight, up_weight, down_weight, cotangent,
):
    hidden = hidden_in[0]
    cot = cotangent[0]
    tokens, width = hidden.shape
    group = 8 * tokens
    ff = gate_weight.shape[1] // 8
    part = width // 8
    core = lax.axis_index("ctx") % 2
    def rows(size):
        return lambda ref: (lambda io, n: io[ref].at[pl.ds(pl.multiple_of(n * size, size), size)])

    gain_tile = jnp.concatenate(
        [row_of(g.astype(F32)) for g in (attn_gain, mlp_gain, query_norm_gain, key_gain)]
        + [jnp.zeros((4, 128), F32)],
        axis=0,
    )
    own_run = (positions[:, :1] // RUN).astype(BF)
    tagged = jnp.concatenate([hidden, jnp.broadcast_to(own_run, (TAG, width))], axis=0)
    plan = Plan()
    relays = [plan.gather_tokens(0, 5, X_ROWS)]
    plan.gather_group(1, 6, 8)
    relays += [
        plan.weights(2, 7, part, 256, 0),
        plan.weights(3, 7, part, 128, 256),
        plan.weights(4, 7, part, 128, 384),
    ]
    for relay in relays:
        relay()
    x_all, gains, w_qkv = exchange(
        plan, 1, (((8 * X_ROWS, width), BF), ((64, 128), F32), ((width, 512), BF)),
        tagged, gain_tile, query_weight, key_matrix, value_matrix,
    )
    gains = gains.reshape(8, 8, 128)
    attn_scale = gains[:, 0].reshape(1, width)
    mlp_scale = gains[:, 1].reshape(1, width)
    query_scale = gains[:, 2, :16].reshape(1, HEAD)
    key_scale = gains[:, 3, :16].reshape(1, HEAD)
    x_all = x_all.reshape(8, X_ROWS, width)
    own_bf = x_all[:, RUN, 0]
    own = own_bf.astype(jnp.int32)
    x_wide = x_all[:, :RUN].reshape(group, width).astype(F32)
    attn_inverse_all = inverse_rms(x_wide)
    norm_one = (x_wide * attn_inverse_all * attn_scale).astype(BF)
    qkv = dot(norm_one, w_qkv)
    pre = qkv[:, :384].reshape(group, 3, HEAD)
    head_scale = jnp.stack([query_scale, query_scale, key_scale], axis=1)
    head_inverse = inverse_rms(pre)
    place_rows = (own[:, None] * RUN + jnp.arange(RUN, dtype=jnp.int32)[None, :]).reshape(group)
    frequency = 1.0 / THETA ** (jnp.arange(0, HEAD, 2, dtype=F32) / HEAD)
    angle = place_rows.astype(F32)[:, None] * frequency[None, :]
    cos, sin = jnp.cos(angle)[:, None, :], jnp.sin(angle)[:, None, :]
    turned = rotate(pre * head_inverse * head_scale, cos, sin).astype(BF).reshape(group, 384)
    queries = turned[:, :256]
    kv = jnp.concatenate([turned[:, 256:], qkv[:, 384:].astype(BF)], axis=1)
    tag = jnp.pad(jnp.broadcast_to(own_bf[None, :], (TAG, 8)), ((0, 0), (0, 2 * HEAD - 8)))
    kv = jnp.concatenate([kv, tag], axis=0)

    plan = Plan()
    own_kv = block(4, At.chip, KV_ROWS)
    side_kv = block(4, lambda at: at.but(y=1 - at.y).chip(), KV_ROWS)
    half = group // 2

    def upper(io, at):
        return io[4].at[pl.ds(pl.multiple_of(at.chip() * KV_ROWS, 16), half)]

    def lower(io, at):
        return io[4].at[pl.ds(pl.multiple_of(at.chip() * KV_ROWS + half, 16), KV_ROWS - half)]

    def left(of, flip):
        return lambda io, at: of(io, at.but(x=(at.x + 3) % 4, y=1 - at.y if flip else at.y))

    def right(of, flip):
        return lambda io, at: of(io, at.but(x=(at.x + 1) % 4, y=1 - at.y if flip else at.y))

    side = plan.add(Shift(y=1), full(0), own_kv)
    right_id = plan.add(Shift(x=1), full(0), own_kv)
    left_id = plan.add(Shift(x=-1), full(0), own_kv)
    plan.add(None, full(0), own_kv)
    relays = [
        plan.gather_tokens(1, 5, tokens),
        plan.weights(2, 6, part, ff, 0),
        plan.weights(3, 6, part, ff, ff),
    ]
    side_right = plan.add(Shift(x=1), side_kv, side_kv, needs=[side])
    side_left = plan.add(Shift(x=-1), side_kv, side_kv, needs=[side])
    plan.add(Shift(x=1), left(upper, 0), left(upper, 0), needs=[right_id])
    plan.add(Shift(x=-1), right(lower, 0), right(lower, 0), needs=[left_id])
    for relay in relays:
        relay()
    plan.add(Shift(x=1), left(upper, 1), left(upper, 1), needs=[side_right])
    plan.add(Shift(x=-1), right(lower, 1), right(lower, 1), needs=[side_left])
    kv_all, cot_all, w_gu = exchange(
        plan, 2, (((8 * KV_ROWS, 256), BF), ((group, width), BF), ((width, 2 * ff), BF)),
        kv, cot, gate_weight, up_weight,
    )
    order = kv_all.reshape(8, KV_ROWS, 256)[:, 8 * RUN, :8].reshape(64).astype(jnp.int32)
    attention, log_total = attention_forward(order, own, queries, kv_all)
    mixed = attention.astype(BF)
    branch_part = dot(mixed, output_weight).astype(BF)

    plan = Plan()
    plan.return_tokens(0, 1, tokens)
    (branch,) = exchange(plan, 3, (((group, width), BF),), branch_part)
    residual = hidden.astype(F32)
    middle = residual + summed(branch, 8)
    mlp_inverse = inverse_rms(middle)
    norm_two_own = (middle * mlp_inverse * mlp_scale).astype(BF)
    plan = Plan()
    plan.gather_tokens(0, 1, tokens)()
    (norm_two,) = exchange(plan, 4, (((group, width), BF),), norm_two_own)

    gate_up = dot(norm_two, w_gu)
    gate, up = gate_up[:, :ff], gate_up[:, ff:]
    sigma = jax.nn.sigmoid(gate)
    swish = gate * sigma
    inner = (swish * up).astype(BF)
    inner_grad = lax.dot_general(cot_all, down_weight, NT, preferred_element_type=F32)
    gate_up_grad = jnp.concatenate(
        [
            (inner_grad * up * sigma * (1.0 + gate * (1.0 - sigma))).astype(BF),
            (inner_grad * swish).astype(BF),
        ],
        axis=1,
    )
    norm_two_part = lax.dot_general(gate_up_grad, w_gu, NT, preferred_element_type=F32).astype(BF)
    gate_up_wgrad = dot_t(norm_two, gate_up_grad).astype(BF).reshape(8, part, 2 * ff)
    down_wgrad = dot_t(inner, cot_all).astype(BF)

    def theirs(ref, size):
        def pick(io, at):
            cut = pl.ds(pl.multiple_of((1 - at.c) * size, size), size)
            return io[ref].at[..., cut]

        return pick

    def my_half(both, got):
        size = got.shape[-1]
        mine = lax.dynamic_slice_in_dim(both, core * size, size, axis=both.ndim - 1)
        return (mine.astype(F32) + got.astype(F32)).astype(BF)

    plan = Plan()
    plan.return_tokens(0, 3, tokens)
    plan.add(Shift(c=1), theirs(1, ff), full(4))
    plan.add(Shift(c=1), theirs(2, width // 2), full(5))
    norm_two_parts, gate_up_got, down_got = exchange(
        plan, 5, (((group, width), BF), ((8, part, ff), BF), ((ff, width // 2), BF)),
        norm_two_part, gate_up_wgrad, down_wgrad,
    )
    norm_two_grad = summed(norm_two_parts, 8)
    middle_grad = cot.astype(F32) + norm_back(middle, mlp_inverse, mlp_scale, norm_two_grad)
    mlp_gain_part = jnp.sum(norm_two_grad * middle * mlp_inverse, axis=0)
    branch_grad_own = middle_grad.astype(BF)
    gate_up_half = my_half(gate_up_wgrad, gate_up_got)
    down_half = my_half(down_wgrad, down_got)

    plan = Plan()
    relay = plan.gather_tokens(0, 3, tokens)
    plan.scatter_chips(
        lambda io, n: io[1].at[:, pl.ds(pl.multiple_of(n * 16, 16), 16)], lambda io, n: io[4].at[n]
    )
    plan.scatter_chips(rows(ff // 8)(2), lambda io, n: io[5].at[n])
    relay()
    branch_grad, gate_up_pieces, down_pieces = exchange(
        plan, 6, (((group, width), BF), ((8, 8, 16, ff), BF), ((8, ff // 8, width // 2), BF)),
        branch_grad_own, gate_up_half, down_half,
    )
    mixed_grad = lax.dot_general(branch_grad, output_weight, NT, preferred_element_type=F32).astype(BF)
    output_wgrad = dot_t(mixed, branch_grad).astype(BF)
    down_part = dot(inner, down_weight).astype(BF)
    gate_up_sum = jnp.sum(gate_up_pieces.astype(F32), axis=0).astype(BF)
    down_sum = jnp.sum(down_pieces.astype(F32), axis=0).astype(BF)
    query_turn, kv_part = attention_backward(
        order, own, queries, mixed_grad, attention, log_total, kv_all
    )

    plan = Plan()
    plan.scatter_chips(rows(group)(0), rows(group)(4))
    pair = 2 * tokens
    for k in (1, 3, 2):
        plan.add(
            Shift(z=k),
            block(1, lambda at, k=k: (at.z + k) % 4, pair),
            block(5, lambda at: at.z, pair),
        )
    plan.add(None, block(1, lambda at: at.z, pair), block(5, lambda at: at.z, pair))
    plan.add(Shift(c=1), theirs(2, width // 2), full(6))
    plan.scatter_group(
        lambda io, n: io[3].at[n],
        lambda io, n: io[7].at[:, pl.ds(pl.multiple_of(n * ff, ff), ff)],
    )
    n_rows = output_wgrad.shape[0]
    kv_parts, down_parts, output_got, gate_up_own = exchange(
        plan, 7,
        (
            ((8 * group, 256), BF), ((group, width), BF), ((n_rows, width // 2), BF),
            ((16, 8 * ff), BF),
        ),
        kv_part, down_part, output_wgrad, gate_up_sum,
    )
    down_pair = summed(down_parts, 4).astype(BF)
    output_half = my_half(output_wgrad, output_got)
    kv_sum = summed(kv_parts, 8)
    turn = jnp.concatenate([query_turn, kv_sum[:, :HEAD]], axis=1).reshape(group, 3, HEAD)
    head_grad = rotate_back(turn, cos, sin)
    pre_grad = norm_back(pre, head_inverse, head_scale, head_grad)
    head_gain_parts = jnp.sum(head_grad * pre * head_inverse, axis=0)
    qkv_grad = jnp.concatenate(
        [pre_grad.reshape(group, 384).astype(BF), kv_sum[:, HEAD:].astype(BF)], axis=1
    )
    qkv_wgrad = dot_t(norm_one, qkv_grad).astype(BF).reshape(8, part, 512)
    norm_one_wide = lax.dot_general(qkv_grad, w_qkv, NT, preferred_element_type=F32)
    attn_gain_part = jnp.sum(norm_one_wide * x_wide * attn_inverse_all, axis=0)
    query_gain_part = (head_gain_parts[0] + head_gain_parts[1]).reshape(8, 1, 16)
    key_gain_part = head_gain_parts[2].reshape(8, 1, 16)
    gain_parts = jnp.concatenate(
        [
            attn_gain_part.reshape(8, 1, 128),
            mlp_gain_part.reshape(8, 1, 128),
            jnp.pad(query_gain_part, ((0, 0), (0, 0), (0, 112))),
            jnp.pad(key_gain_part, ((0, 0), (0, 0), (0, 112))),
            jnp.zeros((8, 4, 128), F32),
        ],
        axis=1,
    ).reshape(64, 128)

    plan = Plan()
    plan.return_tokens(0, 6, tokens)

    def wgrad_piece(io, chip, c):
        return io[1].at[
            :, pl.ds(pl.multiple_of(chip * 16, 16), 16), pl.ds(pl.multiple_of(c * 256, 256), 256)
        ]

    for shift in [Shift(c=1)] + [
        Shift(s.by[0], s.by[1], c) for s in plan.chip_shifts() for c in (0, 1)
    ]:
        plan.add(
            shift,
            lambda io, at, s=shift: wgrad_piece(io, s.to(at).chip(), s.to(at).c),
            lambda io, at: io[7].at[at.chip() * 2 + at.c],
        )
    plan.add(
        None,
        lambda io, at: wgrad_piece(io, at.chip(), at.c),
        lambda io, at: io[7].at[at.chip() * 2 + at.c],
    )
    plan.scatter_chips(rows(n_rows // 8)(2), lambda io, n: io[8].at[n])
    plan.scatter_group(rows(8)(3), rows(8)(9))

    def stacked_rows(ref, size, total):
        def land(io, chip, c):
            return io[ref].at[pl.ds(pl.multiple_of(c * total + chip * size, size), size)]

        return land, lambda io, c: io[ref].at[pl.ds(pl.multiple_of(c * total, total), total)]

    def side_columns(ref, size):
        def at_core(c):
            return pl.ds(pl.multiple_of(c * (width // 2), width // 2), width // 2)

        def land(io, chip, c):
            return io[ref].at[pl.ds(pl.multiple_of(chip * size, size), size), at_core(c)]

        return land, lambda io, c: io[ref].at[:, at_core(c)]

    later = [
        plan.gather_chips(full(4), *stacked_rows(10, 16, part)),
        plan.gather_chips(full(5), *side_columns(11, ff // 8)),
    ]
    for relay, _ in later:
        relay()
    for _, share in later:
        share()
    norm_one_parts, qkv_pieces, output_pieces, gain_sums, gate_up_final, down_final = exchange(
        plan, 8,
        (
            ((group, width), BF), ((16, 8, 16, 256), BF), ((8, n_rows // 8, width // 2), BF),
            ((64, 128), F32), ((2 * part, 8 * ff), BF), ((ff, width), BF),
        ),
        norm_one_wide.astype(BF), qkv_wgrad, output_half, gain_parts, gate_up_own, down_sum,
    )
    qkv_sum = jnp.sum(qkv_pieces.astype(F32), axis=0).astype(BF)
    output_sum = jnp.sum(output_pieces.astype(F32), axis=0).astype(BF)
    gain_sum = summed(gain_sums, 8)

    plan = Plan()
    to_group = plan.scatter_group(
        lambda io, n: io[0].at[n],
        lambda io, n: io[4].at[:, pl.ds(pl.multiple_of(n * 256, 256), 256)],
    )
    relay_output, share_output = plan.gather_chips(full(1), *side_columns(6, n_rows // 8))
    plan.gather_context(2, 7, 8)
    own_block = block(3, lambda at: at.c, tokens)
    other_block = block(3, lambda at: 1 - at.c, tokens)

    def landed(n):
        return lambda io, at: io[8].at[pl.ds(n * tokens, tokens)]

    plan.add(Shift(d=1), own_block, landed(1), away)
    plan.add(Shift(d=1, c=1), other_block, landed(1), away)
    plan.add(None, own_block, landed(0), home)
    plan.add(Shift(c=1), other_block, landed(0), home)
    relay_qkv, share_qkv = plan.gather_chips(full(4), *stacked_rows(5, 16, part), needs=to_group)
    relay_output()
    relay_qkv()
    share_output()
    share_qkv()
    _, qkv_final, output_final, gain_all, down_last = exchange(
        plan, 9,
        (
            ((16, 2048), BF), ((2 * part, 2048), BF), ((n_rows, width), BF), ((128, 128), F32),
            ((2 * tokens, width), BF),
        ),
        qkv_sum, output_sum, gain_sum, down_pair,
    )
    layer_out = (middle + summed(down_last, 2)).astype(BF)
    attn_inverse = inverse_rms(residual)
    input_grad = middle_grad + norm_back(residual, attn_inverse, attn_scale, summed(norm_one_parts, 8))
    gain_total = summed(gain_all, 16)
    key_value = qkv_final[part:].astype(F32).reshape(part, 8, 2, HEAD)
    return (
        layer_out[None],
        input_grad[None],
        gain_total[0],
        qkv_final[:part].astype(F32),
        key_value[:, :, 0].reshape(part, width),
        key_value[:, :, 1].reshape(part, width),
        output_final.astype(F32),
        gain_total[2, :16],
        gain_total[3, :16],
        gain_total[1],
        gate_up_final[:part].astype(F32),
        gate_up_final[part:].astype(F32),
        down_final.astype(F32),
    )


def solution(mesh):
    tokens = P("dp", ("ctx", "fsdp"), None)
    places = P("dp", ("ctx", "fsdp"))
    vector = P(("dp", "fsdp"))
    matrix = P(("dp", "fsdp"), None)
    in_specs = (
        tokens, places, vector, matrix, matrix, matrix, matrix,
        vector, vector, vector, matrix, matrix, matrix, tokens,
    )
    out_specs = (
        tokens, tokens, vector, matrix, matrix, matrix, matrix,
        vector, vector, vector, matrix, matrix, matrix,
    )
    return jax.shard_map(local, mesh=mesh, in_specs=in_specs, out_specs=out_specs, check_vma=False)
```

time: 769 us -> 547 us (0.71); the launches traced: 771 us -> 537 us
  waiting for transfers between devices: 113 us -> 0 us
  Pallas kernels: 520 us -> 427 us
  blocking collectives: 37.7 us -> 0 us
  other arithmetic: 35.9 us -> 46.3 us
  between operations: 14.6 us -> 4.4 us
  local copies, waits for them, and re-layouts: 18 us -> 26.3 us
    psum x1 -> x0, waiting for transfers between devices: 113 us -> none  [local(): lax.psum((query_wgrad, key_wgrad, value_wgrad, gain_sum.astype(BF)), 'ctx')]
    pallas_call x8 -> x9, Pallas kernels: 445 us -> 351 us  [exchange(): pl.pallas_call(kernel, out_shape=tuple((jax.ShapeDtypeStruct(s, d) for s,...]
    psum x1 -> x0, blocking collectives: 37.7 us -> none  [local(): lax.psum((query_wgrad, key_wgrad, value_wgrad, gain_sum.astype(BF)), 'ctx')]
  transfers between devices with their start and end apart: 1 -> 0, of which waited for: 1 -> 0; matrix products, arithmetic and copies ran while one was open for 1% -> 0% of each run, Pallas kernels for 0% -> 0%
where the time goes in v2:
time: 547 us; the launch traced here: 537 us
  Pallas kernels  427 us (78%)
  other arithmetic  46.3 us (8%)
  matrix products  33.7 us (6%)
  local copies, waits for them, and re-layouts  26.3 us (5%)
    pallas_call x9, Pallas kernels, exchange(): pl.pallas_call(kernel, out_shape=tuple((jax.ShapeDtypeStruct(s, d) for s,...  351 us
    pallas_call x1, Pallas kernels, attention_backward(): pl.pallas_call(backward_kernel, grid_spec=pltpu.PrefetchScalarGridSpec(nu...  44.9 us
    pallas_call x1, Pallas kernels, attention_forward(): pl.pallas_call(forward_kernel, grid_spec=pltpu.PrefetchScalarGridSpec(num...  31.2 us
    dot_general x4, matrix products, dot_t(): lax.dot_general(a, b, (((0,), (0,)), ((), ())), preferred_element_type=F32)  12.2 us
    dot_general x4, matrix products, dot(): return jnp.dot(a, b, preferred_element_type=F32)  11.2 us

profile of v2, /device:TPU:1, one launch (start us, length us, event | category | flops | bytes accessed | tf_op | source)
XLA Modules:
  0.0 537.4 jit_solution(3353513544221191253)
XLA Ops:
  7.0 35.8 %exchange_1.1 = (bf16[1152,1024]{1,0:T(8,128)(2,1)}, f32[64,128]{1,0:T(8,128)}, bf16[1024,512]{1,0:T(8,128)(2,1)}) custom-call(bf16[144,1024]{1,0:T(8,128)(2,1)} %concatenate.33.refs_0_, f32[8,128]{1,0:T(8,128)} %concatenate.34.refs_1_, bf16[128,2048]{1,0:T(8,128)(2,1)} %refs_2_.2, bf16[128,1024]{1,0:T(8,128)(2,1)} %refs_3_.2, bf16[128,1024]{1,0:T(8,128)(2,1)} %refs_4_.1), custom_call_target="tpu_custom_call" | custom-call | tf_op jit(solution)/shard_map/exchange_1/pallas_call | solution.py:145
  43.7 2.1 fusion.1
  45.8 2.2 fusion.3
  59.4 43.1 %exchange_2.1 = (bf16[8320,256]{1,0:T(8,128)(2,1)}, bf16[1024,1024]{1,0:T(8,128)(2,1)}, bf16[1024,768]{1,0:T(8,128)(2,1)}) custom-call(bf16[1040,256]{1,0:T(8,128)(2,1)} %pad_maximum_fusion.9.refs_0_, bf16[128,1024]{1,0:T(8,128)(2,1)} %bitcast.194, bf16[128,3072]{1,0:T(8,128)(2,1)} %refs_2_.3, bf16[128,3072]{1,0:T(8,128)(2,1)} %refs_3_.3), custom_call_target="tpu_custom_call" | custom-call | tf_op jit(solution)/shard_map/exchange_2/pallas_call | solution.py:145
  103.7 31.2 %attention_forward.1 = (f32[1024,256]{1,0:T(8,128)S(1)}, f32[1024,256]{1,0:T(8,128)S(1)}) custom-call(s32[64]{0:T(128)S(1)} %reshape.481.order, s32[8]{0:T(128)S(1)} %bitcast_convert_fusion.2.own, bf16[1024,256]{1,0:T(8,128)(2,1)S(1)} %copy.55.q_ref, bf16[8320,256]{1,0:T(8,128)(2,1)} %get-tuple-element.46.kv_ref), custom_call_target="tpu_custom_call" | custom-call | tf_op jit(solution)/shard_map/attention_forward/pallas_call | solution.py:371
  135.8 2.1 convolution_convert_fusion.1.refs_0_
  137.9 35.3 %exchange_3.1 = bf16[1024,1024]{1,0:T(8,128)(2,1)} custom-call(bf16[1024,1024]{1,0:T(8,128)(2,1)} %convolution_convert_fusion.1.refs_0_), custom_call_target="tpu_custom_call" | custom-call | tf_op jit(solution)/shard_map/exchange_3/pallas_call | solution.py:145
  173.2 2.1 convert_reduce_fusion.3
  176.3 25.6 %exchange_4.1 = bf16[1024,1024]{1,0:T(8,128)(2,1)} custom-call(bf16[128,1024]{1,0:T(8,128)(2,1)} %multiply_convert_fusion.3.refs_0_), custom_call_target="tpu_custom_call" | custom-call | tf_op jit(solution)/shard_map/exchange_4/pallas_call | solution.py:145
  201.9 4.1 fusion.41
  207.6 1.9 convolution_convert_fusion.5.refs_2_
  209.5 3.0 convolution_convert_fusion.3
  212.5 3.2 convolution_convert_fusion.2.refs_0_
  215.7 29.2 %exchange_5.1 = (bf16[1024,1024]{1,0:T(8,128)(2,1)}, bf16[8,128,384]{2,1,0:T(8,128)(2,1)}, bf16[384,512]{1,0:T(8,128)(2,1)}) custom-call(bf16[1024,1024]{1,0:T(8,128)(2,1)} %convolution_convert_fusion.2.refs_0_, bf16[8,128,768]{2,1,0:T(8,128)(2,1)} %bitcast.190, bf16[384,1024]{1,0:T(8,128)(2,1)} %convolution_convert_fusion.5.refs_2_), custom_call_target="tpu_custom_call" | custom-call | tf_op jit(solution)/shard_map/exchange_5/pallas_call | solution.py:145
  244.8 2.0 add_convert_fusion.1.refs_2_
  246.8 2.6 add_convert_fusion.refs_1_
  251.5 33.9 %exchange_6.1 = (bf16[1024,1024]{1,0:T(8,128)(2,1)}, bf16[8,8,16,384]{3,2,1,0:T(8,128)(2,1)}, bf16[8,48,512]{2,1,0:T(8,128)(2,1)}) custom-call(bf16[128,1024]{1,0:T(8,128)(2,1)} %add_convert_fusion.4.refs_0_, bf16[8,128,384]{2,1,0:T(8,128)(2,1)} %add_convert_fusion.refs_1_, bf16[384,512]{1,0:T(8,128)(2,1)} %add_convert_fusion.1.refs_2_), custom_call_target="tpu_custom_call" | custom-call | tf_op jit(solution)/shard_map/exchange_6/pallas_call | solution.py:145
  285.5 3.3 convolution_convert_fusion.6.refs_2_
  290.0 44.9 %attention_backward.1 = (f32[1024,256]{1,0:T(8,128)S(1)}, bf16[8192,256]{1,0:T(8,128)(2,1)}) custom-call(s32[64]{0:T(128)S(1)} %reshape.481.order, s32[8]{0:T(128)S(1)} %bitcast_convert_fusion.2.own, bf16[1024,256]{1,0:T(8,128)(2,1)S(1)} %copy.55.q_ref, bf16[1024,256]{1,0:T(8,128)(2,1)S(1)} %convolution_convert_fusion.7.g_ref, ...), custom_call_target="tpu_custom_call" | custom-call | tf_op jit(solution)/shard_map/attention_backward/pallas_call | solution.py:467
  334.8 1.9 reduce_sum.228.refs_3_
  336.7 3.8 convolution_convert_fusion.refs_1_
  340.5 64.8 %exchange_7.1 = (bf16[8192,256]{1,0:T(8,128)(2,1)}, bf16[1024,1024]{1,0:T(8,128)(2,1)}, bf16[256,512]{1,0:T(8,128)(2,1)}, bf16[16,3072]{1,0:T(8,128)(2,1)}) custom-call(bf16[8192,256]{1,0:T(8,128)(2,1)} %get-tuple-element.56.refs_0_, bf16[1024,1024]{1,0:T(8,128)(2,1)} %convolution_convert_fusion.refs_1_, ...), custom_call_target="tpu_custom_call" | custom-call | tf_op jit(solution)/shard_map/exchange_7/pallas_call | solution.py:145
  405.3 2.9 convert_reduce_fusion
  410.4 1.9 copy.46
  419.4 4.7 fusion.5
  426.8 4.1 convolution_convert_fusion.4
  431.6 56.7 %exchange_8.1 = (bf16[1024,1024]{1,0:T(8,128)(2,1)}, bf16[16,8,16,256]{3,2,1,0:T(8,128)(2,1)}, bf16[8,32,512]{2,1,0:T(8,128)(2,1)}, f32[64,128]{1,0:T(8,128)}, b...) custom-call(bf16[1024,1024]{1,0:T(8,128)(2,1)} %get-tuple-element.81.refs_0_, bf16[8,128,512]{2,1,0:T(8,128)(2,1)} %bitcast.200, ...), custom_call_target="tpu_custom_call" | custom-call | tf_op jit(solution)/shard_map/exchange_8/pallas_call | solution.py:145
  488.3 2.0 reduce_sum.235.refs_0_
  494.6 26.2 %exchange_9.1 = (bf16[16,2048]{1,0:T(8,128)(2,1)}, bf16[256,2048]{1,0:T(8,128)(2,1)}, bf16[256,1024]{1,0:T(8,128)(2,1)}, f32[128,128]{1,0:T(8,128)}, bf16[256,1024]{1,0:T(8,128)(2,1)}) custom-call(bf16[8,16,256]{2,1,0:T(8,128)(2,1)} %reduce_sum.235.refs_0_, bf16[32,512]{1,0:T(8,128)(2,1)} %reduce_sum.236.refs_1_, f32[8,128]{1,0:T(8,128)} %bitcast_reduce_fusion.1.refs_2_, ...), custom_call_target="tpu_custom_call" | custom-call | tf_op jit(solution)/shard_map/exchange_9/pallas_call | solution.py:145
  520.8 2.4 slice_convert_fusion.3
  524.1 2.7 slice_reduce_fusion
  533.6 2.0 slice_convert_fusion
  (158 shorter events, 49.5 us)
Async XLA Ops:
  0.6 205.3 %copy-start = (bf16[384,1024]{1,0:T(8,128)(2,1)S(1)}, bf16[384,1024]{1,0:T(8,128)(2,1)}, u32[]{:S(2)}) copy-start(bf16[384,1024]{1,0:T(8,128)(2,1)} %param.26) | copy-start | bytes 2359300
  45.8 2.3 copy-start.38
  48.0 1.3 copy-start.25
  49.3 1.4 copy-start.12
  49.5 3.8 copy-start.3
  55.2 1.9 copy-start.17
  55.2 1.9 copy-start.19
  103.6 32.2 %copy-start.29 = (bf16[256,1024]{1,0:T(8,128)(2,1)S(1)}, bf16[256,1024]{1,0:T(8,128)(2,1)}, u32[]{:S(2)}) copy-start(bf16[256,1024]{1,0:T(8,128)(2,1)} %param.20) | copy-start | bytes 1572868
  173.2 2.1 copy-start.7
  175.3 74.8 %copy-start.5 = (f32[128,1024]{1,0:T(8,128)}, f32[128,1024]{1,0:T(8,128)S(1)}, u32[]{:S(2)}) copy-start(f32[128,1024]{1,0:T(8,128)S(1)} %convert_reduce_fusion.3) | copy-start | bytes 1572868
  201.9 4.1 copy-start.36
  207.6 1.9 copy-start.39
  207.6 1.9 copy-start.24
  209.5 3.0 copy-start.37
  246.8 2.6 copy-start.21
  285.4 3.3 copy-start.23
  285.4 3.3 copy-start.30
  410.4 1.9 copy-start.18
  410.4 2.0 copy-start.20
  412.4 1.4 copy-start.4
  414.4 1.6 copy-start.13
  415.9 3.5 copy-start.11
  419.4 7.4 %copy-start.34 = (bf16[1024,128]{0,1:T(8,128)(2,1)S(1)}, bf16[1024,128]{0,1:T(8,128)(2,1)}, u32[]{:S(2)}) copy-start(bf16[1024,128]{0,1:T(8,128)(2,1)} %copy.47) | copy-start | bytes 786436
  426.8 4.1 copy-start.33
  431.6 61.7 %copy-start.26 = (bf16[1024,1024]{1,0:T(8,128)(2,1)S(1)}, bf16[1024,1024]{1,0:T(8,128)(2,1)}, u32[]{:S(2)}) copy-start(bf16[1024,1024]{1,0:T(8,128)(2,1)} %get-tuple-element.65) | copy-start | bytes 6291460
  526.8 1.8 copy-start.32
  526.8 1.9 copy-start.22
  528.8 1.3 copy-start.16
  530.1 1.4 copy-start.31
  530.1 2.4 copy-start.35
  531.4 2.1 copy-start.27
  533.6 2.0 copy-start.28
  (8 other events, 8.4 us)

commit v3 on v2

--- a/solution.py
+++ b/solution.py
@@ -12,6 +12,8 @@
 LOG2E = 1.4426950408889634
 RUN = 128
 CHUNK = 512
+VMEM = 60 * 2**20
+UNROLL = 4
 TAG = 16
 X_ROWS = RUN + TAG
 KV_ROWS = 8 * RUN + TAG
@@ -331,7 +333,7 @@
             vals[dst, HEAD:] = jnp.ones((RUN, HEAD), BF)
             return 0
 
-        lax.fori_loop(0, n_runs, place, 0)
+        lax.fori_loop(0, n_runs, place, 0, unroll=8)
 
     run = own[step]
     query = stacked(q_ref)
@@ -350,10 +352,16 @@
     last = run // (CHUNK // RUN)
 
     def plain(j, _):
+        for u in range(UNROLL):
+            visit(j * UNROLL + u, False)
+        return 0
+
+    def single(j, _):
         visit(j, False)
         return 0
 
-    lax.fori_loop(0, last, plain, 0)
+    lax.fori_loop(0, last // UNROLL, plain, 0)
+    lax.fori_loop(last // UNROLL * UNROLL, last, single, 0)
     visit(last, True)
     total = acc[:, HEAD:]
     out = acc[:, :HEAD] / total
@@ -383,7 +391,7 @@
         ),
         out_shape=(jax.ShapeDtypeStruct(q.shape, F32), jax.ShapeDtypeStruct(q.shape, F32)),
         compiler_params=pltpu.CompilerParams(
-            dimension_semantics=("arbitrary",), vmem_limit_bytes=48 * 2**20
+            dimension_semantics=("arbitrary",), vmem_limit_bytes=VMEM
         ),
         name="attention_forward",
     )(order, own, q, kv)
@@ -410,7 +418,7 @@
             vals[dst, :] = kv_ref[src, HEAD:]
             return 0
 
-        lax.fori_loop(0, n_runs, place, 0)
+        lax.fori_loop(0, n_runs, place, 0, unroll=8)
 
     run = own[step]
     query = stacked(q_ref)
@@ -438,10 +446,16 @@
     last = run // (CHUNK // RUN)
 
     def plain(j, _):
+        for u in range(UNROLL):
+            visit(j * UNROLL + u, False)
+        return 0
+
+    def single(j, _):
         visit(j, False)
         return 0
 
-    lax.fori_loop(0, last, plain, 0)
+    lax.fori_loop(0, last // UNROLL, plain, 0)
+    lax.fori_loop(last // UNROLL * UNROLL, last, single, 0)
     visit(last, True)
     out = dq_t[...].T * SCALE
     dq_ref[:, :HEAD] = out[:RUN]
@@ -456,7 +470,7 @@
             dkv_ref[dst, HEAD:] = dv[src, :].astype(BF)
             return 0
 
-        lax.fori_loop(0, n_runs, give, 0)
+        lax.fori_loop(0, n_runs, give, 0, unroll=8)
 
 
 def attention_backward(order, own, q, g, o, log, kv):
@@ -484,20 +498,10 @@
         ),
         out_shape=(jax.ShapeDtypeStruct(q.shape, F32), jax.ShapeDtypeStruct((length, 2 * HEAD), BF)),
         compiler_params=pltpu.CompilerParams(
-            dimension_semantics=("arbitrary",), vmem_limit_bytes=48 * 2**20
+            dimension_semantics=("arbitrary",), vmem_limit_bytes=VMEM
         ),
         name="attention_backward",
     )(order, own, q, g, o, log, kv)
-
-
-def rotate(value, cos, sin):
-    a, b = value[..., : HEAD // 2], value[..., HEAD // 2 :]
-    return jnp.concatenate([a * cos - b * sin, b * cos + a * sin], axis=-1)
-
-
-def rotate_back(grad, cos, sin):
-    a, b = grad[..., : HEAD // 2], grad[..., HEAD // 2 :]
-    return jnp.concatenate([a * cos + b * sin, b * cos - a * sin], axis=-1)
 
 
 def inverse_rms(value):
@@ -510,6 +514,61 @@
     return inverse * scaled - value * inverse * inverse * inverse * inner / value.shape[-1]
 
 
+def finish_kernel(
+    gate_ref, up_ref, down_ref, out_ref, query_ref, pair_ref, parts_ref, grad_ref, x_ref, scale_ref,
+    middle_ref, last_ref,
+    layer_o, input_o, query_o, key_o, value_o, out_o, gate_o, up_o, down_o,
+):
+    for source, target in (
+        (gate_ref, gate_o), (up_ref, up_o), (down_ref, down_o), (out_ref, out_o), (query_ref, query_o)
+    ):
+        target[...] = source[...].astype(F32)
+    for i in range(8):
+        to = slice(i * HEAD, (i + 1) * HEAD)
+        key_o[:, to] = pair_ref[:, 2 * i * HEAD : (2 * i + 1) * HEAD].astype(F32)
+        value_o[:, to] = pair_ref[:, (2 * i + 1) * HEAD : (2 * i + 2) * HEAD].astype(F32)
+    x = x_ref[...].astype(F32)
+    grad = jnp.sum(parts_ref[...].astype(F32), axis=0)
+    input_o[...] = grad_ref[...] + norm_back(x, inverse_rms(x), scale_ref[...], grad)
+    last = jnp.sum(last_ref[...].astype(F32), axis=0)
+    layer_o[...] = (middle_ref[...] + last).astype(BF)
+
+
+def finish(gate_up, down, out, qkv, parts, grad, x, scale, middle, last):
+    steps = 4
+    tokens, width = x.shape
+
+    def rows_of(a, n, offset=0):
+        return pl.BlockSpec((n // steps, a.shape[-1]), lambda i: (i + offset, 0))
+
+    def deep(a):
+        return pl.BlockSpec((a.shape[0], tokens // steps, width), lambda i: (0, i, 0))
+
+    part = qkv.shape[0] // 2
+    specs = [
+        rows_of(gate_up, part), rows_of(gate_up, part, steps), rows_of(down, down.shape[0]),
+        rows_of(out, out.shape[0]), rows_of(qkv, part), rows_of(qkv, part, steps), deep(parts),
+        rows_of(grad, tokens), rows_of(x, tokens), pl.BlockSpec(scale.shape, lambda i: (0, 0)),
+        rows_of(middle, tokens), deep(last),
+    ]
+    shapes = [
+        ((tokens, width), BF), ((tokens, width), F32), ((part, 2 * width), F32), ((part, width), F32),
+        ((part, width), F32), (out.shape, F32), ((part, gate_up.shape[1]), F32),
+        ((part, gate_up.shape[1]), F32), (down.shape, F32),
+    ]
+    return pl.pallas_call(
+        finish_kernel,
+        grid=(steps,),
+        in_specs=specs,
+        out_specs=[pl.BlockSpec((s[0] // steps, s[1]), lambda i: (i, 0)) for s, _ in shapes],
+        out_shape=tuple(jax.ShapeDtypeStruct(s, d) for s, d in shapes),
+        compiler_params=pltpu.CompilerParams(
+            dimension_semantics=("arbitrary",), vmem_limit_bytes=VMEM
+        ),
+        name="finish",
+    )(gate_up, gate_up, down, out, qkv, qkv, parts, grad, x, scale, middle, last)
+
+
 def dot(a, b):
     return jnp.dot(a, b, preferred_element_type=F32)
 
@@ -524,6 +583,133 @@
 
 def row_of(vector):
     return jnp.pad(vector.reshape(1, -1), ((0, 0), (0, 128 - vector.shape[-1])))
+
+
+def project_kernel(x_ref, w_ref, scale_ref, head_ref, cos_ref, sin_ref, tag_ref, n_ref, p_ref, q_ref, kv_ref):
+    step = pl.program_id(0)
+    x = x_ref[0, :RUN, :].astype(F32)
+    low = (x * inverse_rms(x) * scale_ref[...]).astype(BF)
+    n_ref[...] = low
+    out = mm(low, w_ref[...])
+    p_ref[...] = out[:, : 3 * HEAD]
+    turned = []
+    for h in range(3):
+        v = out[:, h * HEAD : (h + 1) * HEAD]
+        v = v * inverse_rms(v) * head_ref[h : h + 1, :]
+        turned.append((v * cos_ref[...] + pltpu.roll(v, HEAD // 2, 1) * sin_ref[...]).astype(BF))
+    q_ref[:, :HEAD] = turned[0]
+    q_ref[:, HEAD:] = turned[1]
+    at = pl.ds(pl.multiple_of(step * RUN, RUN), RUN)
+    kv_ref[at, :HEAD] = turned[2]
+    kv_ref[at, HEAD:] = out[:, 3 * HEAD :].astype(BF)
+
+    @pl.when(step == 0)
+    def _():
+        kv_ref[pl.ds(8 * RUN, TAG), :] = tag_ref[...]
+
+
+def project(x, w, scale, head_scale, cos, sin, tag):
+    width = x.shape[-1]
+    group = 8 * RUN
+
+    def fixed(a):
+        return pl.BlockSpec(a.shape, lambda i: (0,) * a.ndim)
+
+    def moving(n):
+        return pl.BlockSpec((RUN, n), lambda i: (i, 0))
+
+    return pl.pallas_call(
+        project_kernel,
+        grid=(8,),
+        in_specs=[
+            pl.BlockSpec((1, X_ROWS, width), lambda i: (i, 0, 0)),
+            fixed(w), fixed(scale), fixed(head_scale), moving(HEAD), moving(HEAD), fixed(tag),
+        ],
+        out_specs=[
+            moving(width), moving(3 * HEAD), moving(2 * HEAD),
+            pl.BlockSpec((KV_ROWS, 2 * HEAD), lambda i: (0, 0)),
+        ],
+        out_shape=(
+            jax.ShapeDtypeStruct((group, width), BF),
+            jax.ShapeDtypeStruct((group, 3 * HEAD), F32),
+            jax.ShapeDtypeStruct((group, 2 * HEAD), BF),
+            jax.ShapeDtypeStruct((KV_ROWS, 2 * HEAD), BF),
+        ),
+        compiler_params=pltpu.CompilerParams(
+            dimension_semantics=("arbitrary",), vmem_limit_bytes=VMEM
+        ),
+        name="project",
+    )(x, w, scale, head_scale, cos, sin, tag)
+
+
+def unproject_kernel(
+    kv_ref, t_ref, p_ref, x_ref, w_ref, head_ref, cos_ref, sin_ref, mlp_ref,
+    g_ref, n_ref, tile_ref, attn_acc, head_acc,
+):
+    step = pl.program_id(0)
+
+    @pl.when(step == 0)
+    def _():
+        attn_acc[...] = jnp.zeros_like(attn_acc)
+        head_acc[...] = jnp.zeros_like(head_acc)
+
+    kv = kv_ref[0].astype(F32)
+    for chip in range(1, 8):
+        kv = kv + kv_ref[chip].astype(F32)
+    for h in range(3):
+        turn = kv[:, :HEAD] if h == 2 else t_ref[:, h * HEAD : (h + 1) * HEAD]
+        grad = turn * cos_ref[...] - pltpu.roll(turn, HEAD // 2, 1) * sin_ref[...]
+        v = p_ref[:, h * HEAD : (h + 1) * HEAD]
+        inverse = inverse_rms(v)
+        back = norm_back(v, inverse, head_ref[h : h + 1, :], grad)
+        g_ref[:, h * HEAD : (h + 1) * HEAD] = back.astype(BF)
+        head_acc[h // 2 : h // 2 + 1, :] += jnp.sum(grad * v * inverse, axis=0, keepdims=True)
+    g_ref[:, 3 * HEAD :] = kv[:, HEAD:].astype(BF)
+    wide = mm(g_ref[...], w_ref[...], NT)
+    n_ref[...] = wide.astype(BF)
+    x = x_ref[0, :RUN, :].astype(F32)
+    attn_acc[...] += jnp.sum(wide * x * inverse_rms(x), axis=0, keepdims=True)
+
+    @pl.when(step == pl.num_programs(0) - 1)
+    def _():
+        tile_ref[...] = jnp.zeros_like(tile_ref)
+        for j in range(8):
+            tile_ref[j * 8 : j * 8 + 1, :] = attn_acc[:, j * 128 : (j + 1) * 128]
+            tile_ref[j * 8 + 1 : j * 8 + 2, :] = mlp_ref[:, j * 128 : (j + 1) * 128]
+            tile_ref[j * 8 + 2 : j * 8 + 4, :] = head_acc[...]
+
+
+def unproject(kv_parts, turn, pre, x, w, head_scale, cos, sin, mlp_part):
+    width = x.shape[-1]
+    group = 8 * RUN
+
+    def fixed(a):
+        return pl.BlockSpec(a.shape, lambda i: (0,) * a.ndim)
+
+    def moving(n):
+        return pl.BlockSpec((RUN, n), lambda i: (i, 0))
+
+    return pl.pallas_call(
+        unproject_kernel,
+        grid=(8,),
+        in_specs=[
+            pl.BlockSpec((8, RUN, 2 * HEAD), lambda i: (0, i, 0)),
+            moving(2 * HEAD), moving(3 * HEAD),
+            pl.BlockSpec((1, X_ROWS, width), lambda i: (i, 0, 0)),
+            fixed(w), fixed(head_scale), moving(HEAD), moving(HEAD), fixed(mlp_part),
+        ],
+        out_specs=[moving(4 * HEAD), moving(width), pl.BlockSpec((64, 128), lambda i: (0, 0))],
+        out_shape=(
+            jax.ShapeDtypeStruct((group, 4 * HEAD), BF),
+            jax.ShapeDtypeStruct((group, width), BF),
+            jax.ShapeDtypeStruct((64, 128), F32),
+        ),
+        scratch_shapes=[pltpu.VMEM((1, width), F32), pltpu.VMEM((2, HEAD), F32)],
+        compiler_params=pltpu.CompilerParams(
+            dimension_semantics=("arbitrary",), vmem_limit_bytes=VMEM
+        ),
+        name="unproject",
+    )(kv_parts, turn, pre, x, w, head_scale, cos, sin, mlp_part)
 
 
 def local(
@@ -569,22 +755,14 @@
     x_all = x_all.reshape(8, X_ROWS, width)
     own_bf = x_all[:, RUN, 0]
     own = own_bf.astype(jnp.int32)
-    x_wide = x_all[:, :RUN].reshape(group, width).astype(F32)
-    attn_inverse_all = inverse_rms(x_wide)
-    norm_one = (x_wide * attn_inverse_all * attn_scale).astype(BF)
-    qkv = dot(norm_one, w_qkv)
-    pre = qkv[:, :384].reshape(group, 3, HEAD)
-    head_scale = jnp.stack([query_scale, query_scale, key_scale], axis=1)
-    head_inverse = inverse_rms(pre)
+    head_scale = jnp.concatenate([query_scale, query_scale, key_scale], axis=0)
     place_rows = (own[:, None] * RUN + jnp.arange(RUN, dtype=jnp.int32)[None, :]).reshape(group)
     frequency = 1.0 / THETA ** (jnp.arange(0, HEAD, 2, dtype=F32) / HEAD)
-    angle = place_rows.astype(F32)[:, None] * frequency[None, :]
-    cos, sin = jnp.cos(angle)[:, None, :], jnp.sin(angle)[:, None, :]
-    turned = rotate(pre * head_inverse * head_scale, cos, sin).astype(BF).reshape(group, 384)
-    queries = turned[:, :256]
-    kv = jnp.concatenate([turned[:, 256:], qkv[:, 384:].astype(BF)], axis=1)
+    angle = place_rows.astype(F32)[:, None] * jnp.tile(frequency, 2)[None, :]
+    sign = jnp.where(jnp.arange(HEAD) < HEAD // 2, -1.0, 1.0).astype(F32)
+    cos, sin = jnp.cos(angle), jnp.sin(angle) * sign[None, :]
     tag = jnp.pad(jnp.broadcast_to(own_bf[None, :], (TAG, 8)), ((0, 0), (0, 2 * HEAD - 8)))
-    kv = jnp.concatenate([kv, tag], axis=0)
+    norm_one, pre, queries, kv = project(x_all, w_qkv, attn_scale, head_scale, cos, sin, tag)
 
     plan = Plan()
     own_kv = block(4, At.chip, KV_ROWS)
@@ -607,19 +785,17 @@
     right_id = plan.add(Shift(x=1), full(0), own_kv)
     left_id = plan.add(Shift(x=-1), full(0), own_kv)
     plan.add(None, full(0), own_kv)
-    relays = [
-        plan.gather_tokens(1, 5, tokens),
-        plan.weights(2, 6, part, ff, 0),
-        plan.weights(3, 6, part, ff, ff),
-    ]
+    relay_tokens = plan.gather_tokens(1, 5, tokens)
+    relays = [plan.weights(2, 6, part, ff, 0), plan.weights(3, 6, part, ff, ff)]
     side_right = plan.add(Shift(x=1), side_kv, side_kv, needs=[side])
     side_left = plan.add(Shift(x=-1), side_kv, side_kv, needs=[side])
     plan.add(Shift(x=1), left(upper, 0), left(upper, 0), needs=[right_id])
     plan.add(Shift(x=-1), right(lower, 0), right(lower, 0), needs=[left_id])
+    relay_tokens()
+    plan.add(Shift(x=1), left(upper, 1), left(upper, 1), needs=[side_right])
+    plan.add(Shift(x=-1), right(lower, 1), right(lower, 1), needs=[side_left])
     for relay in relays:
         relay()
-    plan.add(Shift(x=1), left(upper, 1), left(upper, 1), needs=[side_right])
-    plan.add(Shift(x=-1), right(lower, 1), right(lower, 1), needs=[side_left])
     kv_all, cot_all, w_gu = exchange(
         plan, 2, (((8 * KV_ROWS, 256), BF), ((group, width), BF), ((width, 2 * ff), BF)),
         kv, cot, gate_weight, up_weight,
@@ -685,12 +861,11 @@
     down_half = my_half(down_wgrad, down_got)
 
     plan = Plan()
-    relay = plan.gather_tokens(0, 3, tokens)
+    plan.gather_tokens(0, 3, tokens)()
     plan.scatter_chips(
         lambda io, n: io[1].at[:, pl.ds(pl.multiple_of(n * 16, 16), 16)], lambda io, n: io[4].at[n]
     )
     plan.scatter_chips(rows(ff // 8)(2), lambda io, n: io[5].at[n])
-    relay()
     branch_grad, gate_up_pieces, down_pieces = exchange(
         plan, 6, (((group, width), BF), ((8, 8, 16, ff), BF), ((8, ff // 8, width // 2), BF)),
         branch_grad_own, gate_up_half, down_half,
@@ -730,32 +905,14 @@
     )
     down_pair = summed(down_parts, 4).astype(BF)
     output_half = my_half(output_wgrad, output_got)
-    kv_sum = summed(kv_parts, 8)
-    turn = jnp.concatenate([query_turn, kv_sum[:, :HEAD]], axis=1).reshape(group, 3, HEAD)
-    head_grad = rotate_back(turn, cos, sin)
-    pre_grad = norm_back(pre, head_inverse, head_scale, head_grad)
-    head_gain_parts = jnp.sum(head_grad * pre * head_inverse, axis=0)
-    qkv_grad = jnp.concatenate(
-        [pre_grad.reshape(group, 384).astype(BF), kv_sum[:, HEAD:].astype(BF)], axis=1
+    qkv_grad, norm_one_part, gain_parts = unproject(
+        kv_parts.reshape(8, group, 2 * HEAD), query_turn, pre, x_all, w_qkv, head_scale, cos, sin,
+        mlp_gain_part.reshape(1, width),
     )
     qkv_wgrad = dot_t(norm_one, qkv_grad).astype(BF).reshape(8, part, 512)
-    norm_one_wide = lax.dot_general(qkv_grad, w_qkv, NT, preferred_element_type=F32)
-    attn_gain_part = jnp.sum(norm_one_wide * x_wide * attn_inverse_all, axis=0)
-    query_gain_part = (head_gain_parts[0] + head_gain_parts[1]).reshape(8, 1, 16)
-    key_gain_part = head_gain_parts[2].reshape(8, 1, 16)
-    gain_parts = jnp.concatenate(
-        [
-            attn_gain_part.reshape(8, 1, 128),
-            mlp_gain_part.reshape(8, 1, 128),
-            jnp.pad(query_gain_part, ((0, 0), (0, 0), (0, 112))),
-            jnp.pad(key_gain_part, ((0, 0), (0, 0), (0, 112))),
-            jnp.zeros((8, 4, 128), F32),
-        ],
-        axis=1,
-    ).reshape(64, 128)
 
     plan = Plan()
-    plan.return_tokens(0, 6, tokens)
+    plan.return_tokens(0, 4, tokens)
 
     def wgrad_piece(io, chip, c):
         return io[1].at[
@@ -768,15 +925,15 @@
         plan.add(
             shift,
             lambda io, at, s=shift: wgrad_piece(io, s.to(at).chip(), s.to(at).c),
-            lambda io, at: io[7].at[at.chip() * 2 + at.c],
+            lambda io, at: io[5].at[at.chip() * 2 + at.c],
         )
     plan.add(
         None,
         lambda io, at: wgrad_piece(io, at.chip(), at.c),
-        lambda io, at: io[7].at[at.chip() * 2 + at.c],
-    )
-    plan.scatter_chips(rows(n_rows // 8)(2), lambda io, n: io[8].at[n])
-    plan.scatter_group(rows(8)(3), rows(8)(9))
+        lambda io, at: io[5].at[at.chip() * 2 + at.c],
+    )
+    plan.scatter_chips(rows(n_rows // 8)(2), lambda io, n: io[6].at[n])
+    plan.scatter_group(rows(8)(3), rows(8)(7))
 
     def stacked_rows(ref, size, total):
         def land(io, chip, c):
@@ -793,75 +950,72 @@
 
         return land, lambda io, c: io[ref].at[:, at_core(c)]
 
+    norm_one_parts, qkv_pieces, output_pieces, gain_sums = exchange(
+        plan, 8,
+        (
+            ((group, width), BF), ((16, 8, 16, 256), BF), ((8, n_rows // 8, width // 2), BF),
+            ((64, 128), F32),
+        ),
+        norm_one_part, qkv_wgrad, output_half, gain_parts,
+    )
+    qkv_sum = jnp.sum(qkv_pieces.astype(F32), axis=0).astype(BF)
+    output_sum = jnp.sum(output_pieces.astype(F32), axis=0).astype(BF)
+    gain_sum = summed(gain_sums, 8)
+
+    plan = Plan()
+    to_group = plan.scatter_group(
+        lambda io, n: io[0].at[n],
+        lambda io, n: io[6].at[:, pl.ds(pl.multiple_of(n * 256, 256), 256)],
+    )
     later = [
-        plan.gather_chips(full(4), *stacked_rows(10, 16, part)),
-        plan.gather_chips(full(5), *side_columns(11, ff // 8)),
+        plan.gather_chips(full(4), *stacked_rows(11, 16, part)),
+        plan.gather_chips(full(5), *side_columns(12, ff // 8)),
+        plan.gather_chips(full(1), *side_columns(8, n_rows // 8)),
     ]
+    plan.gather_context(2, 9, 8)
+    own_block = block(3, lambda at: at.c, tokens)
+    other_block = block(3, lambda at: 1 - at.c, tokens)
+
+    def landed(n):
+        return lambda io, at: io[10].at[pl.ds(n * tokens, tokens)]
+
+    plan.add(Shift(d=1), own_block, landed(1), away)
+    plan.add(Shift(d=1, c=1), other_block, landed(1), away)
+    plan.add(None, own_block, landed(0), home)
+    plan.add(Shift(c=1), other_block, landed(0), home)
+    later.append(plan.gather_chips(full(6), *stacked_rows(7, 16, part), needs=to_group))
     for relay, _ in later:
         relay()
     for _, share in later:
         share()
-    norm_one_parts, qkv_pieces, output_pieces, gain_sums, gate_up_final, down_final = exchange(
-        plan, 8,
-        (
-            ((group, width), BF), ((16, 8, 16, 256), BF), ((8, n_rows // 8, width // 2), BF),
-            ((64, 128), F32), ((2 * part, 8 * ff), BF), ((ff, width), BF),
-        ),
-        norm_one_wide.astype(BF), qkv_wgrad, output_half, gain_parts, gate_up_own, down_sum,
-    )
-    qkv_sum = jnp.sum(qkv_pieces.astype(F32), axis=0).astype(BF)
-    output_sum = jnp.sum(output_pieces.astype(F32), axis=0).astype(BF)
-    gain_sum = summed(gain_sums, 8)
-
-    plan = Plan()
-    to_group = plan.scatter_group(
-        lambda io, n: io[0].at[n],
-        lambda io, n: io[4].at[:, pl.ds(pl.multiple_of(n * 256, 256), 256)],
-    )
-    relay_output, share_output = plan.gather_chips(full(1), *side_columns(6, n_rows // 8))
-    plan.gather_context(2, 7, 8)
-    own_block = block(3, lambda at: at.c, tokens)
-    other_block = block(3, lambda at: 1 - at.c, tokens)
-
-    def landed(n):
-        return lambda io, at: io[8].at[pl.ds(n * tokens, tokens)]
-
-    plan.add(Shift(d=1), own_block, landed(1), away)
-    plan.add(Shift(d=1, c=1), other_block, landed(1), away)
-    plan.add(None, own_block, landed(0), home)
-    plan.add(Shift(c=1), other_block, landed(0), home)
-    relay_qkv, share_qkv = plan.gather_chips(full(4), *stacked_rows(5, 16, part), needs=to_group)
-    relay_output()
-    relay_qkv()
-    share_output()
-    share_qkv()
-    _, qkv_final, output_final, gain_all, down_last = exchange(
+    _, qkv_final, output_final, gain_all, down_last, gate_up_final, down_final = exchange(
         plan, 9,
         (
             ((16, 2048), BF), ((2 * part, 2048), BF), ((n_rows, width), BF), ((128, 128), F32),
-            ((2 * tokens, width), BF),
-        ),
-        qkv_sum, output_sum, gain_sum, down_pair,
-    )
-    layer_out = (middle + summed(down_last, 2)).astype(BF)
-    attn_inverse = inverse_rms(residual)
-    input_grad = middle_grad + norm_back(residual, attn_inverse, attn_scale, summed(norm_one_parts, 8))
+            ((2 * tokens, width), BF), ((2 * part, 8 * ff), BF), ((ff, width), BF),
+        ),
+        qkv_sum, output_sum, gain_sum, down_pair, gate_up_own, down_sum,
+    )
+    layer_out, input_grad, query_wgrad, key_wgrad, value_wgrad, output_wgrad, gate_wgrad, up_wgrad, down_wgrad = finish(
+        gate_up_final, down_final, output_final, qkv_final, norm_one_parts.reshape(8, tokens, width),
+        middle_grad, hidden, attn_scale, middle, down_last.reshape(2, tokens, width),
+    )
     gain_total = summed(gain_all, 16)
-    key_value = qkv_final[part:].astype(F32).reshape(part, 8, 2, HEAD)
+    head = lax.axis_index("dp") * 4 + lax.axis_index("fsdp")
     return (
         layer_out[None],
         input_grad[None],
         gain_total[0],
-        qkv_final[:part].astype(F32),
-        key_value[:, :, 0].reshape(part, width),
-        key_value[:, :, 1].reshape(part, width),
-        output_final.astype(F32),
-        gain_total[2, :16],
-        gain_total[3, :16],
+        query_wgrad,
+        key_wgrad,
+        value_wgrad,
+        output_wgrad,
+        lax.dynamic_slice_in_dim(gain_total[2], head * 16, 16),
+        lax.dynamic_slice_in_dim(gain_total[3], head * 16, 16),
         gain_total[1],
-        gate_up_final[:part].astype(F32),
-        gate_up_final[part:].astype(F32),
-        down_final.astype(F32),
+        gate_wgrad,
+        up_wgrad,
+        down_wgrad,
     )
 
 

time: 547 us -> 493 us (0.901); the launches traced: 537 us -> 492 us
  other arithmetic: 46.3 us -> 24.8 us
  local copies, waits for them, and re-layouts: 26.3 us -> 9.39 us
  matrix products: 33.7 us -> 27.9 us
    pallas_call x0 -> x3, Pallas kernels: none -> 26.7 us  [the longest x1 10.6 us: unproject(): pl.pallas_call(unproject_kernel, grid=(8,), in_specs=[pl.BlockSpec((8, RU...]
    pallas_call x9, Pallas kernels: 351 us -> 335 us  [exchange(): pl.pallas_call(kernel, out_shape=tuple((jax.ShapeDtypeStruct(s, d) for s,...]
    unnamed x86 -> x40, local copies, waits for them, and re-layouts: 10 us -> 0.09 us
    convert_element_type x5 -> x1, other arithmetic: 6.72 us -> 0.07 us  [local(): angle = place_rows.astype(F32)[:, None] * jnp.tile(frequency, 2)[None, :]]
    slice x8 -> x0, local copies, waits for them, and re-layouts: 5.93 us -> none  [the longest x1 2.74 us: local(): key_value[:, :, 1].reshape(part, width)]
    pallas_call x1, Pallas kernels: 31.2 us -> 25.5 us  [attention_forward(): pl.pallas_call(forward_kernel, grid_spec=pltpu.PrefetchScalarGridSpec(num...]
    dot_general x4 -> x3, matrix products: 11.2 us -> 9.97 us  [dot(): return jnp.dot(a, b, preferred_element_type=F32)]
where the time goes in v3:
time: 493 us; the launch traced here: 492 us
  Pallas kernels  426 us (86%)
  matrix products  27.9 us (6%)
  other arithmetic  24.8 us (5%)
  local copies, waits for them, and re-layouts  9.39 us (2%)
    pallas_call x9, Pallas kernels, exchange(): pl.pallas_call(kernel, out_shape=tuple((jax.ShapeDtypeStruct(s, d) for s,...  335 us
    pallas_call x1, Pallas kernels, attention_backward(): pl.pallas_call(backward_kernel, grid_spec=pltpu.PrefetchScalarGridSpec(nu...  39.5 us
    pallas_call x1, Pallas kernels, attention_forward(): pl.pallas_call(forward_kernel, grid_spec=pltpu.PrefetchScalarGridSpec(num...  25.5 us
    dot_general x4, matrix products, dot_t(): lax.dot_general(a, b, (((0,), (0,)), ((), ())), preferred_element_type=F32)  11.6 us
    pallas_call x1, Pallas kernels, unproject(): pl.pallas_call(unproject_kernel, grid=(8,), in_specs=[pl.BlockSpec((8, RU...  10.6 us
    dot_general x3, matrix products, dot(): return jnp.dot(a, b, preferred_element_type=F32)  9.97 us

profile of v3, /device:TPU:1, one launch (start us, length us, event | category | flops | bytes accessed | tf_op | source)
XLA Modules:
  0.0 492.2 jit_solution(5816249046674057952)
XLA Ops:
  3.3 1.7 concatenate.12.refs_0_
  7.0 35.8 %exchange_1.1 = (bf16[1152,1024]{1,0:T(8,128)(2,1)}, f32[64,128]{1,0:T(8,128)}, bf16[1024,512]{1,0:T(8,128)(2,1)}) custom-call(bf16[144,1024]{1,0:T(8,128)(2,1)} %concatenate.12.refs_0_, f32[8,128]{1,0:T(8,128)} %concatenate.13.refs_1_, bf16[128,2048]{1,0:T(8,128)(2,1)} %refs_2_.2, bf16[128,1024]{1,0:T(8,128)(2,1)} %refs_3_.2, bf16[128,1024]{1,0:T(8,128)(2,1)} %refs_4_.1), custom_call_target="tpu_custom_call" | custom-call | tf_op jit(solution)/shard_map/exchange_1/pallas_call | solution.py:147
  45.5 3.0 fusion.1
  50.6 9.1 %project.1 = (bf16[1024,1024]{1,0:T(8,128)(2,1)}, f32[1024,384]{1,0:T(8,128)}, bf16[1024,256]{1,0:T(8,128)(2,1)}, bf16[1040,256]{1,0:T(8,128)(2,1)}) custom-call(bf16[8,144,1024]{2,1,0:T(8,128)(2,1)} %bitcast.77, bf16[1024,512]{1,0:T(8,128)(2,1)} %get-tuple-element.60.w_ref, f32[1,1024]{1,0:T(1,128)} %get-tuple-element.115.scale_ref, ...), custom_call_target="tpu_custom_call" | custom-call | tf_op jit(solution)/shard_map/project/pallas_call | solution.py:621
  59.6 43.4 %exchange_2.1 = (bf16[8320,256]{1,0:T(8,128)(2,1)}, bf16[1024,1024]{1,0:T(8,128)(2,1)}, bf16[1024,768]{1,0:T(8,128)(2,1)}) custom-call(bf16[1040,256]{1,0:T(8,128)(2,1)} %get-tuple-element.62.refs_0_, bf16[128,1024]{1,0:T(8,128)(2,1)} %bitcast.89, bf16[128,3072]{1,0:T(8,128)(2,1)} %refs_2_.3, bf16[128,3072]{1,0:T(8,128)(2,1)} %refs_3_.3), custom_call_target="tpu_custom_call" | custom-call | tf_op jit(solution)/shard_map/exchange_2/pallas_call | solution.py:147
  104.9 25.5 %attention_forward.1 = (f32[1024,256]{1,0:T(8,128)}, f32[1024,256]{1,0:T(8,128)}) custom-call(s32[64]{0:T(128)} %reshape.163.order, s32[8]{0:T(128)} %convert_element_type.128.own, bf16[1024,256]{1,0:T(8,128)(2,1)} %get-tuple-element.64.q_ref, bf16[8320,256]{1,0:T(8,128)(2,1)} %get-tuple-element.63.kv_ref), custom_call_target="tpu_custom_call" | custom-call | tf_op jit(solution)/shard_map/attention_forward/pallas_call | solution.py:379
  130.4 3.3 convolution_convert_fusion.1.refs_0_
  133.7 28.9 %exchange_3.1 = bf16[1024,1024]{1,0:T(8,128)(2,1)} custom-call(bf16[1024,1024]{1,0:T(8,128)(2,1)} %convolution_convert_fusion.1.refs_0_), custom_call_target="tpu_custom_call" | custom-call | tf_op jit(solution)/shard_map/exchange_3/pallas_call | solution.py:147
  162.5 2.1 convert_reduce_fusion.1
  165.6 25.6 %exchange_4.1 = bf16[1024,1024]{1,0:T(8,128)(2,1)} custom-call(bf16[128,1024]{1,0:T(8,128)(2,1)} %multiply_convert_fusion.3.refs_0_), custom_call_target="tpu_custom_call" | custom-call | tf_op jit(solution)/shard_map/exchange_4/pallas_call | solution.py:147
  191.2 4.1 fusion.11
  195.3 1.6 multiply_convert_fusion.2
  196.9 1.9 convolution_convert_fusion.5.refs_2_
  198.8 3.0 convolution_convert_fusion.3
  201.8 3.2 convolution_convert_fusion.2.refs_0_
  205.0 29.0 %exchange_5.1 = (bf16[1024,1024]{1,0:T(8,128)(2,1)}, bf16[8,128,384]{2,1,0:T(8,128)(2,1)}, bf16[384,512]{1,0:T(8,128)(2,1)}) custom-call(bf16[1024,1024]{1,0:T(8,128)(2,1)} %convolution_convert_fusion.2.refs_0_, bf16[8,128,768]{2,1,0:T(8,128)(2,1)} %bitcast.81, bf16[384,1024]{1,0:T(8,128)(2,1)} %convolution_convert_fusion.5.refs_2_), custom_call_target="tpu_custom_call" | custom-call | tf_op jit(solution)/shard_map/exchange_5/pallas_call | solution.py:147
  234.0 2.0 add_convert_fusion.1.refs_2_
  236.0 2.4 add_convert_fusion.refs_1_
  240.6 34.6 %exchange_6.1 = (bf16[1024,1024]{1,0:T(8,128)(2,1)}, bf16[8,8,16,384]{3,2,1,0:T(8,128)(2,1)}, bf16[8,48,512]{2,1,0:T(8,128)(2,1)}) custom-call(bf16[128,1024]{1,0:T(8,128)(2,1)} %get-tuple-element.107.refs_0_, bf16[8,128,384]{2,1,0:T(8,128)(2,1)} %add_convert_fusion.refs_1_, bf16[384,512]{1,0:T(8,128)(2,1)} %add_convert_fusion.1.refs_2_), custom_call_target="tpu_custom_call" | custom-call | tf_op jit(solution)/shard_map/exchange_6/pallas_call | solution.py:147
  275.2 3.3 convolution_convert_fusion.6.refs_2_
  278.5 1.6 convolution_convert_fusion.7.g_ref
  280.0 39.5 %attention_backward.1 = (f32[1024,256]{1,0:T(8,128)}, bf16[8192,256]{1,0:T(8,128)(2,1)}) custom-call(s32[64]{0:T(128)} %reshape.163.order, s32[8]{0:T(128)} %convert_element_type.128.own, bf16[1024,256]{1,0:T(8,128)(2,1)} %get-tuple-element.64.q_ref, bf16[1024,256]{1,0:T(8,128)(2,1)} %convolution_convert_fusion.7.g_ref, ...), custom_call_target="tpu_custom_call" | custom-call | tf_op jit(solution)/shard_map/attention_backward/pallas_call | solution.py:481
  320.3 2.6 convolution_convert_fusion.refs_1_
  322.9 55.4 %exchange_7.1 = (bf16[8192,256]{1,0:T(8,128)(2,1)}, bf16[1024,1024]{1,0:T(8,128)(2,1)}, bf16[256,512]{1,0:T(8,128)(2,1)}, bf16[16,3072]{1,0:T(8,128)(2,1)}) custom-call(bf16[8192,256]{1,0:T(8,128)(2,1)} %get-tuple-element.73.refs_0_, bf16[1024,1024]{1,0:T(8,128)(2,1)} %convolution_convert_fusion.refs_1_, ...), custom_call_target="tpu_custom_call" | custom-call | tf_op jit(solution)/shard_map/exchange_7/pallas_call | solution.py:147
  378.4 1.7 add_convert_fusion.2.refs_2_
  380.1 10.6 %unproject.1 = (bf16[1024,512]{1,0:T(8,128)(2,1)}, bf16[1024,1024]{1,0:T(8,128)(2,1)}, f32[64,128]{1,0:T(8,128)}) custom-call(bf16[8,1024,256]{2,1,0:T(8,128)(2,1)} %bitcast.80, f32[1024,256]{1,0:T(8,128)} %get-tuple-element.76.t_ref, f32[1024,384]{1,0:T(8,128)} %get-tuple-element.77.p_ref, bf16[8,144,1024]{2,1,0:T(8,128)(2,1)} %bitcast.78, ...), custom_call_target="tpu_custom_call" | custom-call | tf_op jit(solution)/shard_map/unproject/pallas_call | solution.py:692
  390.8 3.5 convolution_convert_fusion.4
  394.3 48.2 %exchange_8.1 = (bf16[1024,1024]{1,0:T(8,128)(2,1)}, bf16[16,8,16,256]{3,2,1,0:T(8,128)(2,1)}, bf16[8,32,512]{2,1,0:T(8,128)(2,1)}, f32[64,128]{1,0:T(8,128)}) custom-call(bf16[1024,1024]{1,0:T(8,128)(2,1)} %get-tuple-element.78.refs_0_, bf16[8,128,512]{2,1,0:T(8,128)(2,1)} %bitcast.88, bf16[256,512]{1,0:T(8,128)(2,1)} %add_convert_fusion.2.refs_2_, ...), custom_call_target="tpu_custom_call" | custom-call | tf_op jit(solution)/shard_map/exchange_8/pallas_call | solution.py:147
  442.4 2.1 reduce_sum.129.refs_0_
  444.5 1.6 reduce_sum.130.refs_1_
  449.4 34.0 %exchange_9.1 = (bf16[16,2048]{1,0:T(8,128)(2,1)}, bf16[256,2048]{1,0:T(8,128)(2,1)}, bf16[256,1024]{1,0:T(8,128)(2,1)}, f32[128,128]{1,0:T(8,128)}, bf16[256,10...) custom-call(bf16[8,16,256]{2,1,0:T(8,128)(2,1)} %reduce_sum.129.refs_0_, ...), custom_call_target="tpu_custom_call" | custom-call | tf_op jit(solution)/shard_map/exchange_9/pallas_call | solution.py:147
  483.5 7.0 %finish.1 = (bf16[128,1024]{1,0:T(8,128)(2,1)}, f32[128,1024]{1,0:T(8,128)}, f32[128,2048]{1,0:T(8,128)}, f32[128,1024]{1,0:T(8,128)}, f32[128,1024]{1,0:T(8,128...) custom-call(bf16[256,3072]{1,0:T(8,128)(2,1)} %get-tuple-element.89.gate_ref.up_ref, ...), custom_call_target="tpu_custom_call" | custom-call | tf_op jit(solution)/shard_map/finish/pallas_call | solution.py:559
  (76 shorter events, 17.6 us)
Async XLA Ops:
  0.6 194.7 %copy-start = (bf16[384,1024]{1,0:T(8,128)(2,1)S(1)}, bf16[384,1024]{1,0:T(8,128)(2,1)}, u32[]{:S(2)}) copy-start(bf16[384,1024]{1,0:T(8,128)(2,1)} %param.26) | copy-start | bytes 2359300
  104.9 25.5 %copy-start.12 = (bf16[256,1024]{1,0:T(8,128)(2,1)S(1)}, bf16[256,1024]{1,0:T(8,128)(2,1)}, u32[]{:S(2)}) copy-start(bf16[256,1024]{1,0:T(8,128)(2,1)} %param.20) | copy-start | bytes 1572868
  162.5 2.1 copy-start.5
  164.8 74.7 %copy-start.1 = (f32[128,1024]{1,0:T(8,128)}, f32[128,1024]{1,0:T(8,128)S(1)}, u32[]{:S(2)}) copy-start(f32[128,1024]{1,0:T(8,128)S(1)} %get-tuple-element.110.middle_ref) | copy-start | bytes 1572868
  191.2 4.1 copy-start.16
  196.9 1.9 copy-start.18
  196.9 1.9 copy-start.8
  198.8 3.0 copy-start.17
  205.0 31.0 %copy-start.3 = (bf16[1024,768]{1,0:T(8,128)(2,1)S(1)}, bf16[1024,768]{1,0:T(8,128)(2,1)}, u32[]{:S(2)}) copy-start(bf16[1024,768]{1,0:T(8,128)(2,1)} %convolution_convert_fusion.3) | copy-start | bytes 4718596
  236.0 2.4 copy-start.6
  238.4 1.1 copy-start.10
  238.7 36.5 %copy-start.2 = (f32[1024,256]{1,0:T(8,128)S(1)}, f32[1024,256]{1,0:T(8,128)}, u32[]{:S(2)}) copy-start(f32[1024,256]{1,0:T(8,128)} %get-tuple-element.65.o_ref) | copy-start | bytes 3145732
  275.2 3.3 copy-start.7
  280.0 39.5 %copy-start.11 = (bf16[8,8,16,384]{3,2,1,0:T(8,128)(2,1)S(1)}, bf16[8,8,16,384]{3,2,1,0:T(8,128)(2,1)}, u32[]{:S(2)}) copy-start(bf16[8,8,16,384]{3,2,1,0:T(8,128)(2,1)} %get-tuple-element.74) | copy-start | bytes 2359300
  280.0 40.3 %copy-start.19 = (bf16[1024,384]{0,1:T(8,128)(2,1)S(1)}, bf16[1024,384]{0,1:T(8,128)(2,1)}, u32[]{:S(2)}) copy-start(bf16[1024,384]{0,1:T(8,128)(2,1)} %copy-done.18) | copy-start | bytes 2359300
  322.9 55.4 %copy-start.4 = (bf16[256,1024]{1,0:T(8,128)(2,1)S(1)}, bf16[256,1024]{1,0:T(8,128)(2,1)}, u32[]{:S(2)}) copy-start(bf16[256,1024]{1,0:T(8,128)(2,1)} %convolution_convert_fusion.6.refs_2_) | copy-start | bytes 1572868
  380.1 10.6 %copy-start.15 = (bf16[1024,1024]{1,0:T(8,128)(2,1)S(1)}, bf16[1024,1024]{1,0:T(8,128)(2,1)}, u32[]{:S(2)}) copy-start(bf16[1024,1024]{1,0:T(8,128)(2,1)} %get-tuple-element.79) | copy-start | bytes 6291460
  394.3 53.2 %copy-start.9 = (bf16[1024,1024]{1,0:T(8,128)(2,1)S(1)}, bf16[1024,1024]{1,0:T(8,128)(2,1)}, u32[]{:S(2)}) copy-start(bf16[1024,1024]{1,0:T(8,128)(2,1)} %get-tuple-element.86) | copy-start | bytes 6291460
  442.4 6.4 %copy-start.13 = (bf16[8,48,512]{2,1,0:T(8,128)(2,1)S(1)}, bf16[8,48,512]{2,1,0:T(8,128)(2,1)}, u32[]{:S(2)}) copy-start(bf16[8,48,512]{2,1,0:T(8,128)(2,1)} %get-tuple-element.88) | copy-start | bytes 1179652
  483.5 7.0 %copy-start.14 = (f32[128,128]{1,0:T(8,128)S(1)}, f32[128,128]{1,0:T(8,128)}, u32[]{:S(2)}) copy-start(f32[128,128]{1,0:T(8,128)} %get-tuple-element.97) | copy-start | bytes 196612

commit v4 on v3

--- a/solution.py
+++ b/solution.py
@@ -76,12 +76,24 @@
         self.shift, self.src, self.dst, self.cond, self.needs = shift, src, dst, cond, needs
 
 
-def exchange(ops, collective_id, out_shapes, *arrays):
+class Work:
+    def __init__(self, inputs, outs, scratch, greets, body):
+        self.inputs, self.outs, self.scratch, self.greets, self.body = inputs, outs, scratch, greets, body
+
+
+def exchange(ops, collective_id, out_shapes, *arrays, work=None):
     n_in, n_out, n_ops = len(arrays), len(out_shapes), len(ops)
+    work = work or Work([], [], [], [], None)
+    n_more, n_made = len(work.inputs), len(work.outs)
 
     def kernel(*refs):
-        io = refs[: n_in + n_out]
-        send_sem, recv_sem = refs[n_in + n_out :]
+        refs = list(refs)
+        ins, more = refs[:n_in], refs[n_in : n_in + n_more]
+        refs = refs[n_in + n_more :]
+        outs, made = refs[:n_out], refs[n_out : n_out + n_made]
+        send_sem, recv_sem = refs[n_out + n_made : n_out + n_made + 2]
+        scratch = refs[n_out + n_made + 2 :]
+        io = ins + outs
         me = here()
 
         def when(cond, act):
@@ -103,6 +115,10 @@
 
             when(op.cond and op.cond(source), greet)
             count = count + (1 if op.cond is None else jnp.where(op.cond(me), 1, 0))
+        for shift in work.greets:
+            source = shift.back(me)
+            pl.semaphore_signal(barrier, inc=1, device_id=source.device(), device_id_type=MESH)
+            count = count + 1
         pl.semaphore_wait(barrier, count)
 
         def copy(t, sender):
@@ -139,23 +155,33 @@
             for need in op.needs:
                 arrive(need)
             when(op.cond and op.cond(me), lambda t=t: copy(t, me).start())
+        if work.body is not None:
+            work.body(me, more, outs, made, scratch)
         for t, op in enumerate(ops):
             arrive(t)
             if op.shift is not None:
                 when(op.cond and op.cond(me), lambda t=t: copy(t, me).wait_send())
 
+    anywhere = pl.BlockSpec(memory_space=pl.ANY)
     return pl.pallas_call(
         kernel,
-        out_shape=tuple(jax.ShapeDtypeStruct(s, d) for s, d in out_shapes),
-        in_specs=[pl.BlockSpec(memory_space=pl.ANY)] * n_in,
-        out_specs=tuple([pl.BlockSpec(memory_space=pl.ANY)] * n_out),
+        out_shape=tuple(jax.ShapeDtypeStruct(s, d) for s, d in out_shapes)
+        + tuple(jax.ShapeDtypeStruct(s, d) for s, d in work.outs),
+        in_specs=[anywhere] * n_in + [pl.BlockSpec(memory_space=m) for _, m in work.inputs],
+        out_specs=tuple([anywhere] * n_out + [pl.BlockSpec(memory_space=pltpu.VMEM)] * n_made),
         scratch_shapes=[
             pltpu.SemaphoreType.DMA((n_ops,)),
             pltpu.SemaphoreType.DMA((n_ops,)),
-        ],
-        compiler_params=pltpu.CompilerParams(collective_id=collective_id, has_side_effects=True),
+        ]
+        + work.scratch,
+        compiler_params=pltpu.CompilerParams(
+            collective_id=collective_id,
+            has_side_effects=True,
+            vmem_limit_bytes=VMEM if work.body else None,
+        ),
         name="exchange_%d" % collective_id,
-    )(*arrays)
+    )(*arrays, *(a for a, _ in work.inputs))
+
 
 def home(at):
     return at.c == at.d
@@ -397,111 +423,139 @@
     )(order, own, q, kv)
 
 
-def backward_kernel(
-    order, own, q_ref, g_ref, o_ref, l_ref, kv_ref, dq_ref, dkv_ref,
-    keys, keys_t, vals, dk, dv, dq_t, q_t, g_t,
-):
-    step = pl.program_id(0)
-    n_runs = order.shape[0]
-
-    @pl.when(step == 0)
-    def _():
-        dk[...] = jnp.zeros_like(dk)
-        dv[...] = jnp.zeros_like(dv)
-
-        def place(r, _):
-            src = pl.ds(pl.multiple_of(r // 8 * KV_ROWS + r % 8 * RUN, 16), RUN)
-            dst = pl.ds(pl.multiple_of(order[r] * RUN, RUN), RUN)
-            k = kv_ref[src, :HEAD]
-            keys[dst, :] = k
-            keys_t[:, dst] = k.T
-            vals[dst, :] = kv_ref[src, HEAD:]
+def attention_backward(order, own, q, g, o, log, kv):
+    tokens = q.shape[0]
+    runs = tokens // RUN
+    half = tokens // 2
+    chips = order.shape[0] // runs
+
+    def body(me, more, outs, made, scratch):
+        order_ref, own_ref, q_ref, g_ref, o_ref, l_ref, kv_ref = more
+        (landed,) = outs[:1]
+        (dq_ref,) = made
+        q2, g2, q_t, g_t, rows, dq_t, dk, dv, keys_t, send, send_sem, recv_sem, own_sem = scratch
+        mine = me.chip()
+
+        def prepare(i, _):
+            at = pl.ds(pl.multiple_of(i * RUN, RUN), RUN)
+            cut = pl.ds(pl.multiple_of(i % 2 * 2 * RUN, 2 * RUN), 2 * RUN)
+            query, grad = stacked(q_ref.at[at]), stacked(g_ref.at[at])
+            j = i // 2
+            q2[j, cut, :] = query
+            g2[j, cut, :] = grad
+            q_t[j, :, cut] = query.T
+            g_t[j, :, cut] = grad.T
+            rows[j, 0:1, cut] = jnp.sum((grad.astype(F32) * stacked(o_ref.at[at])).T, axis=0, keepdims=True)
+            rows[j, 1:2, cut] = stacked(l_ref.at[at]).T[:1]
             return 0
 
-        lax.fori_loop(0, n_runs, place, 0, unroll=8)
-
-    run = own[step]
-    query = stacked(q_ref)
-    grad = stacked(g_ref)
-    q_t[...] = query.T
-    g_t[...] = grad.T
-    delta = jnp.sum((grad.astype(F32) * stacked(o_ref)).T, axis=0, keepdims=True)
-    log = stacked(l_ref).T[:1]
-    dq_t[...] = jnp.zeros_like(dq_t)
-
-    def visit(j, masked):
-        at = pl.ds(pl.multiple_of(j * CHUNK, CHUNK), CHUNK)
-        s = mm(keys[at, :], q_t[...])
-        p = jnp.exp2(s * (SCALE * LOG2E) - log)
-        if masked:
-            row = lax.broadcasted_iota(jnp.int32, p.shape, 1) % RUN + run * RUN
-            col = lax.broadcasted_iota(jnp.int32, p.shape, 0) + j * CHUNK
-            p = jnp.where(col <= row, p, 0.0)
-        dp = mm(vals[at, :], g_t[...])
-        ds = (p * (dp - delta)).astype(BF)
-        dv[at, :] += mm(p.astype(BF), grad)
-        dk[at, :] += mm(ds, query)
-        dq_t[...] += mm(keys_t[:, at], ds)
-
-    last = run // (CHUNK // RUN)
-
-    def plain(j, _):
-        for u in range(UNROLL):
-            visit(j * UNROLL + u, False)
-        return 0
-
-    def single(j, _):
-        visit(j, False)
-        return 0
-
-    lax.fori_loop(0, last // UNROLL, plain, 0)
-    lax.fori_loop(last // UNROLL * UNROLL, last, single, 0)
-    visit(last, True)
-    out = dq_t[...].T * SCALE
-    dq_ref[:, :HEAD] = out[:RUN]
-    dq_ref[:, HEAD:] = out[RUN:]
-
-    @pl.when(step == pl.num_programs(0) - 1)
-    def _():
-        def give(r, _):
-            dst = pl.ds(pl.multiple_of(r * RUN, RUN), RUN)
-            src = pl.ds(pl.multiple_of(order[r] * RUN, RUN), RUN)
-            dkv_ref[dst, :HEAD] = (dk[src, :] * SCALE).astype(BF)
-            dkv_ref[dst, HEAD:] = dv[src, :].astype(BF)
+        lax.fori_loop(0, runs, prepare, 0)
+        dq_t[...] = jnp.zeros_like(dq_t)
+
+        def per_run(j, value):
+            return jnp.concatenate(
+                [jnp.broadcast_to(value(own_ref[j * 2 + u]), (1, 2 * RUN)) for u in (0, 1)], axis=1
+            )
+
+        def remote(step, chip, slot):
+            return pltpu.make_async_remote_copy(
+                src_ref=send.at[step],
+                dst_ref=landed.at[slot],
+                send_sem=send_sem.at[step],
+                recv_sem=recv_sem.at[slot],
+                device_id=(chip * 2 + me.c, me.d, me.z),
+                device_id_type=MESH,
+            )
+
+        def one_chip(step, chip, diagonal):
+            base = chip * KV_ROWS
+            for r in range(runs):
+                cut = slice(r * RUN, (r + 1) * RUN)
+                keys_t[:, cut] = kv_ref[pl.ds(pl.multiple_of(base + r * RUN, 16), RUN), :HEAD].T
+            dk[...] = jnp.zeros_like(dk)
+            dv[...] = jnp.zeros_like(dv)
+
+            def visit(j, part):
+                at = pl.ds(pl.multiple_of(base + part * half, 16), half)
+                cut = slice(part * half, (part + 1) * half)
+                s = mm(kv_ref[at, :HEAD], q_t[j]) * (SCALE * LOG2E)
+                log = rows[j, 1:2, :]
+                pieces = []
+                for r in range(runs // 2):
+                    run = order_ref[chip * runs + part * (runs // 2) + r]
+                    piece = s[r * RUN : (r + 1) * RUN]
+                    if diagonal:
+                        ahead = lax.broadcasted_iota(jnp.int32, piece.shape, 0) - (
+                            lax.broadcasted_iota(jnp.int32, piece.shape, 1) % RUN
+                        )
+                        seen = ahead <= per_run(j, lambda mine: (mine - run) * RUN)
+                        pieces.append(jnp.where(seen, jnp.exp2(piece - log), 0.0))
+                    else:
+                        hide = per_run(j, lambda mine: jnp.where(run <= mine, 0.0, 1e30))
+                        pieces.append(jnp.exp2(piece - (log + hide)))
+                p = jnp.concatenate(pieces, axis=0)
+                dp = mm(kv_ref[at, HEAD:], g_t[j])
+                ds = (p * (dp - rows[j, 0:1, :])).astype(BF)
+                dv[cut, :] += mm(p.astype(BF), g2[j])
+                dk[cut, :] += mm(ds, q2[j])
+                dq_t[j] += mm(keys_t[:, cut], ds)
+
+            def two_runs(j, _):
+                visit(j, 0)
+                visit(j, 1)
+                return 0
+
+            lax.fori_loop(0, runs // 2, two_runs, 0)
+            send[step, :, :HEAD] = (dk[...] * SCALE).astype(BF)
+            send[step, :, HEAD:] = dv[...].astype(BF)
+
+        def other_chip(step, _):
+            chip = (mine + 1 + step) % chips
+            one_chip(step, chip, False)
+            remote(step, chip, mine).start()
             return 0
 
-        lax.fori_loop(0, n_runs, give, 0, unroll=8)
-
-
-def attention_backward(order, own, q, g, o, log, kv):
-    length = order.shape[0] * RUN
-    tokens = q.shape[0]
-    block = pl.BlockSpec((RUN, 2 * HEAD), lambda i, *_: (i, 0))
-    all_rows = pl.BlockSpec((length, 2 * HEAD), lambda i, *_: (0, 0))
-    return pl.pallas_call(
-        backward_kernel,
-        grid_spec=pltpu.PrefetchScalarGridSpec(
-            num_scalar_prefetch=2,
-            grid=(tokens // RUN,),
-            in_specs=[block, block, block, block, pl.BlockSpec(kv.shape, lambda i, *_: (0, 0))],
-            out_specs=[block, all_rows],
-            scratch_shapes=[
-                pltpu.VMEM((length, HEAD), BF),
-                pltpu.VMEM((HEAD, length), BF),
-                pltpu.VMEM((length, HEAD), BF),
-                pltpu.VMEM((length, HEAD), F32),
-                pltpu.VMEM((length, HEAD), F32),
-                pltpu.VMEM((HEAD, 2 * RUN), F32),
-                pltpu.VMEM((HEAD, 2 * RUN), BF),
-                pltpu.VMEM((HEAD, 2 * RUN), BF),
-            ],
-        ),
-        out_shape=(jax.ShapeDtypeStruct(q.shape, F32), jax.ShapeDtypeStruct((length, 2 * HEAD), BF)),
-        compiler_params=pltpu.CompilerParams(
-            dimension_semantics=("arbitrary",), vmem_limit_bytes=VMEM
-        ),
-        name="attention_backward",
-    )(order, own, q, g, o, log, kv)
+        lax.fori_loop(0, chips - 1, other_chip, 0)
+        one_chip(chips - 1, mine, True)
+        keep = pltpu.make_async_copy(send.at[chips - 1], landed.at[mine], own_sem)
+        keep.start()
+
+        def give(i, _):
+            at = pl.ds(pl.multiple_of(i * RUN, RUN), RUN)
+            cut = pl.ds(pl.multiple_of(i % 2 * 2 * RUN, 2 * RUN), 2 * RUN)
+            out = dq_t[i // 2, :, cut].T * SCALE
+            dq_ref[at, :HEAD] = out[:RUN]
+            dq_ref[at, HEAD:] = out[RUN:]
+            return 0
+
+        lax.fori_loop(0, runs, give, 0)
+        keep.wait()
+        for step in range(chips - 1):
+            remote(step, (mine + 1 + step) % chips, mine).wait_send()
+            remote(step, (mine + 1 + step) % chips, (mine + 1 + step) % chips).wait_recv()
+
+    smem, vmem = pltpu.SMEM, pltpu.VMEM
+    return Work(
+        inputs=[(order, smem), (own, smem), (q, vmem), (g, vmem), (o, vmem), (log, vmem), (kv, vmem)],
+        outs=[(q.shape, F32)],
+        scratch=[
+            pltpu.VMEM((runs // 2, 4 * RUN, HEAD), BF),
+            pltpu.VMEM((runs // 2, 4 * RUN, HEAD), BF),
+            pltpu.VMEM((runs // 2, HEAD, 4 * RUN), BF),
+            pltpu.VMEM((runs // 2, HEAD, 4 * RUN), BF),
+            pltpu.VMEM((runs // 2, 8, 4 * RUN), F32),
+            pltpu.VMEM((runs // 2, HEAD, 4 * RUN), F32),
+            pltpu.VMEM((tokens, HEAD), F32),
+            pltpu.VMEM((tokens, HEAD), F32),
+            pltpu.VMEM((HEAD, tokens), BF),
+            pltpu.VMEM((chips, tokens, 2 * HEAD), BF),
+            pltpu.SemaphoreType.DMA((chips,)),
+            pltpu.SemaphoreType.DMA((chips,)),
+            pltpu.SemaphoreType.DMA(()),
+        ],
+        greets=Plan().chip_shifts(),
+        body=body,
+    )
 
 
 def inverse_rms(value):
@@ -875,38 +929,35 @@
     down_part = dot(inner, down_weight).astype(BF)
     gate_up_sum = jnp.sum(gate_up_pieces.astype(F32), axis=0).astype(BF)
     down_sum = jnp.sum(down_pieces.astype(F32), axis=0).astype(BF)
-    query_turn, kv_part = attention_backward(
-        order, own, queries, mixed_grad, attention, log_total, kv_all
-    )
 
     plan = Plan()
-    plan.scatter_chips(rows(group)(0), rows(group)(4))
     pair = 2 * tokens
     for k in (1, 3, 2):
         plan.add(
             Shift(z=k),
-            block(1, lambda at, k=k: (at.z + k) % 4, pair),
-            block(5, lambda at: at.z, pair),
+            block(0, lambda at, k=k: (at.z + k) % 4, pair),
+            block(4, lambda at: at.z, pair),
         )
-    plan.add(None, block(1, lambda at: at.z, pair), block(5, lambda at: at.z, pair))
-    plan.add(Shift(c=1), theirs(2, width // 2), full(6))
+    plan.add(None, block(0, lambda at: at.z, pair), block(4, lambda at: at.z, pair))
+    plan.add(Shift(c=1), theirs(1, width // 2), full(5))
     plan.scatter_group(
-        lambda io, n: io[3].at[n],
-        lambda io, n: io[7].at[:, pl.ds(pl.multiple_of(n * ff, ff), ff)],
+        lambda io, n: io[2].at[n],
+        lambda io, n: io[6].at[:, pl.ds(pl.multiple_of(n * ff, ff), ff)],
     )
     n_rows = output_wgrad.shape[0]
-    kv_parts, down_parts, output_got, gate_up_own = exchange(
+    kv_parts, down_parts, output_got, gate_up_own, query_turn = exchange(
         plan, 7,
         (
-            ((8 * group, 256), BF), ((group, width), BF), ((n_rows, width // 2), BF),
+            ((8, group, 256), BF), ((group, width), BF), ((n_rows, width // 2), BF),
             ((16, 8 * ff), BF),
         ),
-        kv_part, down_part, output_wgrad, gate_up_sum,
+        down_part, output_wgrad, gate_up_sum,
+        work=attention_backward(order, own, queries, mixed_grad, attention, log_total, kv_all),
     )
     down_pair = summed(down_parts, 4).astype(BF)
     output_half = my_half(output_wgrad, output_got)
     qkv_grad, norm_one_part, gain_parts = unproject(
-        kv_parts.reshape(8, group, 2 * HEAD), query_turn, pre, x_all, w_qkv, head_scale, cos, sin,
+        kv_parts, query_turn, pre, x_all, w_qkv, head_scale, cos, sin,
         mlp_gain_part.reshape(1, width),
     )
     qkv_wgrad = dot_t(norm_one, qkv_grad).astype(BF).reshape(8, part, 512)

time: 493 us -> 475 us (0.963)
  Pallas kernels: 426 us -> 406 us
    pallas_call x1 -> x0, Pallas kernels: 39.5 us -> none  [attention_backward(): pl.pallas_call(backward_kernel, grid_spec=pltpu.PrefetchScalarGridSpec(nu...]
    pallas_call x9, Pallas kernels: 335 us -> 352 us  [exchange(): pl.pallas_call(kernel, out_shape=tuple((jax.ShapeDtypeStruct(s, d) for s,...]
where the time goes in v4:
time: 475 us; the launch traced here: 474 us
  Pallas kernels  406 us (85%)
  matrix products  28 us (6%)
  other arithmetic  27.7 us (6%)
  local copies, waits for them, and re-layouts  9.35 us (2%)
    pallas_call x9, Pallas kernels, exchange(): pl.pallas_call(kernel, out_shape=tuple((jax.ShapeDtypeStruct(s, d) for s,...  352 us
    pallas_call x1, Pallas kernels, attention_forward(): pl.pallas_call(forward_kernel, grid_spec=pltpu.PrefetchScalarGridSpec(num...  27.1 us
    dot_general x4, matrix products, dot_t(): lax.dot_general(a, b, (((0,), (0,)), ((), ())), preferred_element_type=F32)  11.7 us
    pallas_call x1, Pallas kernels, unproject(): pl.pallas_call(unproject_kernel, grid=(8,), in_specs=[pl.BlockSpec((8, RU...  10.6 us
    dot_general x3, matrix products, dot(): return jnp.dot(a, b, preferred_element_type=F32)  9.93 us

profile of v4, /device:TPU:1, one launch (start us, length us, event | category | flops | bytes accessed | tf_op | source)
XLA Modules:
  0.0 474.3 jit_solution(5018696689608744499)
XLA Ops:
  5.4 1.7 concatenate.12.refs_0_
  7.1 35.8 %exchange_1.1 = (bf16[1152,1024]{1,0:T(8,128)(2,1)}, f32[64,128]{1,0:T(8,128)}, bf16[1024,512]{1,0:T(8,128)(2,1)}) custom-call(bf16[144,1024]{1,0:T(8,128)(2,1)} %concatenate.12.refs_0_, f32[8,128]{1,0:T(8,128)} %concatenate.13.refs_1_, bf16[128,2048]{1,0:T(8,128)(2,1)} %refs_2_.2, bf16[128,1024]{1,0:T(8,128)(2,1)} %refs_3_.2, bf16[128,1024]{1,0:T(8,128)(2,1)} %refs_4_.1), custom_call_target="tpu_custom_call" | custom-call | tf_op jit(solution)/shard_map/exchange_1/pallas_call | solution.py:166
  48.1 3.0 fusion.1
  51.1 9.1 %project.1 = (bf16[1024,1024]{1,0:T(8,128)(2,1)}, f32[1024,384]{1,0:T(8,128)}, bf16[1024,256]{1,0:T(8,128)(2,1)}, bf16[1040,256]{1,0:T(8,128)(2,1)}) custom-call(bf16[8,144,1024]{2,1,0:T(8,128)(2,1)} %bitcast.76, bf16[1024,512]{1,0:T(8,128)(2,1)} %get-tuple-element.59.w_ref, f32[1,1024]{1,0:T(1,128)} %get-tuple-element.113.scale_ref, ...), custom_call_target="tpu_custom_call" | custom-call | tf_op jit(solution)/shard_map/project/pallas_call | solution.py:675
  60.2 43.4 %exchange_2.1 = (bf16[8320,256]{1,0:T(8,128)(2,1)}, bf16[1024,1024]{1,0:T(8,128)(2,1)}, bf16[1024,768]{1,0:T(8,128)(2,1)}) custom-call(bf16[1040,256]{1,0:T(8,128)(2,1)} %get-tuple-element.61.refs_0_, bf16[128,1024]{1,0:T(8,128)(2,1)} %bitcast.87, bf16[128,3072]{1,0:T(8,128)(2,1)} %refs_2_.3, bf16[128,3072]{1,0:T(8,128)(2,1)} %refs_3_.3), custom_call_target="tpu_custom_call" | custom-call | tf_op jit(solution)/shard_map/exchange_2/pallas_call | solution.py:166
  104.9 27.1 %attention_forward.1 = (f32[1024,256]{1,0:T(8,128)}, f32[1024,256]{1,0:T(8,128)}) custom-call(s32[64]{0:T(128)} %reshape.159.order.refs_3_, s32[8]{0:T(128)} %convert_element_type.129.own.refs_4_, bf16[1024,256]{1,0:T(8,128)(2,1)} %get-tuple-element.63.q_ref.refs_5_, bf16[8320,256]{1,0:T(8,128)(2,1)} %get-tuple-element.62.kv_ref.refs_9_), custom_call_target="tpu_custom_call" | custom-call | tf_op jit(solution)/shard_map/attention_forward/pallas_call | solution.py:405
  132.0 3.3 convolution_convert_fusion.1.refs_0_
  135.2 28.9 %exchange_3.1 = bf16[1024,1024]{1,0:T(8,128)(2,1)} custom-call(bf16[1024,1024]{1,0:T(8,128)(2,1)} %convolution_convert_fusion.1.refs_0_), custom_call_target="tpu_custom_call" | custom-call | tf_op jit(solution)/shard_map/exchange_3/pallas_call | solution.py:166
  164.2 2.1 convert_reduce_fusion.1
  167.2 25.0 %exchange_4.1 = bf16[1024,1024]{1,0:T(8,128)(2,1)} custom-call(bf16[128,1024]{1,0:T(8,128)(2,1)} %multiply_convert_fusion.3.refs_0_), custom_call_target="tpu_custom_call" | custom-call | tf_op jit(solution)/shard_map/exchange_4/pallas_call | solution.py:166
  192.2 4.1 fusion.11
  196.3 1.6 multiply_convert_fusion.1
  197.9 2.0 convolution_convert_fusion.5.refs_2_
  199.9 3.0 convolution_convert_fusion.3
  202.9 3.2 convolution_convert_fusion.2.refs_0_
  206.1 28.8 %exchange_5.1 = (bf16[1024,1024]{1,0:T(8,128)(2,1)}, bf16[8,128,384]{2,1,0:T(8,128)(2,1)}, bf16[384,512]{1,0:T(8,128)(2,1)}) custom-call(bf16[1024,1024]{1,0:T(8,128)(2,1)} %convolution_convert_fusion.2.refs_0_, bf16[8,128,768]{2,1,0:T(8,128)(2,1)} %bitcast.79, bf16[384,1024]{1,0:T(8,128)(2,1)} %convolution_convert_fusion.5.refs_2_), custom_call_target="tpu_custom_call" | custom-call | tf_op jit(solution)/shard_map/exchange_5/pallas_call | solution.py:166
  235.0 2.1 add_convert_fusion.1.refs_2_
  237.1 2.2 add_convert_fusion.refs_1_
  241.5 34.2 %exchange_6.1 = (bf16[1024,1024]{1,0:T(8,128)(2,1)}, bf16[8,8,16,384]{3,2,1,0:T(8,128)(2,1)}, bf16[8,48,512]{2,1,0:T(8,128)(2,1)}) custom-call(bf16[128,1024]{1,0:T(8,128)(2,1)} %get-tuple-element.105.refs_0_, bf16[8,128,384]{2,1,0:T(8,128)(2,1)} %add_convert_fusion.refs_1_, bf16[384,512]{1,0:T(8,128)(2,1)} %add_convert_fusion.1.refs_2_), custom_call_target="tpu_custom_call" | custom-call | tf_op jit(solution)/shard_map/exchange_6/pallas_call | solution.py:166
  275.8 1.9 reduce_sum.127.refs_2_
  277.7 1.7 reduce_sum.133.refs_5_
  279.4 3.3 convolution_convert_fusion.7.refs_1_
  284.2 2.6 convolution_convert_fusion.refs_0_
  286.8 77.8 %exchange_7.1 = (bf16[8,1024,256]{2,1,0:T(8,128)(2,1)}, bf16[1024,1024]{1,0:T(8,128)(2,1)}, bf16[256,512]{1,0:T(8,128)(2,1)}, bf16[16,3072]{1,0:T(8,128)(2,1)}, f32[1024,256]{1,0:T(8,128)}) custom-call(bf16[1024,1024]{1,0:T(8,128)(2,1)} %convolution_convert_fusion.refs_0_, bf16[256,1024]{1,0:T(8,128)(2,1)} %convolution_convert_fusion.7.refs_1_, ...), custom_call_target="tpu_custom_call" | custom-call | tf_op jit(solution)/shard_map/exchange_7/pallas_call | solution.py:166
  364.6 1.7 add_convert_fusion.2.refs_2_
  366.3 10.6 %unproject.1 = (bf16[1024,512]{1,0:T(8,128)(2,1)}, bf16[1024,1024]{1,0:T(8,128)(2,1)}, f32[64,128]{1,0:T(8,128)}) custom-call(bf16[8,1024,256]{2,1,0:T(8,128)(2,1)} %get-tuple-element.73.kv_ref, f32[1024,256]{1,0:T(8,128)} %get-tuple-element.74.t_ref, f32[1024,384]{1,0:T(8,128)} %get-tuple-element.75.p_ref, bf16[8,144,1024]{2,1,0:T(8,128)(2,1)} %bitcast.77, ...), custom_call_target="tpu_custom_call" | custom-call | tf_op jit(solution)/shard_map/unproject/pallas_call | solution.py:746
  377.0 3.5 convolution_convert_fusion.4
  380.4 45.4 %exchange_8.1 = (bf16[1024,1024]{1,0:T(8,128)(2,1)}, bf16[16,8,16,256]{3,2,1,0:T(8,128)(2,1)}, bf16[8,32,512]{2,1,0:T(8,128)(2,1)}, f32[64,128]{1,0:T(8,128)}) custom-call(bf16[1024,1024]{1,0:T(8,128)(2,1)} %get-tuple-element.76.refs_0_, bf16[8,128,512]{2,1,0:T(8,128)(2,1)} %bitcast.86, bf16[256,512]{1,0:T(8,128)(2,1)} %add_convert_fusion.2.refs_2_, ...), custom_call_target="tpu_custom_call" | custom-call | tf_op jit(solution)/shard_map/exchange_8/pallas_call | solution.py:166
  425.9 2.0 reduce_sum.129.refs_0_
  429.3 1.6 reduce_sum.130.refs_1_
  432.2 32.4 %exchange_9.1 = (bf16[16,2048]{1,0:T(8,128)(2,1)}, bf16[256,2048]{1,0:T(8,128)(2,1)}, bf16[256,1024]{1,0:T(8,128)(2,1)}, f32[128,128]{1,0:T(8,128)}, bf16[256,10...) custom-call(bf16[8,16,256]{2,1,0:T(8,128)(2,1)} %reduce_sum.129.refs_0_, ...), custom_call_target="tpu_custom_call" | custom-call | tf_op jit(solution)/shard_map/exchange_9/pallas_call | solution.py:166
  467.2 7.0 %finish.1 = (bf16[128,1024]{1,0:T(8,128)(2,1)}, f32[128,1024]{1,0:T(8,128)}, f32[128,2048]{1,0:T(8,128)}, f32[128,1024]{1,0:T(8,128)}, f32[128,1024]{1,0:T(8,128...) custom-call(bf16[256,3072]{1,0:T(8,128)(2,1)} %get-tuple-element.87.gate_ref.up_ref, ...), custom_call_target="tpu_custom_call" | custom-call | tf_op jit(solution)/shard_map/finish/pallas_call | solution.py:613
  (69 shorter events, 18.5 us)
Async XLA Ops:
  0.6 195.7 %copy-start = (bf16[384,1024]{1,0:T(8,128)(2,1)S(1)}, bf16[384,1024]{1,0:T(8,128)(2,1)}, u32[]{:S(2)}) copy-start(bf16[384,1024]{1,0:T(8,128)(2,1)} %param.26) | copy-start | bytes 2359300
  104.9 27.1 %copy-start.11 = (bf16[256,1024]{1,0:T(8,128)(2,1)S(1)}, bf16[256,1024]{1,0:T(8,128)(2,1)}, u32[]{:S(2)}) copy-start(bf16[256,1024]{1,0:T(8,128)(2,1)} %param.20) | copy-start | bytes 1572868
  164.1 2.1 copy-start.5
  166.4 74.0 %copy-start.1 = (f32[128,1024]{1,0:T(8,128)}, f32[128,1024]{1,0:T(8,128)S(1)}, u32[]{:S(2)}) copy-start(f32[128,1024]{1,0:T(8,128)S(1)} %get-tuple-element.108.middle_ref) | copy-start | bytes 1572868
  192.2 4.1 copy-start.13
  197.9 2.0 copy-start.15
  197.9 2.0 copy-start.8
  199.9 3.0 copy-start.14
  206.1 31.0 %copy-start.3 = (bf16[1024,768]{1,0:T(8,128)(2,1)S(1)}, bf16[1024,768]{1,0:T(8,128)(2,1)}, u32[]{:S(2)}) copy-start(bf16[1024,768]{1,0:T(8,128)(2,1)} %convolution_convert_fusion.3) | copy-start | bytes 4718596
  235.0 4.4 copy-start.6
  239.3 1.1 copy-start.10
  240.4 38.9 %copy-start.2 = (f32[1024,256]{1,0:T(8,128)S(1)}, f32[1024,256]{1,0:T(8,128)}, u32[]{:S(2)}) copy-start(f32[1024,256]{1,0:T(8,128)} %get-tuple-element.64.refs_7_) | copy-start | bytes 3145732
  279.4 3.3 copy-start.7
  282.6 1.5 copy-start.16
  286.8 77.8 %copy-start.4 = (bf16[256,1024]{1,0:T(8,128)(2,1)S(1)}, bf16[256,1024]{1,0:T(8,128)(2,1)}, u32[]{:S(2)}) copy-start(bf16[256,1024]{1,0:T(8,128)(2,1)} %convolution_convert_fusion.7.refs_1_) | copy-start | bytes 1572868
  366.3 10.6 %copy-start.12 = (bf16[1024,1024]{1,0:T(8,128)(2,1)S(1)}, bf16[1024,1024]{1,0:T(8,128)(2,1)}, u32[]{:S(2)}) copy-start(bf16[1024,1024]{1,0:T(8,128)(2,1)} %get-tuple-element.77) | copy-start | bytes 6291460
  380.4 50.4 %copy-start.9 = (bf16[1024,1024]{1,0:T(8,128)(2,1)S(1)}, bf16[1024,1024]{1,0:T(8,128)(2,1)}, u32[]{:S(2)}) copy-start(bf16[1024,1024]{1,0:T(8,128)(2,1)} %get-tuple-element.84) | copy-start | bytes 6291460

commit v5 on v4

--- a/solution.py
+++ b/solution.py
@@ -14,6 +14,7 @@
 CHUNK = 512
 VMEM = 60 * 2**20
 UNROLL = 4
+SLOTS = 2
 TAG = 16
 X_ROWS = RUN + TAG
 KV_ROWS = 8 * RUN + TAG
@@ -72,8 +73,9 @@
 
 
 class Op:
-    def __init__(self, shift, src, dst, cond=None, needs=()):
+    def __init__(self, shift, src, dst, cond=None, needs=(), stage=0):
         self.shift, self.src, self.dst, self.cond, self.needs = shift, src, dst, cond, needs
+        self.stage = stage
 
 
 class Work:
@@ -93,7 +95,7 @@
         outs, made = refs[:n_out], refs[n_out : n_out + n_made]
         send_sem, recv_sem = refs[n_out + n_made : n_out + n_made + 2]
         scratch = refs[n_out + n_made + 2 :]
-        io = ins + outs
+        io = ins + outs + made + scratch
         me = here()
 
         def when(cond, act):
@@ -123,8 +125,6 @@
 
         def copy(t, sender):
             op = ops[t]
-            if op.shift is None:
-                return pltpu.make_async_copy(op.src(io, me), op.dst(io, me), send_sem.at[t])
             return pltpu.make_async_remote_copy(
                 src_ref=op.src(io, sender),
                 dst_ref=op.dst(io, sender),
@@ -134,33 +134,73 @@
                 device_id_type=MESH,
             )
 
-        arrived = set()
-
-        def arrive(t):
-            if t in arrived:
-                return
-            arrived.add(t)
-            op = ops[t]
-            source = me if op.shift is None else op.shift.back(me)
-
-            def wait():
+        local = [t for t in range(n_ops) if ops[t].shift is None]
+        views = [ops[t].src(io, me) for t in local]
+
+        def run(*buffers):
+            held = dict(zip(local, buffers))
+
+            def fetch(t):
+                return pltpu.make_async_copy(ops[t].src(io, me), held[t], send_sem.at[t])
+
+            def store(t):
+                return pltpu.make_async_copy(held[t], ops[t].dst(io, me), recv_sem.at[t])
+
+            arrived, fetched = set(), set()
+
+            def pass_on(t):
+                if t in fetched:
+                    return
+                fetched.add(t)
+
+                def act():
+                    fetch(t).wait()
+                    store(t).start()
+
+                when(ops[t].cond and ops[t].cond(me), act)
+
+            def arrive(t):
+                if t in arrived:
+                    return
+                arrived.add(t)
+                op = ops[t]
                 if op.shift is None:
-                    copy(t, me).wait()
+                    pass_on(t)
+                    when(op.cond and op.cond(me), lambda: store(t).wait())
                 else:
-                    copy(t, source).wait_recv()
-
-            when(op.cond and op.cond(source), wait)
-
-        for t, op in enumerate(ops):
-            for need in op.needs:
-                arrive(need)
-            when(op.cond and op.cond(me), lambda t=t: copy(t, me).start())
-        if work.body is not None:
-            work.body(me, more, outs, made, scratch)
-        for t, op in enumerate(ops):
-            arrive(t)
-            if op.shift is not None:
-                when(op.cond and op.cond(me), lambda t=t: copy(t, me).wait_send())
+                    source = op.shift.back(me)
+                    when(op.cond and op.cond(source), lambda: copy(t, source).wait_recv())
+
+            def start(t):
+                if ops[t].shift is None:
+                    fetch(t).start()
+                else:
+                    copy(t, me).start()
+
+            def begin(stage):
+                for t, op in enumerate(ops):
+                    if op.stage != stage:
+                        continue
+                    if op.needs:
+                        for early in local:
+                            if early < t and ops[early].stage <= stage:
+                                pass_on(early)
+                    for need in op.needs:
+                        arrive(need)
+                    when(op.cond and op.cond(me), lambda t=t: start(t))
+                for t in local:
+                    if ops[t].stage == stage:
+                        pass_on(t)
+
+            begin(0)
+            if work.body is not None:
+                work.body(me, more, outs, made, scratch, begin, arrive)
+            for t, op in enumerate(ops):
+                arrive(t)
+                if op.shift is not None:
+                    when(op.cond and op.cond(me), lambda t=t: copy(t, me).wait_send())
+
+        pl.run_scoped(run, *(pltpu.VMEM(v.shape, v.dtype) for v in views))
 
     anywhere = pl.BlockSpec(memory_space=pl.ANY)
     return pl.pallas_call(
@@ -304,14 +344,17 @@
         )
         return ids
 
-    def scatter_chips(self, src, dst):
+    def scatter_chips(self, src, dst, stage=0):
         for shift in self.chip_shifts():
             self.add(
                 shift,
                 lambda io, at, s=shift: src(io, s.to(at).chip()),
                 lambda io, at: dst(io, at.chip()),
+                stage=stage,
             )
-        self.add(None, lambda io, at: src(io, at.chip()), lambda io, at: dst(io, at.chip()))
+        self.add(
+            None, lambda io, at: src(io, at.chip()), lambda io, at: dst(io, at.chip()), stage=stage
+        )
 
     def gather_chips(self, src, land, whole, needs=()):
         at_own = lambda io, at: land(io, at.chip(), at.c)
@@ -335,6 +378,7 @@
 
 NT = (((1,), (1,)), ((), ()))
 NN = (((1,), (0,)), ((), ()))
+TN = (((0,), (0,)), ((), ()))
 
 
 def mm(a, b, dims=NN):
@@ -429,7 +473,7 @@
     half = tokens // 2
     chips = order.shape[0] // runs
 
-    def body(me, more, outs, made, scratch):
+    def body(me, more, outs, made, scratch, begin, arrive):
         order_ref, own_ref, q_ref, g_ref, o_ref, l_ref, kv_ref = more
         (landed,) = outs[:1]
         (dq_ref,) = made
@@ -641,7 +685,7 @@
 
 def project_kernel(x_ref, w_ref, scale_ref, head_ref, cos_ref, sin_ref, tag_ref, n_ref, p_ref, q_ref, kv_ref):
     step = pl.program_id(0)
-    x = x_ref[0, :RUN, :].astype(F32)
+    x = jnp.concatenate([x_ref[n, :RUN, :] for n in range(SLOTS)], axis=0).astype(F32)
     low = (x * inverse_rms(x) * scale_ref[...]).astype(BF)
     n_ref[...] = low
     out = mm(low, w_ref[...])
@@ -653,7 +697,7 @@
         turned.append((v * cos_ref[...] + pltpu.roll(v, HEAD // 2, 1) * sin_ref[...]).astype(BF))
     q_ref[:, :HEAD] = turned[0]
     q_ref[:, HEAD:] = turned[1]
-    at = pl.ds(pl.multiple_of(step * RUN, RUN), RUN)
+    at = pl.ds(pl.multiple_of(step * SLOTS * RUN, SLOTS * RUN), SLOTS * RUN)
     kv_ref[at, :HEAD] = turned[2]
     kv_ref[at, HEAD:] = out[:, 3 * HEAD :].astype(BF)
 
@@ -670,13 +714,13 @@
         return pl.BlockSpec(a.shape, lambda i: (0,) * a.ndim)
 
     def moving(n):
-        return pl.BlockSpec((RUN, n), lambda i: (i, 0))
+        return pl.BlockSpec((SLOTS * RUN, n), lambda i: (i, 0))
 
     return pl.pallas_call(
         project_kernel,
-        grid=(8,),
+        grid=(8 // SLOTS,),
         in_specs=[
-            pl.BlockSpec((1, X_ROWS, width), lambda i: (i, 0, 0)),
+            pl.BlockSpec((SLOTS, X_ROWS, width), lambda i: (i, 0, 0)),
             fixed(w), fixed(scale), fixed(head_scale), moving(HEAD), moving(HEAD), fixed(tag),
         ],
         out_specs=[
@@ -721,7 +765,7 @@
     g_ref[:, 3 * HEAD :] = kv[:, HEAD:].astype(BF)
     wide = mm(g_ref[...], w_ref[...], NT)
     n_ref[...] = wide.astype(BF)
-    x = x_ref[0, :RUN, :].astype(F32)
+    x = jnp.concatenate([x_ref[n, :RUN, :] for n in range(SLOTS)], axis=0).astype(F32)
     attn_acc[...] += jnp.sum(wide * x * inverse_rms(x), axis=0, keepdims=True)
 
     @pl.when(step == pl.num_programs(0) - 1)
@@ -741,15 +785,15 @@
         return pl.BlockSpec(a.shape, lambda i: (0,) * a.ndim)
 
     def moving(n):
-        return pl.BlockSpec((RUN, n), lambda i: (i, 0))
+        return pl.BlockSpec((SLOTS * RUN, n), lambda i: (i, 0))
 
     return pl.pallas_call(
         unproject_kernel,
-        grid=(8,),
+        grid=(8 // SLOTS,),
         in_specs=[
-            pl.BlockSpec((8, RUN, 2 * HEAD), lambda i: (0, i, 0)),
+            pl.BlockSpec((8, SLOTS * RUN, 2 * HEAD), lambda i: (0, i, 0)),
             moving(2 * HEAD), moving(3 * HEAD),
-            pl.BlockSpec((1, X_ROWS, width), lambda i: (i, 0, 0)),
+            pl.BlockSpec((SLOTS, X_ROWS, width), lambda i: (i, 0, 0)),
             fixed(w), fixed(head_scale), moving(HEAD), moving(HEAD), fixed(mlp_part),
         ],
         out_specs=[moving(4 * HEAD), moving(width), pl.BlockSpec((64, 128), lambda i: (0, 0))],
@@ -960,31 +1004,37 @@
         kv_parts, query_turn, pre, x_all, w_qkv, head_scale, cos, sin,
         mlp_gain_part.reshape(1, width),
     )
-    qkv_wgrad = dot_t(norm_one, qkv_grad).astype(BF).reshape(8, part, 512)
 
     plan = Plan()
-    plan.return_tokens(0, 4, tokens)
-
-    def wgrad_piece(io, chip, c):
-        return io[1].at[
-            :, pl.ds(pl.multiple_of(chip * 16, 16), 16), pl.ds(pl.multiple_of(c * 256, 256), 256)
-        ]
-
-    for shift in [Shift(c=1)] + [
-        Shift(s.by[0], s.by[1], c) for s in plan.chip_shifts() for c in (0, 1)
-    ]:
-        plan.add(
-            shift,
-            lambda io, at, s=shift: wgrad_piece(io, s.to(at).chip(), s.to(at).c),
-            lambda io, at: io[5].at[at.chip() * 2 + at.c],
-        )
-    plan.add(
-        None,
-        lambda io, at: wgrad_piece(io, at.chip(), at.c),
-        lambda io, at: io[5].at[at.chip() * 2 + at.c],
-    )
-    plan.scatter_chips(rows(n_rows // 8)(2), lambda io, n: io[6].at[n])
-    plan.scatter_group(rows(8)(3), rows(8)(7))
+    plan.return_tokens(0, 3, tokens)
+    plan.scatter_chips(rows(n_rows // 8)(1), lambda io, n: io[5].at[n])
+    plan.scatter_group(rows(8)(2), rows(8)(6))
+    swap = plan.add(Shift(c=1), theirs(7, 256), full(8), stage=1)
+    plan.scatter_chips(
+        lambda io, n: io[9].at[:, pl.ds(pl.multiple_of(n * 16, 16), 16)],
+        lambda io, n: io[4].at[n],
+        stage=2,
+    )
+
+    def weight_grads(me, more, outs, made, scratch, begin, arrive):
+        norm_ref, grad_ref = more
+        both, got, total = scratch
+        mine = pl.ds(pl.multiple_of(me.c * 256, 256), 256)
+
+        def some_rows(j, _):
+            cut = pl.ds(pl.multiple_of(j * part, part), part)
+            both[j] = mm(norm_ref[:, cut], grad_ref[...], TN).astype(BF)
+            return 0
+
+        def add(j, _):
+            total[j] = (both[j, :, mine].astype(F32) + got[j].astype(F32)).astype(BF)
+            return 0
+
+        lax.fori_loop(0, 8, some_rows, 0)
+        begin(1)
+        arrive(swap)
+        lax.fori_loop(0, 8, add, 0)
+        begin(2)
 
     def stacked_rows(ref, size, total):
         def land(io, chip, c):
@@ -1004,10 +1054,18 @@
     norm_one_parts, qkv_pieces, output_pieces, gain_sums = exchange(
         plan, 8,
         (
-            ((group, width), BF), ((16, 8, 16, 256), BF), ((8, n_rows // 8, width // 2), BF),
+            ((group, width), BF), ((8, 8, 16, 256), BF), ((8, n_rows // 8, width // 2), BF),
             ((64, 128), F32),
         ),
-        norm_one_part, qkv_wgrad, output_half, gain_parts,
+        norm_one_part, output_half, gain_parts,
+        work=Work(
+            [(norm_one, pltpu.VMEM), (qkv_grad, pltpu.VMEM)], [],
+            [
+                pltpu.VMEM((8, part, 512), BF), pltpu.VMEM((8, part, 256), BF),
+                pltpu.VMEM((8, part, 256), BF),
+            ],
+            [], weight_grads,
+        ),
     )
     qkv_sum = jnp.sum(qkv_pieces.astype(F32), axis=0).astype(BF)
     output_sum = jnp.sum(output_pieces.astype(F32), axis=0).astype(BF)

time: 475 us -> 465 us (0.979)
  Pallas kernels: 406 us -> 397 us
    pallas_call x9, Pallas kernels: 352 us -> 347 us  [exchange(): pl.pallas_call(kernel, out_shape=tuple((jax.ShapeDtypeStruct(s, d) for s,...]
    dot_general x4 -> x3, matrix products: 11.7 us -> 8.24 us  [dot_t(): lax.dot_general(a, b, (((0,), (0,)), ((), ())), preferred_element_type=F32)]
where the time goes in v5:
time: 465 us; the launch traced here: 462 us
  Pallas kernels  397 us (85%)
  other arithmetic  27.5 us (6%)
  matrix products  24.5 us (5%)
  local copies, waits for them, and re-layouts  9.35 us (2%)
    pallas_call x9, Pallas kernels, exchange(): pl.pallas_call(kernel, out_shape=tuple((jax.ShapeDtypeStruct(s, d) for s,...  347 us
    pallas_call x1, Pallas kernels, attention_forward(): pl.pallas_call(forward_kernel, grid_spec=pltpu.PrefetchScalarGridSpec(num...  27.1 us
    dot_general x3, matrix products, dot(): return jnp.dot(a, b, preferred_element_type=F32)  9.93 us

profile of v5, /device:TPU:1, one launch (start us, length us, event | category | flops | bytes accessed | tf_op | source)
XLA Modules:
  0.0 461.9 jit_solution(17046110004371578788)
XLA Ops:
  5.4 1.7 concatenate.12.refs_0_
  7.1 35.8 %exchange_1.1 = (bf16[1152,1024]{1,0:T(8,128)(2,1)}, f32[64,128]{1,0:T(8,128)}, bf16[1024,512]{1,0:T(8,128)(2,1)}) custom-call(bf16[144,1024]{1,0:T(8,128)(2,1)} %concatenate.12.refs_0_, f32[8,128]{1,0:T(8,128)} %concatenate.13.refs_1_, bf16[128,2048]{1,0:T(8,128)(2,1)} %refs_2_.2, bf16[128,1024]{1,0:T(8,128)(2,1)} %refs_3_.2, bf16[128,1024]{1,0:T(8,128)(2,1)} %refs_4_.1), custom_call_target="tpu_custom_call" | custom-call | tf_op jit(solution)/shard_map/exchange_1/pallas_call | solution.py:206
  48.1 3.0 fusion.1
  51.1 6.8 %project.1 = (bf16[1024,1024]{1,0:T(8,128)(2,1)}, f32[1024,384]{1,0:T(8,128)}, bf16[1024,256]{1,0:T(8,128)(2,1)}, bf16[1040,256]{1,0:T(8,128)(2,1)}) custom-call(bf16[8,144,1024]{2,1,0:T(8,128)(2,1)} %bitcast.73, bf16[1024,512]{1,0:T(8,128)(2,1)} %get-tuple-element.59.w_ref, f32[1,1024]{1,0:T(1,128)} %get-tuple-element.113.scale_ref, ...), custom_call_target="tpu_custom_call" | custom-call | tf_op jit(solution)/shard_map/project/pallas_call | solution.py:719
  57.9 43.3 %exchange_2.1 = (bf16[8320,256]{1,0:T(8,128)(2,1)}, bf16[1024,1024]{1,0:T(8,128)(2,1)}, bf16[1024,768]{1,0:T(8,128)(2,1)}) custom-call(bf16[1040,256]{1,0:T(8,128)(2,1)} %get-tuple-element.61.refs_0_, bf16[128,1024]{1,0:T(8,128)(2,1)} %bitcast.83, bf16[128,3072]{1,0:T(8,128)(2,1)} %refs_2_.3, bf16[128,3072]{1,0:T(8,128)(2,1)} %refs_3_.3), custom_call_target="tpu_custom_call" | custom-call | tf_op jit(solution)/shard_map/exchange_2/pallas_call | solution.py:206
  102.6 27.1 %attention_forward.1 = (f32[1024,256]{1,0:T(8,128)}, f32[1024,256]{1,0:T(8,128)}) custom-call(s32[64]{0:T(128)} %reshape.155.order.refs_3_, s32[8]{0:T(128)} %convert_element_type.126.own.refs_4_, bf16[1024,256]{1,0:T(8,128)(2,1)} %get-tuple-element.63.q_ref.refs_5_, bf16[8320,256]{1,0:T(8,128)(2,1)} %get-tuple-element.62.kv_ref.refs_9_), custom_call_target="tpu_custom_call" | custom-call | tf_op jit(solution)/shard_map/attention_forward/pallas_call | solution.py:449
  129.7 3.3 convolution_convert_fusion.1.refs_0_
  133.0 28.9 %exchange_3.1 = bf16[1024,1024]{1,0:T(8,128)(2,1)} custom-call(bf16[1024,1024]{1,0:T(8,128)(2,1)} %convolution_convert_fusion.1.refs_0_), custom_call_target="tpu_custom_call" | custom-call | tf_op jit(solution)/shard_map/exchange_3/pallas_call | solution.py:206
  161.9 2.1 convert_reduce_fusion.1
  165.0 25.1 %exchange_4.1 = bf16[1024,1024]{1,0:T(8,128)(2,1)} custom-call(bf16[128,1024]{1,0:T(8,128)(2,1)} %multiply_convert_fusion.3.refs_0_), custom_call_target="tpu_custom_call" | custom-call | tf_op jit(solution)/shard_map/exchange_4/pallas_call | solution.py:206
  190.1 4.1 fusion.11
  194.2 1.6 multiply_convert_fusion.1
  195.8 2.0 convolution_convert_fusion.4.refs_2_
  197.7 3.0 convolution_convert_fusion.3
  200.7 3.2 convolution_convert_fusion.2.refs_0_
  203.9 28.8 %exchange_5.1 = (bf16[1024,1024]{1,0:T(8,128)(2,1)}, bf16[8,128,384]{2,1,0:T(8,128)(2,1)}, bf16[384,512]{1,0:T(8,128)(2,1)}) custom-call(bf16[1024,1024]{1,0:T(8,128)(2,1)} %convolution_convert_fusion.2.refs_0_, bf16[8,128,768]{2,1,0:T(8,128)(2,1)} %bitcast.76, bf16[384,1024]{1,0:T(8,128)(2,1)} %convolution_convert_fusion.4.refs_2_), custom_call_target="tpu_custom_call" | custom-call | tf_op jit(solution)/shard_map/exchange_5/pallas_call | solution.py:206
  232.8 2.1 add_convert_fusion.1.refs_2_
  234.9 2.2 add_convert_fusion.refs_1_
  239.3 32.8 %exchange_6.1 = (bf16[1024,1024]{1,0:T(8,128)(2,1)}, bf16[8,8,16,384]{3,2,1,0:T(8,128)(2,1)}, bf16[8,48,512]{2,1,0:T(8,128)(2,1)}) custom-call(bf16[128,1024]{1,0:T(8,128)(2,1)} %get-tuple-element.105.refs_0_, bf16[8,128,384]{2,1,0:T(8,128)(2,1)} %add_convert_fusion.refs_1_, bf16[384,512]{1,0:T(8,128)(2,1)} %add_convert_fusion.1.refs_2_), custom_call_target="tpu_custom_call" | custom-call | tf_op jit(solution)/shard_map/exchange_6/pallas_call | solution.py:206
  272.1 1.9 reduce_sum.127.refs_2_
  274.1 1.7 reduce_sum.133.refs_5_
  275.7 3.3 convolution_convert_fusion.6.refs_1_
  279.0 1.5 convolution_convert_fusion.5.refs_6_
  280.6 2.6 convolution_convert_fusion.refs_0_
  283.1 78.3 %exchange_7.1 = (bf16[8,1024,256]{2,1,0:T(8,128)(2,1)}, bf16[1024,1024]{1,0:T(8,128)(2,1)}, bf16[256,512]{1,0:T(8,128)(2,1)}, bf16[16,3072]{1,0:T(8,128)(2,1)}, f32[1024,256]{1,0:T(8,128)}) custom-call(bf16[1024,1024]{1,0:T(8,128)(2,1)} %convolution_convert_fusion.refs_0_, bf16[256,1024]{1,0:T(8,128)(2,1)} %convolution_convert_fusion.6.refs_1_, ...), custom_call_target="tpu_custom_call" | custom-call | tf_op jit(solution)/shard_map/exchange_7/pallas_call | solution.py:206
  361.5 1.7 add_convert_fusion.2.refs_1_
  363.2 9.2 %unproject.1 = (bf16[1024,512]{1,0:T(8,128)(2,1)}, bf16[1024,1024]{1,0:T(8,128)(2,1)}, f32[64,128]{1,0:T(8,128)}) custom-call(bf16[8,1024,256]{2,1,0:T(8,128)(2,1)} %get-tuple-element.73.kv_ref, f32[1024,256]{1,0:T(8,128)} %get-tuple-element.74.t_ref, f32[1024,384]{1,0:T(8,128)} %get-tuple-element.75.p_ref, bf16[8,144,1024]{2,1,0:T(8,128)(2,1)} %bitcast.74, ...), custom_call_target="tpu_custom_call" | custom-call | tf_op jit(solution)/shard_map/unproject/pallas_call | solution.py:790
  372.5 42.5 %exchange_8.1 = (bf16[1024,1024]{1,0:T(8,128)(2,1)}, bf16[8,8,16,256]{3,2,1,0:T(8,128)(2,1)}, bf16[8,32,512]{2,1,0:T(8,128)(2,1)}, f32[64,128]{1,0:T(8,128)}) custom-call(bf16[1024,1024]{1,0:T(8,128)(2,1)} %get-tuple-element.76.refs_0_, bf16[256,512]{1,0:T(8,128)(2,1)} %add_convert_fusion.2.refs_1_, f32[64,128]{1,0:T(8,128)} %get-tuple-element.78.refs_2_, ...), custom_call_target="tpu_custom_call" | custom-call | tf_op jit(solution)/shard_map/exchange_8/pallas_call | solution.py:206
  415.0 1.8 reduce_sum.129.refs_0_
  418.1 1.6 reduce_sum.130.refs_1_
  421.0 31.1 %exchange_9.1 = (bf16[16,2048]{1,0:T(8,128)(2,1)}, bf16[256,2048]{1,0:T(8,128)(2,1)}, bf16[256,1024]{1,0:T(8,128)(2,1)}, f32[128,128]{1,0:T(8,128)}, bf16[256,10...) custom-call(bf16[8,16,256]{2,1,0:T(8,128)(2,1)} %reduce_sum.129.refs_0_, ...), custom_call_target="tpu_custom_call" | custom-call | tf_op jit(solution)/shard_map/exchange_9/pallas_call | solution.py:206
  454.7 7.0 %finish.1 = (bf16[128,1024]{1,0:T(8,128)(2,1)}, f32[128,1024]{1,0:T(8,128)}, f32[128,2048]{1,0:T(8,128)}, f32[128,1024]{1,0:T(8,128)}, f32[128,1024]{1,0:T(8,128...) custom-call(bf16[256,3072]{1,0:T(8,128)(2,1)} %get-tuple-element.87.gate_ref.up_ref, ...), custom_call_target="tpu_custom_call" | custom-call | tf_op jit(solution)/shard_map/finish/pallas_call | solution.py:657
  (66 shorter events, 17.0 us)
Async XLA Ops:
  0.6 193.5 %copy-start = (bf16[384,1024]{1,0:T(8,128)(2,1)S(1)}, bf16[384,1024]{1,0:T(8,128)(2,1)}, u32[]{:S(2)}) copy-start(bf16[384,1024]{1,0:T(8,128)(2,1)} %param.26) | copy-start | bytes 2359300
  102.6 27.1 %copy-start.11 = (bf16[256,1024]{1,0:T(8,128)(2,1)S(1)}, bf16[256,1024]{1,0:T(8,128)(2,1)}, u32[]{:S(2)}) copy-start(bf16[256,1024]{1,0:T(8,128)(2,1)} %param.20) | copy-start | bytes 1572868
  161.9 2.1 copy-start.5
  164.1 74.1 %copy-start.1 = (f32[128,1024]{1,0:T(8,128)}, f32[128,1024]{1,0:T(8,128)S(1)}, u32[]{:S(2)}) copy-start(f32[128,1024]{1,0:T(8,128)S(1)} %get-tuple-element.108.middle_ref) | copy-start | bytes 1572868
  190.1 4.1 copy-start.12
  195.7 2.0 copy-start.14
  195.8 2.0 copy-start.8
  197.7 3.0 copy-start.13
  203.9 31.0 %copy-start.3 = (bf16[1024,768]{1,0:T(8,128)(2,1)S(1)}, bf16[1024,768]{1,0:T(8,128)(2,1)}, u32[]{:S(2)}) copy-start(bf16[1024,768]{1,0:T(8,128)(2,1)} %convolution_convert_fusion.3) | copy-start | bytes 4718596
  232.7 4.4 copy-start.6
  237.1 1.1 copy-start.10
  238.2 37.5 %copy-start.2 = (f32[1024,256]{1,0:T(8,128)S(1)}, f32[1024,256]{1,0:T(8,128)}, u32[]{:S(2)}) copy-start(f32[1024,256]{1,0:T(8,128)} %get-tuple-element.64.refs_7_) | copy-start | bytes 3145732
  275.7 3.3 copy-start.7
  279.0 1.5 copy-start.15
  283.1 78.3 %copy-start.4 = (bf16[256,1024]{1,0:T(8,128)(2,1)S(1)}, bf16[256,1024]{1,0:T(8,128)(2,1)}, u32[]{:S(2)}) copy-start(bf16[256,1024]{1,0:T(8,128)(2,1)} %convolution_convert_fusion.6.refs_1_) | copy-start | bytes 1572868
  372.5 47.3 %copy-start.9 = (bf16[1024,1024]{1,0:T(8,128)(2,1)S(1)}, bf16[1024,1024]{1,0:T(8,128)(2,1)}, u32[]{:S(2)}) copy-start(bf16[1024,1024]{1,0:T(8,128)(2,1)} %get-tuple-element.84) | copy-start | bytes 6291460
